TPU v7x, 128 devices: a whole 4x4x4 slice. The times are simulated.
128 devices in a mesh: role: 2 (over y_hi), dev: 64 (over z, x, y_lo, core).
Axes of the slice: x: 4, y: 4 (y_hi: 2, y_lo: 2; y = y_hi * 2 + y_lo), z: 4, core: 2. Of those that a mesh axis runs over, the one named last changes fastest.
Arguments:
- hidden: bfloat16 [1024, 7168], P(('role', 'dev')), may hold values from -6 to 6
- router: bfloat16 [7168, 32], replicated, may hold values from -0.0625 to 0.0625
- routes: int32 [1024, 8], P(('role', 'dev')), may hold values from 0 to 31, all different within a row; in each aligned block of 8 rows (0 to 7, 8 to 15, ...) at most 4 rows name the same one
- w_gate: bfloat16 [128, 7168, 256], P(('role', 'dev')), may hold values from -0.0625 to 0.0625
- w_up: bfloat16 [128, 7168, 256], P(('role', 'dev')), may hold values from -0.0625 to 0.0625
- w_down: bfloat16 [128, 256, 7168], P(('role', 'dev')), may hold values from -0.1875 to 0.1875
- w_latent: bfloat16 [7168, 576], replicated, may hold values from -0.0625 to 0.0625
- lengths: int32 [1024], P(('role', 'dev')), may hold values from 1 to 384, 196608 in all
- latent_cache: bfloat16 [1024, 384, 576], P(('role', 'dev')), may hold values from -4 to 4
- queries: bfloat16 [1024, 128, 576], P(('role', 'dev')), may hold values from -32 to 32
Outputs:
- layer_out: bfloat16 [1024, 7168], P(('role', 'dev'))
- attention: bfloat16 [1024, 128, 512], P(('role', 'dev'))
Inputs may be any that keep to these rules, and one draw needn't show every extreme that they name: `routes`: in the rows of one device no expert is named by more than 4 tokens.
All inputs are finite; a program needn't handle non-finite values. No bound on the sum of `lengths` on one device may be relied on, other than what follows from the above.
Results may differ from a plain program's by a relative error of at most 0.0065.
Values may be sent and summed in bfloat16 or wider, within the bound.
No kernel may reach another device: no remote copies, remote signals or barrier semaphores. Data moves between devices by JAX's collectives and lax.ppermute only.
A program may use at most 128 MiB of HBM per device.

v0:
```python
import math

import jax
import jax.numpy as jnp
from jax import lax
from jax.sharding import PartitionSpec as P

KVL = 512
QK_DIM = 192


def normalize(values):
    return values * lax.rsqrt(jnp.mean(values * values, axis=-1, keepdims=True) + 1e-06)


def prepare(router, experts, capacity, hidden, routes):
    normed = normalize(hidden.astype(jnp.float32)).astype(jnp.bfloat16)
    logits = jnp.dot(normed, router, preferred_element_type=jnp.float32)
    labels = jnp.arange(experts, dtype=jnp.int32)
    chosen = routes[:, :, None] == labels[None, None, :]
    picked = jnp.sum(jnp.where(chosen, logits[:, None, :], 0.0), axis=2)
    affinity = jax.nn.sigmoid(picked)
    weights = 2.5 * affinity / jnp.sum(affinity, axis=1, keepdims=True)
    flat_ids = routes.reshape(-1)
    member = (flat_ids[:, None] == labels[None, :]).astype(jnp.int32)
    before = jnp.cumsum(member, axis=0) - member
    slots = jnp.sum(before * member, axis=1).reshape(routes.shape)
    places = routes * capacity + slots
    cells = jnp.arange(experts * capacity, dtype=jnp.int32)
    layout = jnp.sum((cells[:, None, None] == places[None, :, :]).astype(jnp.int32), axis=2).astype(
        jnp.bfloat16
    )
    outgoing = jnp.dot(layout, normed, preferred_element_type=jnp.float32).astype(jnp.bfloat16)
    return (weights, places, outgoing.reshape(experts, capacity, normed.shape[1]))


def expert_block(token_rows, gate_slab, up_slab, down_slab):
    flat_rows = token_rows.reshape(-1, token_rows.shape[-1])
    gated = jnp.dot(flat_rows, gate_slab, preferred_element_type=jnp.float32)
    lifted = jnp.dot(flat_rows, up_slab, preferred_element_type=jnp.float32)
    inner = (jax.nn.silu(gated) * lifted).astype(jnp.bfloat16)
    return (
        jnp.dot(inner, down_slab, preferred_element_type=jnp.float32)
        .astype(jnp.bfloat16)
        .reshape(token_rows.shape)
    )


def rotate(values, positions):
    half = values.shape[-1] // 2
    indices = jnp.arange(half, dtype=jnp.float32)
    inverse = jnp.exp(indices * (-2.0 * math.log(10000.0) / values.shape[-1]))
    angles = positions.astype(jnp.float32)[:, None] * inverse[None, :]
    leading = values[:, :half]
    trailing = values[:, half:]
    return jnp.concatenate(
        [
            leading * jnp.cos(angles) - trailing * jnp.sin(angles),
            leading * jnp.sin(angles) + trailing * jnp.cos(angles),
        ],
        axis=1,
    )


def attend(layer_out, w_latent, lengths, latent_cache, queries):
    input_new = normalize(layer_out.astype(jnp.float32)).astype(jnp.bfloat16)
    projected = jnp.dot(input_new, w_latent, preferred_element_type=jnp.float32)
    latent_new = normalize(projected[:, :KVL]).astype(jnp.bfloat16)
    rotary_new = rotate(projected[:, KVL:], lengths).astype(jnp.bfloat16)
    key_new = jnp.concatenate([latent_new, rotary_new], axis=1)
    scale = 1.0 / math.sqrt(QK_DIM)
    positions_all = latent_cache.shape[1]
    scores = (
        jnp.einsum("rhc,rjc->rhj", queries, latent_cache, preferred_element_type=jnp.float32)
        * scale
    )
    own = jnp.einsum("rhc,rc->rh", queries, key_new, preferred_element_type=jnp.float32) * scale
    positions = jnp.arange(positions_all, dtype=jnp.int32)
    valid = positions[None, None, :] < lengths[:, None, None]
    masked = jnp.where(valid, scores, -jnp.inf)
    highest = jnp.maximum(jnp.max(masked, axis=2), own)
    probs = jnp.where(valid, jnp.exp(masked - highest[:, :, None]), 0.0).astype(jnp.bfloat16)
    own_prob = jnp.exp(own - highest).astype(jnp.bfloat16)
    total = jnp.sum(probs.astype(jnp.float32), axis=2) + own_prob.astype(jnp.float32)
    summed = jnp.einsum(
        "rhj,rjc->rhc", probs, latent_cache[:, :, :KVL], preferred_element_type=jnp.float32
    )
    summed = (
        summed
        + own_prob.astype(jnp.float32)[:, :, None] * latent_new.astype(jnp.float32)[:, None, :]
    )
    return (summed / total[:, :, None]).astype(jnp.bfloat16)


def body(hidden, router, routes, w_gate, w_up, w_down, w_latent, lengths, latent_cache, queries):
    dev_count = lax.axis_size("dev")
    experts = dev_count // 2
    rows_here, top_count = routes.shape
    capacity = max(4, rows_here * top_count // experts)
    width = hidden.shape[1]
    weights, places, outgoing = prepare(router, experts, capacity, hidden, routes)
    sending = jnp.tile(outgoing, (4, 1, 1))
    partial_rows = expert_block(
        lax.all_to_all(sending, ("role", "dev"), split_axis=0, concat_axis=0, tiled=True),
        w_gate[0],
        w_up[0],
        w_down[0],
    )
    returned = lax.all_to_all(
        partial_rows, ("role", "dev"), split_axis=0, concat_axis=0, tiled=True
    )
    halves = returned.reshape(2, dev_count, capacity, width)
    paired = (halves[0].astype(jnp.float32) + halves[1].astype(jnp.float32)).astype(jnp.bfloat16)
    quads = paired.reshape(2, experts, capacity, width)
    expert_out = (quads[0].astype(jnp.float32) + quads[1].astype(jnp.float32)).astype(jnp.bfloat16)
    picked = expert_out.reshape(experts * capacity, width)[places]
    mixture = jnp.sum(weights[..., None] * picked.astype(jnp.float32), axis=1)
    layer_out = (hidden.astype(jnp.float32) + mixture).astype(jnp.bfloat16)
    attention = attend(layer_out, w_latent, lengths, latent_cache, queries)
    return (layer_out, attention)


def solution(mesh):
    return jax.shard_map(
        body,
        mesh=mesh,
        in_specs=(
            P(("role", "dev"), None),
            P(),
            P(("role", "dev"), None),
            P(("role", "dev"), None, None),
            P(("role", "dev"), None, None),
            P(("role", "dev"), None, None),
            P(),
            P(("role", "dev")),
            P(("role", "dev"), None, None),
            P(("role", "dev"), None, None),
        ),
        out_specs=(P(("role", "dev"), None), P(("role", "dev"), None, None)),
        check_vma=False,
    )
```

profile of v0, /device:TPU:98, one launch (start us, length us, event | category | flops | bytes accessed | tf_op | source)
XLA Modules:
  0.0 293.1 jit_solution(12378253437438837155)
XLA Ops:
  0.6 0.9 eq.45
  1.6 0.1 reduce_window_sum.11
  1.7 0.2 select_reduce_fusion
  1.9 0.7 compare_select_fusion
  2.6 0.1 convert_reduce_fusion.1
  2.7 1.1 fusion.21
  3.8 1.6 convolution_convert_fusion.1
  5.4 1.7 tile.10
  7.1 6.7 %tile.11 = bf16[4,32,4,7168]{3,2,1,0:T(4,128)(2,1)} broadcast(bf16[32,4,7168]{2,1,0:T(4,128)(2,1)} %tile.10), dimensions={1,2,3} | broadcast | bytes 9175040 | tf_op jit(solution)/shard_map/tile | solution.py:102
  13.8 99.8 %all_to_all.10 = bf16[128,4,7168]{2,1,0:T(4,128)(2,1)} all-to-all(bf16[128,4,7168]{2,1,0:T(4,128)(2,1)} %bitcast.30), channel_id=1, replica_groups=mesh['role'=2,'dev'=64] {'role','dev'}, dimensions={0} | all-to-all | bytes 14680064 | tf_op jit(solution)/shard_map/all_to_all | solution.py:104
  113.6 12.1 %reshape.117 = bf16[512,7168]{1,0:T(8,128)(2,1)} reshape(bf16[128,4,7168]{2,1,0:T(4,128)(2,1)} %all_to_all.10) | data formatting | bytes 14680064 | tf_op jit(solution)/shard_map/reshape | solution.py:38
  125.7 6.2 %fusion.3 = f32[512,256]{1,0:T(8,128)S(1)} fusion(bf16[512,7168]{1,0:T(8,128)(2,1)} %reshape.117, bf16[1,7168,256]{2,1,0:T(8,128)(2,1)} %param.13), kind=kOutput, calls=%fused_computation.7 | convolution fusion | flops 1879048192 | bytes 11534336 | tf_op jit(solution)/shard_map/dot_general | solution.py:39
  131.9 16.0 %convolution_convert_fusion = bf16[512,7168]{1,0:T(8,128)(2,1)} fusion(bf16[1,256,7168]{2,1,0:T(8,128)(2,1)} %param.15, bf16[512,7168]{1,0:T(8,128)(2,1)} %reshape.117, bf16[1,7168,256]{2,1,0:T(8,128)(2,1)} %param.14, f32[512,256]{1,0:T(8,128)S(1)} %fusion.3), kind=kOutput, calls=%fused_computation.1 | convolution fusion | flops 3762552832 | bytes 22544384 | tf_op jit(solution)/shard_map/dot_general | solution.py:43
  147.9 12.6 %reshape.118 = bf16[128,4,7168]{2,1,0:T(4,128)(2,1)} reshape(bf16[512,7168]{1,0:T(8,128)(2,1)} %convolution_convert_fusion) | data formatting | bytes 14680064 | tf_op jit(solution)/shard_map/reshape | solution.py:45
  160.6 7.0 %all-to-all-start.1 = ((bf16[128,4,7168]{2,1,0:T(4,128)(2,1)}), bf16[128,4,7168]{2,1,0:T(4,128)(2,1)}, u32[]{:S(2)}, u32[]{:S(2)}) async-start(bf16[128,4,7168]{2,1,0:T(4,128)(2,1)} %reshape.118), calls=%async_computation.1 | async-start | bytes 14680064 | tf_op jit(solution)/shard_map/all_to_all | solution.py:109
  167.7 0.3 fusion.28
  168.0 0.2 select_reduce_fusion.1
  168.2 0.1 fusion.43
  168.4 4.2 %fusion.50 = (f32[8,128]{1,0:T(8,128)S(1)}, f32[8,128,384]{2,1,0:T(8,128)}) fusion(bf16[8,128,576]{1,2,0:T(8,128)(2,1)S(1)} %copy-done, bf16[8,384,576]{1,2,0:T(8,128)(2,1)} %param.18, pred[8,384]{1,0:T(8,128)(4,1)S(1)} %iota_compare_fusion.3), kind=kOutput, calls=%fused_computation.75 | convolution fusion | flops 454163456 | bytes 6298624 | tf_op jit(solution)/shard_map/rhc,rjc->rhj/dot_general | solution.py:74
  172.7 96.8 %all-to-all-done.1 = bf16[128,4,7168]{2,1,0:T(4,128)(2,1)} async-done(((bf16[128,4,7168]{2,1,0:T(4,128)(2,1)}), bf16[128,4,7168]{2,1,0:T(4,128)(2,1)}, u32[]{:S(2)}, u32[]{:S(2)}) %all-to-all-start.1) | async-done | bytes 7340064 | tf_op jit(solution)/shard_map/all_to_all | solution.py:109
  269.4 5.0 %add_convert_fusion = bf16[64,4,7168]{2,1,0:T(4,128)(2,1)S(1)} fusion(bf16[128,4,7168]{2,1,0:T(4,128)(2,1)} %all-to-all-done.1), kind=kLoop, calls=%fused_computation.3 | loop fusion | flops 7340032 | bytes 11010048 | tf_op jit(solution)/shard_map/convert_element_type | solution.py:113
  274.5 2.2 add_convert_fusion.1
  276.7 2.9 %convert_element_type.103 = bf16[128,7168]{1,0:T(8,128)(2,1)S(1)} reshape(bf16[32,4,7168]{2,1,0:T(4,128)(2,1)} %add_convert_fusion.1) | data formatting | bytes 3670016 | tf_op jit(solution)/shard_map/convert_element_type | solution.py:115
  279.6 2.0 gather_fusion
  281.7 1.9 fusion.7
  283.6 0.2 fusion.19
  283.9 5.7 %fusion.24 = f32[8,576]{1,0:T(8,128)S(1)} fusion(bf16[7168,576]{0,1:T(8,128)(2,1)} %param.16, bf16[8,7168]{1,0:T(8,128)(2,1)S(1)} %get-tuple-element.7, f32[8]{0:T(128)S(1)} %add_rsqrt_fusion.1), kind=kOutput, calls=%fused_computation.31 | convolution fusion | flops 66232320 | bytes 8390688 | tf_op jit(solution)/shard_map/dot_general | solution.py:67
  289.6 0.1 multiply_reduce_fusion
  289.8 0.1 fusion.38
  290.0 0.3 fusion.31
  290.3 0.5 convert_reduce_fusion
  290.9 2.2 divide_convert_fusion
  (31 shorter events, 0.6 us)
Async XLA Ops:
  0.6 167.8 %copy-start = (bf16[8,128,576]{1,2,0:T(8,128)(2,1)S(1)}, bf16[8,128,576]{1,2,0:T(8,128)(2,1)}, u32[]{:S(2)}) copy-start(bf16[8,128,576]{1,2,0:T(8,128)(2,1)} %param.19) | copy-start | bytes 3538948
  160.6 7.1 %copy-start.7 = (s32[8]{0:T(128)S(1)}, s32[8]{0:T(128)}, u32[]{:S(2)}) copy-start(s32[8]{0:T(128)} %param.17) | copy-start | bytes 100
  160.6 7.1 %copy-start.3 = (bf16[8,7168]{1,0:T(8,128)(2,1)S(1)}, bf16[8,7168]{1,0:T(8,128)(2,1)}, u32[]{:S(2)}) copy-start(bf16[8,7168]{1,0:T(8,128)(2,1)} %param.10) | copy-start | bytes 344068
  160.6 7.1 %copy-start.5 = (bf16[7168,32]{0,1:T(8,128)(2,1)S(1)}, bf16[7168,32]{0,1:T(8,128)(2,1)}, u32[]{:S(2)}) copy-start(bf16[7168,32]{0,1:T(8,128)(2,1)} %param.11) | copy-start | bytes 1376260
  160.6 7.4 %copy-start.6 = (s32[8,8]{1,0:T(8,128)S(1)}, s32[8,8]{1,0:T(8,128)}, u32[]{:S(2)}) copy-start(s32[8,8]{1,0:T(8,128)} %param.12) | copy-start | bytes 772
  160.6 108.8 %all-to-all-start.1 = ((bf16[128,4,7168]{2,1,0:T(4,128)(2,1)}), bf16[128,4,7168]{2,1,0:T(4,128)(2,1)}, u32[]{:S(2)}, u32[]{:S(2)}) async-start(bf16[128,4,7168]{2,1,0:T(4,128)(2,1)} %reshape.118), calls=%async_computation.1 | async-start | bytes 14680064 | tf_op jit(solution)/shard_map/all_to_all | solution.py:109
  283.8 5.8 %copy-start.4 = (bf16[8,7168]{1,0:T(8,128)(2,1)}, bf16[8,7168]{1,0:T(8,128)(2,1)S(1)}, u32[]{:S(2)}) copy-start(bf16[8,7168]{1,0:T(8,128)(2,1)S(1)} %get-tuple-element.7) | copy-start | bytes 344068
  283.8 6.5 %copy-start.1 = (f32[8,128,384]{2,1,0:T(8,128)S(1)}, f32[8,128,384]{2,1,0:T(8,128)}, u32[]{:S(2)}) copy-start(f32[8,128,384]{2,1,0:T(8,128)} %get-tuple-element.13) | copy-start | bytes 4718596
  283.8 7.0 %copy-start.2 = (bf16[8,384,576]{1,2,0:T(8,128)(2,1)S(1)}, bf16[8,384,576]{1,2,0:T(8,128)(2,1)}, u32[]{:S(2)}) copy-start(bf16[8,384,576]{1,2,0:T(8,128)(2,1)} %param.18) | copy-start | bytes 10616836
where the time goes:
time: 294 us; the launch traced here: 293 us
  blocking collectives  99.8 us (34%)
  waiting for transfers between devices  96.8 us (33%)
  local copies, waits for them, and re-layouts  39.2 us (13%)
  matrix products  36.5 us (12%)
  other arithmetic  13 us (4%)
  starting transfers between devices  6.99 us (2%)
    all_to_all x1, blocking collectives, body(): lax.all_to_all(sending, ('role', 'dev'), split_axis=0, concat_axis=0, til...  99.8 us
    all_to_all x1, waiting for transfers between devices, body(): lax.all_to_all(partial_rows, ('role', 'dev'), split_axis=0, concat_axis=0...  96.8 us
    dot_general x1, matrix products, expert_block(): jnp.dot(inner, down_slab, preferred_element_type=jnp.float32)  16 us
    reshape x1, local copies, waits for them, and re-layouts, expert_block(): return jnp.dot(inner, down_slab, preferred_element_type=jnp.float32).asty...  12.6 us
    reshape x1, local copies, waits for them, and re-layouts, expert_block(): flat_rows = token_rows.reshape(-1, token_rows.shape[-1])  12.1 us
    another operation x2, local copies, waits for them, and re-layouts, body(): sending = jnp.tile(outgoing, (4, 1, 1))  8.39 us
    all_to_all x1, starting transfers between devices, body(): lax.all_to_all(partial_rows, ('role', 'dev'), split_axis=0, concat_axis=0...  6.99 us
    dot_general x1, matrix products, expert_block(): gated = jnp.dot(flat_rows, gate_slab, preferred_element_type=jnp.float32)  6.18 us
  transfers between devices with their start and end apart: 1, of which 1 were waited for; matrix products, arithmetic and copies ran while one was open for 2% of the time, Pallas kernels for 0%

commit v1 on v0

v1 whole, which is shorter than its diff:
```python
import math

import jax
import jax.numpy as jnp
from jax import lax
from jax.sharding import PartitionSpec as P

KVL = 512
QK_DIM = 192
AXES = ("role", "dev")
LANES = 128


def place(yh, z, x, yl, core):
    return (((yh * 4 + z) * 4 + x) * 2 + yl) * 2 + core


def shift_pairs(core_axes, offset):
    pairs = []
    for yh in range(2):
        for z in range(4):
            for x in range(4):
                for yl in range(2):
                    for core in range(2):
                        spot = {"x": x, "y": yh * 2 + yl, "z": z}
                        axis = core_axes[core]
                        spot[axis] = (spot[axis] + offset) % 4
                        there = place(spot["y"] // 2, spot["z"], spot["x"], spot["y"] % 2, core)
                        pairs.append((there, place(yh, z, x, yl, core)))
    return pairs


AXIS = {"a": ("x", "z"), "b": ("z", "x"), "y": ("y", "y")}


def shift(values, axis, offset):
    return lax.ppermute(values, AXES, shift_pairs(AXIS[axis], offset))


def swap_cores(values):
    return lax.ppermute(values, AXES, [(d, d ^ 1) for d in range(128)])


def gather(values, axis):
    near = shift(values, axis, 1)
    back = shift(values, axis, 3)
    far = shift(values, axis, 2)
    return [values, near, far, back]


def reduce(blocks, axis):
    near = shift(blocks[1], axis, 3)
    back = shift(blocks[3], axis, 1)
    far = shift(blocks[2], axis, 2)
    f = jnp.float32
    return blocks[0].astype(f) + near.astype(f) + back.astype(f) + far.astype(f)


def normalize(values):
    return values * lax.rsqrt(jnp.mean(values * values, axis=-1, keepdims=True) + 1e-06)


def prepare(router, routes, hidden):
    experts = router.shape[1]
    normed = normalize(hidden.astype(jnp.float32)).astype(jnp.bfloat16)
    logits = jnp.dot(normed, router, preferred_element_type=jnp.float32)
    labels = jnp.arange(experts, dtype=jnp.int32)
    chosen = jnp.any(routes[:, :, None] == labels[None, None, :], axis=1)
    affinity = jnp.where(chosen, jax.nn.sigmoid(logits), 0.0)
    weights = 2.5 * affinity / jnp.sum(affinity, axis=1, keepdims=True)
    high = weights.astype(jnp.bfloat16)
    low = (weights - high.astype(jnp.float32)).astype(jnp.bfloat16)
    pad = jnp.zeros((hidden.shape[0], LANES - 2 * experts), jnp.bfloat16)
    return normed, jnp.concatenate([high, low, pad], axis=1)


def rotate(values, positions):
    half = values.shape[-1] // 2
    indices = jnp.arange(half, dtype=jnp.float32)
    inverse = jnp.exp(indices * (-2.0 * math.log(10000.0) / values.shape[-1]))
    angles = positions.astype(jnp.float32)[:, None] * inverse[None, :]
    leading = values[:, :half]
    trailing = values[:, half:]
    return jnp.concatenate(
        [
            leading * jnp.cos(angles) - trailing * jnp.sin(angles),
            leading * jnp.sin(angles) + trailing * jnp.cos(angles),
        ],
        axis=1,
    )


def attend_cache(lengths, latent_cache, queries):
    scale = 1.0 / math.sqrt(QK_DIM)
    scores = (
        jnp.einsum("rhc,rjc->rhj", queries, latent_cache, preferred_element_type=jnp.float32)
        * scale
    )
    positions = jnp.arange(latent_cache.shape[1], dtype=jnp.int32)
    valid = positions[None, None, :] < lengths[:, None, None]
    highest = jnp.max(jnp.where(valid, scores, -jnp.inf), axis=2)
    probs = jnp.where(valid, jnp.exp(scores - highest[:, :, None]), 0.0).astype(jnp.bfloat16)
    total = jnp.sum(probs.astype(jnp.float32), axis=2)
    summed = jnp.einsum(
        "rhj,rjc->rhc", probs, latent_cache[:, :, :KVL], preferred_element_type=jnp.float32
    )
    return highest, total, summed


def attend_own(layer_out, w_latent, lengths, queries, highest, total, summed):
    input_new = normalize(layer_out.astype(jnp.float32)).astype(jnp.bfloat16)
    projected = jnp.dot(input_new, w_latent, preferred_element_type=jnp.float32)
    latent_new = normalize(projected[:, :KVL]).astype(jnp.bfloat16)
    rotary_new = rotate(projected[:, KVL:], lengths).astype(jnp.bfloat16)
    key_new = jnp.concatenate([latent_new, rotary_new], axis=1)
    scale = 1.0 / math.sqrt(QK_DIM)
    own = jnp.einsum("rhc,rc->rh", queries, key_new, preferred_element_type=jnp.float32) * scale
    top = jnp.maximum(highest, own)
    fade = jnp.exp(highest - top)
    own_prob = jnp.exp(own - top)
    whole = total * fade + own_prob
    mixed = (
        summed * (fade / whole)[:, :, None]
        + (own_prob / whole)[:, :, None] * latent_new.astype(jnp.float32)[:, None, :]
    )
    return mixed.astype(jnp.bfloat16)


def body(hidden, router, routes, w_gate, w_up, w_down, w_latent, lengths, latent_cache, queries):
    bf, f32 = jnp.bfloat16, jnp.float32
    rows, width = hidden.shape
    experts = router.shape[1]
    cut = width // LANES * 2 // 3 // 2 * 2 * LANES + 2 * LANES
    cut = 38 * LANES if width == 7168 else cut
    rest = width - cut
    mine = lax.rem(lax.axis_index("dev"), experts)

    normed, gates = prepare(router, routes, hidden)
    other_gate, other_up, other_down = swap_cores(w_gate[0]), swap_cores(w_up[0]), swap_cores(w_down[0])

    first = jnp.stack(gather(normed[:, :cut], "y"))
    second = jnp.stack(gather(jnp.concatenate([normed[:, cut:], gates], axis=1), "a"))
    both = gather(jnp.concatenate([first, second], axis=2), "b")
    first = jnp.stack([block[:, :, :cut] for block in both])
    second = jnp.stack([block[:, :, cut:] for block in both])
    firsts = gather(first, "a")
    seconds = gather(second, "y")

    gates_all = jnp.stack([block[..., rest:] for block in seconds]).astype(f32)
    gates_all = gates_all[..., :experts] + gates_all[..., experts : 2 * experts]
    labels = jnp.arange(experts)
    gate_own = jnp.sum(jnp.where(labels == mine, gates_all, 0.0), axis=-1)
    gate_other = jnp.sum(jnp.where(labels == mine + 1 - 2 * (mine % 2), gates_all, 0.0), axis=-1)
    gate_own, gate_other = [
        jnp.transpose(g, (2, 1, 0, 3)).reshape(-1, 1) for g in (gate_own, gate_other)
    ]

    count = 64 * rows
    left = jnp.stack(firsts).reshape(count, cut)
    right = jnp.transpose(jnp.stack([block[..., :rest] for block in seconds]), (2, 1, 0, 3, 4))
    right = right.reshape(count, rest)

    def lift(slab):
        return jnp.dot(left, slab[:cut], preferred_element_type=f32) + jnp.dot(
            right, slab[cut:], preferred_element_type=f32
        )

    inner = jnp.concatenate(
        [
            (jax.nn.silu(lift(w_gate[0])) * lift(w_up[0]) * gate_own).astype(bf),
            (jax.nn.silu(lift(other_gate)) * lift(other_up) * gate_other).astype(bf),
        ],
        axis=1,
    )
    down = jnp.concatenate([w_down[0], other_down], axis=0)
    inner_turned = jnp.transpose(inner.reshape(4, 4, 4, rows, -1), (2, 1, 0, 3, 4)).reshape(count, -1)
    first = jnp.dot(inner, down[:, :cut], preferred_element_type=f32).astype(bf)
    second = jnp.dot(inner_turned, down[:, cut:], preferred_element_type=f32).astype(bf)

    first = reduce(first.reshape(4, 4, 4, rows, cut), "a")
    second = reduce(second.reshape(4, 4, 4, rows, rest), "y")
    both = reduce(jnp.concatenate([first, second], axis=3).astype(bf), "b").astype(bf)
    first = reduce(both[..., :cut], "y")
    second = reduce(both[..., cut:], "a")
    mixture = jnp.concatenate([first, second], axis=1)
    layer_out = (hidden.astype(f32) + mixture).astype(bf)

    highest, total, summed = attend_cache(lengths, latent_cache, queries)
    attention = attend_own(layer_out, w_latent, lengths, queries, highest, total, summed)
    return (layer_out, attention)


def solution(mesh):
    both = P(AXES)
    return jax.shard_map(
        body,
        mesh=mesh,
        in_specs=(both, P(), both, both, both, both, P(), both, both, both),
        out_specs=(both, both),
        check_vma=False,
    )
```

time: 294 us -> 207 us (0.70)
  the two profiles are of different devices: /device:TPU:98 before, /device:TPU:0 now
where the time goes in v1:
time: 207 us; the launch traced here: 206 us
  waiting for transfers between devices  104 us (50%)
  starting transfers between devices  52.8 us (26%)
  matrix products  30.8 us (15%)
  other arithmetic  11.8 us (6%)
  local copies, waits for them, and re-layouts  5.38 us (3%)
    ppermute x30, waiting for transfers between devices, shift(): return lax.ppermute(values, AXES, shift_pairs(AXIS[axis], offset))  104 us
    ppermute x30, starting transfers between devices, shift(): return lax.ppermute(values, AXES, shift_pairs(AXIS[axis], offset))  52.1 us
    dot_general x4, matrix products, lift(): jnp.dot(left, slab[:cut], preferred_element_type=f32)  9.51 us
    dot_general x4, matrix products, lift(): jnp.dot(right, slab[cut:], preferred_element_type=f32)  5.82 us
    dot_general x1, matrix products, body(): first = jnp.dot(inner, down[:, :cut], preferred_element_type=f32).astype(bf)  5.23 us
  transfers between devices with their start and end apart: 33, of which 18 were waited for; matrix products, arithmetic and copies ran while one was open for 16% of the time, Pallas kernels for 0%

profile of v1, /device:TPU:0, one launch (start us, length us, event | category | flops | bytes accessed | tf_op | source)
XLA Modules:
  0.0 206.1 jit_solution(202998671483590360)
XLA Ops:
  5.2 2.9 %collective-permute-start.3 = (bf16[8,2432]{1,0:T(8,128)(2,1)S(1)}, bf16[8,2432]{1,0:T(8,128)(2,1)S(1)}, u32[]{:S(2)}, u32[]{:S(2)}) collective-permute-start(bf16[8,2432]{1,0:T(8,128)(2,1)S(1)} %concatenate.25), channel_id=1, source_target_pairs={{4,0},{17,1},{6,2},{19,3},{8,4},{21,5},{10,6},{23,7},{12,8},{25,9}... | collective-permute-start | bytes 116744 | tf_op jit(solution)/shard_map/ppermute | solution.py:37
  9.7 3.1 %collective-permute-start = (bf16[8,4864]{1,0:T(8,128)(2,1)S(1)}, bf16[8,4864]{1,0:T(8,128)(2,1)S(1)}, u32[]{:S(2)}, u32[]{:S(2)}) collective-permute-start(bf16[8,4864]{1,0:T(8,128)(2,1)S(1)} %get-tuple-element.28), channel_id=1, source_target_pairs={{2,0},{3,1},{64,2},{65,3},{6,4},{7,5},{68,6},{69,7},{10,8},{11,9},... | collective-permute-start | bytes 233480 | tf_op jit(solution)/shard_map/ppermute | solution.py:37
  16.1 2.9 %collective-permute-done.1 = bf16[8,4864]{1,0:T(8,128)(2,1)S(1)} collective-permute-done((bf16[8,4864]{1,0:T(8,128)(2,1)S(1)}, bf16[8,4864]{1,0:T(8,128)(2,1)S(1)}, u32[]{:S(2)}, u32[]{:S(2)}) %collective-permute-start.1) | collective-permute-done | bytes 77856 | tf_op jit(solution)/shard_map/ppermute | solution.py:37
  19.8 2.3 %collective-permute-start.8 = (bf16[4,8,7296]{2,1,0:T(8,128)(2,1)S(1)}, bf16[4,8,7296]{2,1,0:T(8,128)(2,1)S(1)}, u32[]{:S(2)}, u32[]{:S(2)}) collective-permute-start(bf16[4,8,7296]{2,1,0:T(8,128)(2,1)S(1)} %maximum_maximum_fusion), channel_id=1, source_target_pairs={{48,0},{13,1},{50,2},{15,3},{52,4},{1,5},{54,6},{3,7},{56,8},{5,9}... | collective-permute-start | bytes 1400840 | tf_op jit(solution)/shard_map/ppermute | solution.py:37
  22.1 3.0 %collective-permute-start.7 = (bf16[4,8,7296]{2,1,0:T(8,128)(2,1)S(1)}, bf16[4,8,7296]{2,1,0:T(8,128)(2,1)S(1)}, u32[]{:S(2)}, u32[]{:S(2)}) collective-permute-start(bf16[4,8,7296]{2,1,0:T(8,128)(2,1)S(1)} %maximum_maximum_fusion), channel_id=1, source_target_pairs={{32,0},{9,1},{34,2},{11,3},{36,4},{13,5},{38,6},{15,7},{40,8},{1,9... | collective-permute-start | bytes 1400840 | tf_op jit(solution)/shard_map/ppermute | solution.py:37
  26.2 4.0 %collective-permute-done.8 = bf16[4,8,7296]{2,1,0:T(8,128)(2,1)S(1)} collective-permute-done((bf16[4,8,7296]{2,1,0:T(8,128)(2,1)S(1)}, bf16[4,8,7296]{2,1,0:T(8,128)(2,1)S(1)}, u32[]{:S(2)}, u32[]{:S(2)}) %collective-permute-start.8) | collective-permute-done | bytes 466976 | tf_op jit(solution)/shard_map/ppermute | solution.py:37
  30.2 6.4 %collective-permute-done.7 = bf16[4,8,7296]{2,1,0:T(8,128)(2,1)S(1)} collective-permute-done((bf16[4,8,7296]{2,1,0:T(8,128)(2,1)S(1)}, bf16[4,8,7296]{2,1,0:T(8,128)(2,1)S(1)}, u32[]{:S(2)}, u32[]{:S(2)}) %collective-permute-start.7) | collective-permute-done | bytes 466976 | tf_op jit(solution)/shard_map/ppermute | solution.py:37
  38.0 2.4 %collective-permute-start.9 = (bf16[4,4,8,4864]{3,2,1,0:T(8,128)(2,1)}, bf16[4,4,8,4864]{3,2,1,0:T(8,128)(2,1)}, u32[]{:S(2)}, u32[]{:S(2)}) collective-permute-start(bf16[4,4,8,4864]{3,2,1,0:T(8,128)(2,1)} %get-tuple-element.20), channel_id=1, source_target_pairs={{4,0},{17,1},{6,2},{19,3},{8,4},{21,5},{10,6},{23,7},{12,8},{25,9}... | collective-permute-start | bytes 3735560 | tf_op jit(solution)/shard_map/ppermute | solution.py:37
  42.2 14.8 %collective-permute-done.14 = bf16[4,4,8,2432]{3,2,0,1:T(8,128)(2,1)S(1)} collective-permute-done((bf16[4,4,8,2432]{3,2,0,1:T(8,128)(2,1)S(1)}, bf16[4,4,8,2432]{3,2,0,1:T(8,128)(2,1)S(1)}, u32[]{:S(2)}, u32[]{:S(2)}) %collective-permute-start.14) | collective-permute-done | bytes 622624 | tf_op jit(solution)/shard_map/ppermute | solution.py:37
  57.8 13.5 %collective-permute-done.13 = bf16[4,4,8,2432]{3,2,0,1:T(8,128)(2,1)S(1)} collective-permute-done((bf16[4,4,8,2432]{3,2,0,1:T(8,128)(2,1)S(1)}, bf16[4,4,8,2432]{3,2,0,1:T(8,128)(2,1)S(1)}, u32[]{:S(2)}, u32[]{:S(2)}) %collective-permute-start.13) | collective-permute-done | bytes 622624 | tf_op jit(solution)/shard_map/ppermute | solution.py:37
  72.3 11.0 %collective-permute-done.12 = bf16[4,4,8,2432]{3,2,0,1:T(8,128)(2,1)S(1)} collective-permute-done((bf16[4,4,8,2432]{3,2,0,1:T(8,128)(2,1)S(1)}, bf16[4,4,8,2432]{3,2,0,1:T(8,128)(2,1)S(1)}, u32[]{:S(2)}, u32[]{:S(2)}) %collective-permute-start.12) | collective-permute-done | bytes 622624 | tf_op jit(solution)/shard_map/ppermute | solution.py:37
  83.3 5.5 %collective-permute-start.11 = (bf16[4,4,8,4864]{3,2,1,0:T(8,128)(2,1)}, bf16[4,4,8,4864]{3,2,1,0:T(8,128)(2,1)}, u32[]{:S(2)}, u32[]{:S(2)}) collective-permute-start(bf16[4,4,8,4864]{3,2,1,0:T(8,128)(2,1)} %get-tuple-element.20), channel_id=1, source_target_pairs={{12,0},{49,1},{14,2},{51,3},{0,4},{53,5},{2,6},{55,7},{4,8},{57,9}... | collective-permute-start | bytes 3735560 | tf_op jit(solution)/shard_map/ppermute | solution.py:37
  95.5 7.9 %collective-permute-done.11 = bf16[4,4,8,4864]{3,2,1,0:T(8,128)(2,1)} collective-permute-done((bf16[4,4,8,4864]{3,2,1,0:T(8,128)(2,1)}, bf16[4,4,8,4864]{3,2,1,0:T(8,128)(2,1)}, u32[]{:S(2)}, u32[]{:S(2)}) %collective-permute-start.11) | collective-permute-done | bytes 1245216 | tf_op jit(solution)/shard_map/ppermute | solution.py:37
  103.5 2.3 %pad_maximum_fusion = bf16[4,4,4,8,4864]{4,3,2,1,0:T(8,128)(2,1)S(1)} fusion(bf16[1,4,4,8,4864]{4,3,2,1,0:T(8,128)(2,1)} %bitcast.15, bf16[1,4,4,8,4864]{4,3,2,1,0:T(8,128)(2,1)} %bitcast.14, bf16[1,4,4,8,4864]{4,3,2,1,0:T(8,128)(2,1)} %bitcast.13, bf16[1,4,4,8,4864]{4,3,2,1,0:T(8,128)(2,1)S(1)} %get-tuple-element.19), kind=kLoop, calls=%fused_computation.4 | loop fusion | flops 7471104 | bytes 9961472 | tf_op jit(solution)/shard_map/stack | solution.py:159
  111.0 2.1 %fusion.32 = f32[512,256]{0,1:T(8,128)S(1)} fusion(bf16[512,2304]{1,0:T(8,128)(2,1)S(1)} %bitcast.162, bf16[7168,256]{1,0:T(8,128)(2,1)} %collective-permute-done.16), kind=kOutput, calls=%fused_computation.41 | convolution fusion | flops 603979776 | bytes 4063232 | tf_op jit(solution)/shard_map/dot_general | solution.py:164
  113.1 3.2 %fusion.26 = f32[512,256]{0,1:T(8,128)S(1)} fusion(f32[512,256]{0,1:T(8,128)S(1)} %fusion.34, bf16[512,4864]{1,0:T(8,128)(2,1)S(1)} %bitcast.155, bf16[7168,256]{1,0:T(8,128)(2,1)} %collective-permute-done.15), kind=kOutput, calls=%fused_computation.39 | convolution fusion | flops 1275199488 | bytes 8519680 | tf_op jit(solution)/shard_map/dot_general | solution.py:164
  116.3 3.3 %multiply_convert_fusion = bf16[512,256]{0,1:T(8,128)(2,1)S(1)} fusion(f32[512,256]{0,1:T(8,128)S(1)} %fusion.26, f32[512]{0:T(512)S(1)} %mul.159, f32[512,256]{0,1:T(8,128)S(1)} %fusion.32, bf16[512,4864]{1,0:T(8,128)(2,1)S(1)} %bitcast.156, bf16[7168,256]{1,0:T(8,128)(2,1)} %collective-permute-done.16), kind=kOutput, calls=%fused_computation.70 | convolution fusion | flops 1276116992 | bytes 8783872 | tf_op jit(solution)/shard_map/dot_general | solution.py:164
  119.9 3.0 %convolution_convert_fusion.1 = bf16[512,2304]{1,0:T(8,128)(2,1)S(1)} fusion(bf16[512,512]{1,0:T(8,128)(2,1)S(1)} %bitcast.163, bf16[256,7168]{1,0:T(8,128)(2,1)} %collective-permute-done.17, bf16[256,7168]{1,0:T(8,128)(2,1)} %bitcast.46), kind=kOutput, calls=%fused_computation.5 | convolution fusion | flops 1213857792 | bytes 10223616 | tf_op jit(solution)/shard_map/dot_general | solution.py:178
  123.2 3.2 %collective-permute-start.22 = (bf16[4,4,8,2304]{3,2,1,0:T(8,128)(2,1)S(1)}, bf16[4,4,8,2304]{3,2,1,0:T(8,128)(2,1)S(1)}, u32[]{:S(2)}, u32[]{:S(2)}) collective-permute-start(bf16[4,4,8,2304]{3,2,1,0:T(8,128)(2,1)S(1)} %bitcast.169), channel_id=1, source_target_pairs={{2,0},{3,1},{64,2},{65,3},{6,4},{7,5},{68,6},{69,7},{10,8},{11,9},... | collective-permute-start | bytes 1769480 | tf_op jit(solution)/shard_map/ppermute | solution.py:37
  126.4 5.2 %convolution_convert_fusion = bf16[512,4864]{1,0:T(8,128)(2,1)S(1)} fusion(bf16[256,7168]{1,0:T(8,128)(2,1)} %bitcast.46, bf16[256,7168]{1,0:T(8,128)(2,1)} %collective-permute-done.17, bf16[512,256]{0,1:T(8,128)(2,1)S(1)} %multiply_convert_fusion, bf16[512,256]{0,1:T(8,128)(2,1)S(1)} %multiply_convert_fusion.1), kind=kOutput, calls=%fused_computation | convolution fusion | flops 2563637248 | bytes 12845056 | tf_op jit(solution)/shard_map/dot_general | solution.py:177
  132.0 2.6 %collective-permute-start.18 = (bf16[4,4,8,4864]{3,2,1,0:T(8,128)(2,1)S(1)}, bf16[4,4,8,4864]{3,2,1,0:T(8,128)(2,1)S(1)}, u32[]{:S(2)}, u32[]{:S(2)}) collective-permute-start(bf16[4,4,8,4864]{3,2,1,0:T(8,128)(2,1)S(1)} %bitcast.167), channel_id=1, source_target_pairs={{12,0},{49,1},{14,2},{51,3},{0,4},{53,5},{2,6},{55,7},{4,8},{57,9}... | collective-permute-start | bytes 3735560 | tf_op jit(solution)/shard_map/ppermute | solution.py:37
  135.3 9.5 %collective-permute-done.21 = bf16[4,4,8,2304]{3,2,1,0:T(8,128)(2,1)S(1)} collective-permute-done((bf16[4,4,8,2304]{3,2,1,0:T(8,128)(2,1)S(1)}, bf16[4,4,8,2304]{3,2,1,0:T(8,128)(2,1)S(1)}, u32[]{:S(2)}, u32[]{:S(2)}) %collective-permute-start.21) | collective-permute-done | bytes 589856 | tf_op jit(solution)/shard_map/ppermute | solution.py:37
  145.2 4.9 %collective-permute-done.18 = bf16[4,4,8,4864]{3,2,1,0:T(8,128)(2,1)S(1)} collective-permute-done((bf16[4,4,8,4864]{3,2,1,0:T(8,128)(2,1)S(1)}, bf16[4,4,8,4864]{3,2,1,0:T(8,128)(2,1)S(1)}, u32[]{:S(2)}, u32[]{:S(2)}) %collective-permute-start.18) | collective-permute-done | bytes 1245216 | tf_op jit(solution)/shard_map/ppermute | solution.py:37
  151.4 12.3 %collective-permute-done.20 = bf16[4,4,8,4864]{3,2,1,0:T(8,128)(2,1)S(1)} collective-permute-done((bf16[4,4,8,4864]{3,2,1,0:T(8,128)(2,1)S(1)}, bf16[4,4,8,4864]{3,2,1,0:T(8,128)(2,1)S(1)}, u32[]{:S(2)}, u32[]{:S(2)}) %collective-permute-start.20) | collective-permute-done | bytes 1245216 | tf_op jit(solution)/shard_map/ppermute | solution.py:37
  164.5 6.8 %collective-permute-start.24 = (bf16[4,8,7168]{2,1,0:T(8,128)(2,1)S(1)}, bf16[4,8,7168]{2,1,0:T(8,128)(2,1)S(1)}, u32[]{:S(2)}, u32[]{:S(2)}) collective-permute-start(bf16[4,8,7168]{2,1,0:T(8,128)(2,1)S(1)} %get-tuple-element.16), channel_id=1, source_target_pairs={{48,0},{13,1},{50,2},{15,3},{52,4},{1,5},{54,6},{3,7},{56,8},{5,9}... | collective-permute-start | bytes 1376264 | tf_op jit(solution)/shard_map/ppermute | solution.py:37
  171.3 4.7 %collective-permute-start.26 = (bf16[4,8,7168]{2,1,0:T(8,128)(2,1)S(1)}, bf16[4,8,7168]{2,1,0:T(8,128)(2,1)S(1)}, u32[]{:S(2)}, u32[]{:S(2)}) collective-permute-start(bf16[4,8,7168]{2,1,0:T(8,128)(2,1)S(1)} %get-tuple-element.17), channel_id=1, source_target_pairs={{32,0},{9,1},{34,2},{11,3},{36,4},{13,5},{38,6},{15,7},{40,8},{1,9... | collective-permute-start | bytes 1376264 | tf_op jit(solution)/shard_map/ppermute | solution.py:37
  177.7 2.9 %collective-permute-done.25 = bf16[4,8,7168]{2,1,0:T(8,128)(2,1)S(1)} collective-permute-done((bf16[4,8,7168]{2,1,0:T(8,128)(2,1)S(1)}, bf16[4,8,7168]{2,1,0:T(8,128)(2,1)S(1)}, u32[]{:S(2)}, u32[]{:S(2)}) %collective-permute-start.25) | collective-permute-done | bytes 458784 | tf_op jit(solution)/shard_map/ppermute | solution.py:37
  180.7 5.5 %collective-permute-done.26 = bf16[4,8,7168]{2,1,0:T(8,128)(2,1)S(1)} collective-permute-done((bf16[4,8,7168]{2,1,0:T(8,128)(2,1)S(1)}, bf16[4,8,7168]{2,1,0:T(8,128)(2,1)S(1)}, u32[]{:S(2)}, u32[]{:S(2)}) %collective-permute-start.26) | collective-permute-done | bytes 458784 | tf_op jit(solution)/shard_map/ppermute | solution.py:37
  186.4 2.9 %collective-permute-start.30 = (bf16[8,2304]{1,0:T(8,128)(2,1)S(1)}, bf16[8,2304]{1,0:T(8,128)(2,1)S(1)}, u32[]{:S(2)}, u32[]{:S(2)}) collective-permute-start(bf16[8,2304]{1,0:T(8,128)(2,1)S(1)} %get-tuple-element.24), channel_id=1, source_target_pairs={{12,0},{49,1},{14,2},{51,3},{0,4},{53,5},{2,6},{55,7},{4,8},{57,9}... | collective-permute-start | bytes 110600 | tf_op jit(solution)/shard_map/ppermute | solution.py:37
  197.7 3.0 %collective-permute-done.29 = bf16[8,4864]{1,0:T(8,128)(2,1)S(1)} collective-permute-done((bf16[8,4864]{1,0:T(8,128)(2,1)S(1)}, bf16[8,4864]{1,0:T(8,128)(2,1)S(1)}, u32[]{:S(2)}, u32[]{:S(2)}) %collective-permute-start.29) | collective-permute-done | bytes 77856 | tf_op jit(solution)/shard_map/ppermute | solution.py:37
  201.0 2.2 %fusion.66 = f32[8,576]{1,0:T(8,128)S(1)} fusion(bf16[7168,576]{0,1:T(8,128)(2,1)S(1)} %bitcast.152, bf16[8,7168]{1,0:T(8,128)(2,1)S(1)} %get-tuple-element.7, f32[8]{0:T(128)S(1)} %add_rsqrt_fusion.1), kind=kOutput, calls=%fused_computation.106 | convolution fusion | flops 66232320 | bytes 8390688 | tf_op jit(solution)/shard_map/dot_general | solution.py:112
  203.9 2.2 %add_convert_fusion = bf16[8,128,512]{2,1,0:T(8,128)(2,1)} fusion(bf16[8,384,576]{1,2,0:T(8,128)(2,1)S(1)} %copy-done.1, f32[8,512]{1,0:T(8,128)S(1)} %get-tuple-element.4, f32[8,128]{1,0:T(8,128)S(1)} %get-tuple-element.32, f32[8,128]{1,0:T(8,128)S(1)} %get-tuple-element.31, f32[8,128,384]{2,1,0:T(8,128)S(1)} %get-tuple-element.38, ...), kind=kOutput, calls=%fused_computation.28 | convolution fusion | flops 405929984 | bytes 5798912 | tf_op jit(solution)/shard_map/rhj,rjc->rhc/dot_general | solution.py:104
  (130 shorter events, 43.4 us)
Async XLA Ops:
  5.2 8.3 %collective-permute-start.3 = (bf16[8,2432]{1,0:T(8,128)(2,1)S(1)}, bf16[8,2432]{1,0:T(8,128)(2,1)S(1)}, u32[]{:S(2)}, u32[]{:S(2)}) collective-permute-start(bf16[8,2432]{1,0:T(8,128)(2,1)S(1)} %concatenate.25), channel_id=1, source_target_pairs={{4,0},{17,1},{6,2},{19,3},{8,4},{21,5},{10,6},{23,7},{12,8},{25,9}... | collective-permute-start | bytes 116744 | tf_op jit(solution)/shard_map/ppermute | solution.py:37
  8.0 6.5 %collective-permute-start.4 = (bf16[8,2432]{1,0:T(8,128)(2,1)S(1)}, bf16[8,2432]{1,0:T(8,128)(2,1)S(1)}, u32[]{:S(2)}, u32[]{:S(2)}) collective-permute-start(bf16[8,2432]{1,0:T(8,128)(2,1)S(1)} %concatenate.25), channel_id=1, source_target_pairs={{8,0},{33,1},{10,2},{35,3},{12,4},{37,5},{14,6},{39,7},{0,8},{41,9... | collective-permute-start | bytes 116744 | tf_op jit(solution)/shard_map/ppermute | solution.py:37
  8.8 5.7 %collective-permute-start.5 = (bf16[8,2432]{1,0:T(8,128)(2,1)S(1)}, bf16[8,2432]{1,0:T(8,128)(2,1)S(1)}, u32[]{:S(2)}, u32[]{:S(2)}) collective-permute-start(bf16[8,2432]{1,0:T(8,128)(2,1)S(1)} %concatenate.25), channel_id=1, source_target_pairs={{12,0},{49,1},{14,2},{51,3},{0,4},{53,5},{2,6},{55,7},{4,8},{57,9}... | collective-permute-start | bytes 116744 | tf_op jit(solution)/shard_map/ppermute | solution.py:37
  9.7 6.4 %collective-permute-start = (bf16[8,4864]{1,0:T(8,128)(2,1)S(1)}, bf16[8,4864]{1,0:T(8,128)(2,1)S(1)}, u32[]{:S(2)}, u32[]{:S(2)}) collective-permute-start(bf16[8,4864]{1,0:T(8,128)(2,1)S(1)} %get-tuple-element.28), channel_id=1, source_target_pairs={{2,0},{3,1},{64,2},{65,3},{6,4},{7,5},{68,6},{69,7},{10,8},{11,9},... | collective-permute-start | bytes 233480 | tf_op jit(solution)/shard_map/ppermute | solution.py:37
  12.8 6.2 %collective-permute-start.1 = (bf16[8,4864]{1,0:T(8,128)(2,1)S(1)}, bf16[8,4864]{1,0:T(8,128)(2,1)S(1)}, u32[]{:S(2)}, u32[]{:S(2)}) collective-permute-start(bf16[8,4864]{1,0:T(8,128)(2,1)S(1)} %get-tuple-element.28), channel_id=1, source_target_pairs={{64,0},{65,1},{66,2},{67,3},{68,4},{69,5},{70,6},{71,7},{72,8},{73... | collective-permute-start | bytes 233480 | tf_op jit(solution)/shard_map/ppermute | solution.py:37
  13.4 6.4 %collective-permute-start.2 = (bf16[8,4864]{1,0:T(8,128)(2,1)S(1)}, bf16[8,4864]{1,0:T(8,128)(2,1)S(1)}, u32[]{:S(2)}, u32[]{:S(2)}) collective-permute-start(bf16[8,4864]{1,0:T(8,128)(2,1)S(1)} %get-tuple-element.28), channel_id=1, source_target_pairs={{66,0},{67,1},{0,2},{1,3},{70,4},{71,5},{4,6},{5,7},{74,8},{75,9},... | collective-permute-start | bytes 233480 | tf_op jit(solution)/shard_map/ppermute | solution.py:37
  14.5 94.4 %collective-permute-start.15 = (bf16[7168,256]{1,0:T(8,128)(2,1)}, bf16[7168,256]{1,0:T(8,128)(2,1)}, u32[]{:S(2)}, u32[]{:S(2)}) collective-permute-start(bf16[7168,256]{1,0:T(8,128)(2,1)} %bitcast.188), channel_id=1, source_target_pairs={{0,1},{1,0},{2,3},{3,2},{4,5},{5,4},{6,7},{7,6},{8,9},{9,8},{10,11... | collective-permute-start | bytes 11010056 | tf_op jit(solution)/shard_map/ppermute | solution.py:41
  14.5 96.5 %collective-permute-start.16 = (bf16[7168,256]{1,0:T(8,128)(2,1)}, bf16[7168,256]{1,0:T(8,128)(2,1)}, u32[]{:S(2)}, u32[]{:S(2)}) collective-permute-start(bf16[7168,256]{1,0:T(8,128)(2,1)} %bitcast.189), channel_id=1, source_target_pairs={{0,1},{1,0},{2,3},{3,2},{4,5},{5,4},{6,7},{7,6},{8,9},{9,8},{10,11... | collective-permute-start | bytes 11010056 | tf_op jit(solution)/shard_map/ppermute | solution.py:41
  19.8 10.4 %collective-permute-start.8 = (bf16[4,8,7296]{2,1,0:T(8,128)(2,1)S(1)}, bf16[4,8,7296]{2,1,0:T(8,128)(2,1)S(1)}, u32[]{:S(2)}, u32[]{:S(2)}) collective-permute-start(bf16[4,8,7296]{2,1,0:T(8,128)(2,1)S(1)} %maximum_maximum_fusion), channel_id=1, source_target_pairs={{48,0},{13,1},{50,2},{15,3},{52,4},{1,5},{54,6},{3,7},{56,8},{5,9}... | collective-permute-start | bytes 1400840 | tf_op jit(solution)/shard_map/ppermute | solution.py:37
  22.1 14.5 %collective-permute-start.7 = (bf16[4,8,7296]{2,1,0:T(8,128)(2,1)S(1)}, bf16[4,8,7296]{2,1,0:T(8,128)(2,1)S(1)}, u32[]{:S(2)}, u32[]{:S(2)}) collective-permute-start(bf16[4,8,7296]{2,1,0:T(8,128)(2,1)S(1)} %maximum_maximum_fusion), channel_id=1, source_target_pairs={{32,0},{9,1},{34,2},{11,3},{36,4},{13,5},{38,6},{15,7},{40,8},{1,9... | collective-permute-start | bytes 1400840 | tf_op jit(solution)/shard_map/ppermute | solution.py:37
  25.1 11.6 %collective-permute-start.6 = (bf16[4,8,7296]{2,1,0:T(8,128)(2,1)S(1)}, bf16[4,8,7296]{2,1,0:T(8,128)(2,1)S(1)}, u32[]{:S(2)}, u32[]{:S(2)}) collective-permute-start(bf16[4,8,7296]{2,1,0:T(8,128)(2,1)S(1)} %maximum_maximum_fusion), channel_id=1, source_target_pairs={{16,0},{5,1},{18,2},{7,3},{20,4},{9,5},{22,6},{11,7},{24,8},{13,9}... | collective-permute-start | bytes 1400840 | tf_op jit(solution)/shard_map/ppermute | solution.py:37
  38.0 57.2 %collective-permute-start.9 = (bf16[4,4,8,4864]{3,2,1,0:T(8,128)(2,1)}, bf16[4,4,8,4864]{3,2,1,0:T(8,128)(2,1)}, u32[]{:S(2)}, u32[]{:S(2)}) collective-permute-start(bf16[4,4,8,4864]{3,2,1,0:T(8,128)(2,1)} %get-tuple-element.20), channel_id=1, source_target_pairs={{4,0},{17,1},{6,2},{19,3},{8,4},{21,5},{10,6},{23,7},{12,8},{25,9}... | collective-permute-start | bytes 3735560 | tf_op jit(solution)/shard_map/ppermute | solution.py:37
  40.4 55.2 %collective-permute-start.10 = (bf16[4,4,8,4864]{3,2,1,0:T(8,128)(2,1)}, bf16[4,4,8,4864]{3,2,1,0:T(8,128)(2,1)}, u32[]{:S(2)}, u32[]{:S(2)}) collective-permute-start(bf16[4,4,8,4864]{3,2,1,0:T(8,128)(2,1)} %get-tuple-element.20), channel_id=1, source_target_pairs={{8,0},{33,1},{10,2},{35,3},{12,4},{37,5},{14,6},{39,7},{0,8},{41,9... | collective-permute-start | bytes 3735560 | tf_op jit(solution)/shard_map/ppermute | solution.py:37
  42.0 14.9 %collective-permute-start.14 = (bf16[4,4,8,2432]{3,2,0,1:T(8,128)(2,1)S(1)}, bf16[4,4,8,2432]{3,2,0,1:T(8,128)(2,1)S(1)}, u32[]{:S(2)}, u32[]{:S(2)}) collective-permute-start(bf16[4,4,8,2432]{3,2,0,1:T(8,128)(2,1)S(1)} %pad_maximum_fusion.5), channel_id=1, source_target_pairs={{66,0},{67,1},{0,2},{1,3},{70,4},{71,5},{4,6},{5,7},{74,8},{75,9},... | collective-permute-start | bytes 1867784 | tf_op jit(solution)/shard_map/ppermute | solution.py:37
  57.0 14.3 %collective-permute-start.13 = (bf16[4,4,8,2432]{3,2,0,1:T(8,128)(2,1)S(1)}, bf16[4,4,8,2432]{3,2,0,1:T(8,128)(2,1)S(1)}, u32[]{:S(2)}, u32[]{:S(2)}) collective-permute-start(bf16[4,4,8,2432]{3,2,0,1:T(8,128)(2,1)S(1)} %pad_maximum_fusion.5), channel_id=1, source_target_pairs={{64,0},{65,1},{66,2},{67,3},{68,4},{69,5},{70,6},{71,7},{72,8},{73... | collective-permute-start | bytes 1867784 | tf_op jit(solution)/shard_map/ppermute | solution.py:37
  71.3 11.9 %collective-permute-start.12 = (bf16[4,4,8,2432]{3,2,0,1:T(8,128)(2,1)S(1)}, bf16[4,4,8,2432]{3,2,0,1:T(8,128)(2,1)S(1)}, u32[]{:S(2)}, u32[]{:S(2)}) collective-permute-start(bf16[4,4,8,2432]{3,2,0,1:T(8,128)(2,1)S(1)} %pad_maximum_fusion.5), channel_id=1, source_target_pairs={{2,0},{3,1},{64,2},{65,3},{6,4},{7,5},{68,6},{69,7},{10,8},{11,9},... | collective-permute-start | bytes 1867784 | tf_op jit(solution)/shard_map/ppermute | solution.py:37
  83.3 20.2 %collective-permute-start.11 = (bf16[4,4,8,4864]{3,2,1,0:T(8,128)(2,1)}, bf16[4,4,8,4864]{3,2,1,0:T(8,128)(2,1)}, u32[]{:S(2)}, u32[]{:S(2)}) collective-permute-start(bf16[4,4,8,4864]{3,2,1,0:T(8,128)(2,1)} %get-tuple-element.20), channel_id=1, source_target_pairs={{12,0},{49,1},{14,2},{51,3},{0,4},{53,5},{2,6},{55,7},{4,8},{57,9}... | collective-permute-start | bytes 3735560 | tf_op jit(solution)/shard_map/ppermute | solution.py:37
  95.3 24.6 %collective-permute-start.17 = (bf16[256,7168]{1,0:T(8,128)(2,1)}, bf16[256,7168]{1,0:T(8,128)(2,1)}, u32[]{:S(2)}, u32[]{:S(2)}) collective-permute-start(bf16[256,7168]{1,0:T(8,128)(2,1)} %bitcast.46), channel_id=1, source_target_pairs={{0,1},{1,0},{2,3},{3,2},{4,5},{5,4},{6,7},{7,6},{8,9},{9,8},{10,11... | collective-permute-start | bytes 11010056 | tf_op jit(solution)/shard_map/ppermute | solution.py:41
  123.1 21.7 %collective-permute-start.21 = (bf16[4,4,8,2304]{3,2,1,0:T(8,128)(2,1)S(1)}, bf16[4,4,8,2304]{3,2,1,0:T(8,128)(2,1)S(1)}, u32[]{:S(2)}, u32[]{:S(2)}) collective-permute-start(bf16[4,4,8,2304]{3,2,1,0:T(8,128)(2,1)S(1)} %bitcast.170), channel_id=1, source_target_pairs={{66,0},{67,1},{0,2},{1,3},{70,4},{71,5},{4,6},{5,7},{74,8},{75,9},... | collective-permute-start | bytes 1769480 | tf_op jit(solution)/shard_map/ppermute | solution.py:37
  123.2 21.8 %collective-permute-start.22 = (bf16[4,4,8,2304]{3,2,1,0:T(8,128)(2,1)S(1)}, bf16[4,4,8,2304]{3,2,1,0:T(8,128)(2,1)S(1)}, u32[]{:S(2)}, u32[]{:S(2)}) collective-permute-start(bf16[4,4,8,2304]{3,2,1,0:T(8,128)(2,1)S(1)} %bitcast.169), channel_id=1, source_target_pairs={{2,0},{3,1},{64,2},{65,3},{6,4},{7,5},{68,6},{69,7},{10,8},{11,9},... | collective-permute-start | bytes 1769480 | tf_op jit(solution)/shard_map/ppermute | solution.py:37
  126.4 18.5 %collective-permute-start.23 = (bf16[4,4,8,2304]{3,2,1,0:T(8,128)(2,1)S(1)}, bf16[4,4,8,2304]{3,2,1,0:T(8,128)(2,1)S(1)}, u32[]{:S(2)}, u32[]{:S(2)}) collective-permute-start(bf16[4,4,8,2304]{3,2,1,0:T(8,128)(2,1)S(1)} %bitcast.168), channel_id=1, source_target_pairs={{64,0},{65,1},{66,2},{67,3},{68,4},{69,5},{70,6},{71,7},{72,8},{73... | collective-permute-start | bytes 1769480 | tf_op jit(solution)/shard_map/ppermute | solution.py:37
  132.0 18.2 %collective-permute-start.18 = (bf16[4,4,8,4864]{3,2,1,0:T(8,128)(2,1)S(1)}, bf16[4,4,8,4864]{3,2,1,0:T(8,128)(2,1)S(1)}, u32[]{:S(2)}, u32[]{:S(2)}) collective-permute-start(bf16[4,4,8,4864]{3,2,1,0:T(8,128)(2,1)S(1)} %bitcast.167), channel_id=1, source_target_pairs={{12,0},{49,1},{14,2},{51,3},{0,4},{53,5},{2,6},{55,7},{4,8},{57,9}... | collective-permute-start | bytes 3735560 | tf_op jit(solution)/shard_map/ppermute | solution.py:37
  134.5 16.9 %collective-permute-start.19 = (bf16[4,4,8,4864]{3,2,1,0:T(8,128)(2,1)S(1)}, bf16[4,4,8,4864]{3,2,1,0:T(8,128)(2,1)S(1)}, u32[]{:S(2)}, u32[]{:S(2)}) collective-permute-start(bf16[4,4,8,4864]{3,2,1,0:T(8,128)(2,1)S(1)} %bitcast.166), channel_id=1, source_target_pairs={{4,0},{17,1},{6,2},{19,3},{8,4},{21,5},{10,6},{23,7},{12,8},{25,9}... | collective-permute-start | bytes 3735560 | tf_op jit(solution)/shard_map/ppermute | solution.py:37
  144.8 18.9 %collective-permute-start.20 = (bf16[4,4,8,4864]{3,2,1,0:T(8,128)(2,1)S(1)}, bf16[4,4,8,4864]{3,2,1,0:T(8,128)(2,1)S(1)}, u32[]{:S(2)}, u32[]{:S(2)}) collective-permute-start(bf16[4,4,8,4864]{3,2,1,0:T(8,128)(2,1)S(1)} %bitcast.165), channel_id=1, source_target_pairs={{8,0},{33,1},{10,2},{35,3},{12,4},{37,5},{14,6},{39,7},{0,8},{41,9... | collective-permute-start | bytes 3735560 | tf_op jit(solution)/shard_map/ppermute | solution.py:37
  164.5 13.2 %collective-permute-start.24 = (bf16[4,8,7168]{2,1,0:T(8,128)(2,1)S(1)}, bf16[4,8,7168]{2,1,0:T(8,128)(2,1)S(1)}, u32[]{:S(2)}, u32[]{:S(2)}) collective-permute-start(bf16[4,8,7168]{2,1,0:T(8,128)(2,1)S(1)} %get-tuple-element.16), channel_id=1, source_target_pairs={{48,0},{13,1},{50,2},{15,3},{52,4},{1,5},{54,6},{3,7},{56,8},{5,9}... | collective-permute-start | bytes 1376264 | tf_op jit(solution)/shard_map/ppermute | solution.py:37
  171.3 9.3 %collective-permute-start.25 = (bf16[4,8,7168]{2,1,0:T(8,128)(2,1)S(1)}, bf16[4,8,7168]{2,1,0:T(8,128)(2,1)S(1)}, u32[]{:S(2)}, u32[]{:S(2)}) collective-permute-start(bf16[4,8,7168]{2,1,0:T(8,128)(2,1)S(1)} %get-tuple-element.18), channel_id=1, source_target_pairs={{16,0},{5,1},{18,2},{7,3},{20,4},{9,5},{22,6},{11,7},{24,8},{13,9}... | collective-permute-start | bytes 1376264 | tf_op jit(solution)/shard_map/ppermute | solution.py:37
  171.3 14.8 %collective-permute-start.26 = (bf16[4,8,7168]{2,1,0:T(8,128)(2,1)S(1)}, bf16[4,8,7168]{2,1,0:T(8,128)(2,1)S(1)}, u32[]{:S(2)}, u32[]{:S(2)}) collective-permute-start(bf16[4,8,7168]{2,1,0:T(8,128)(2,1)S(1)} %get-tuple-element.17), channel_id=1, source_target_pairs={{32,0},{9,1},{34,2},{11,3},{36,4},{13,5},{38,6},{15,7},{40,8},{1,9... | collective-permute-start | bytes 1376264 | tf_op jit(solution)/shard_map/ppermute | solution.py:37
  186.4 8.4 %collective-permute-start.30 = (bf16[8,2304]{1,0:T(8,128)(2,1)S(1)}, bf16[8,2304]{1,0:T(8,128)(2,1)S(1)}, u32[]{:S(2)}, u32[]{:S(2)}) collective-permute-start(bf16[8,2304]{1,0:T(8,128)(2,1)S(1)} %get-tuple-element.24), channel_id=1, source_target_pairs={{12,0},{49,1},{14,2},{51,3},{0,4},{53,5},{2,6},{55,7},{4,8},{57,9}... | collective-permute-start | bytes 110600 | tf_op jit(solution)/shard_map/ppermute | solution.py:37
  189.3 6.1 %collective-permute-start.31 = (bf16[8,2304]{1,0:T(8,128)(2,1)S(1)}, bf16[8,2304]{1,0:T(8,128)(2,1)S(1)}, u32[]{:S(2)}, u32[]{:S(2)}) collective-permute-start(bf16[8,2304]{1,0:T(8,128)(2,1)S(1)} %get-tuple-element.26), channel_id=1, source_target_pairs={{4,0},{17,1},{6,2},{19,3},{8,4},{21,5},{10,6},{23,7},{12,8},{25,9}... | collective-permute-start | bytes 110600 | tf_op jit(solution)/shard_map/ppermute | solution.py:37
  189.7 5.7 %collective-permute-start.32 = (bf16[8,2304]{1,0:T(8,128)(2,1)S(1)}, bf16[8,2304]{1,0:T(8,128)(2,1)S(1)}, u32[]{:S(2)}, u32[]{:S(2)}) collective-permute-start(bf16[8,2304]{1,0:T(8,128)(2,1)S(1)} %get-tuple-element.25), channel_id=1, source_target_pairs={{8,0},{33,1},{10,2},{35,3},{12,4},{37,5},{14,6},{39,7},{0,8},{41,9... | collective-permute-start | bytes 110600 | tf_op jit(solution)/shard_map/ppermute | solution.py:37
  191.5 5.7 %collective-permute-start.27 = (bf16[8,4864]{1,0:T(8,128)(2,1)S(1)}, bf16[8,4864]{1,0:T(8,128)(2,1)S(1)}, u32[]{:S(2)}, u32[]{:S(2)}) collective-permute-start(bf16[8,4864]{1,0:T(8,128)(2,1)S(1)} %get-tuple-element.21), channel_id=1, source_target_pairs={{66,0},{67,1},{0,2},{1,3},{70,4},{71,5},{4,6},{5,7},{74,8},{75,9},... | collective-permute-start | bytes 233480 | tf_op jit(solution)/shard_map/ppermute | solution.py:37
  194.8 5.9 %collective-permute-start.29 = (bf16[8,4864]{1,0:T(8,128)(2,1)S(1)}, bf16[8,4864]{1,0:T(8,128)(2,1)S(1)}, u32[]{:S(2)}, u32[]{:S(2)}) collective-permute-start(bf16[8,4864]{1,0:T(8,128)(2,1)S(1)} %get-tuple-element.22), channel_id=1, source_target_pairs={{64,0},{65,1},{66,2},{67,3},{68,4},{69,5},{70,6},{71,7},{72,8},{73... | collective-permute-start | bytes 233480 | tf_op jit(solution)/shard_map/ppermute | solution.py:37
  (10 other events, 301.4 us)

commit v2 on v1

--- a/solution.py
+++ b/solution.py
@@ -1,8 +1,11 @@
+import functools
 import math
 
 import jax
 import jax.numpy as jnp
 from jax import lax
+from jax.experimental import pallas as pl
+from jax.experimental.pallas import tpu as pltpu
 from jax.sharding import PartitionSpec as P
 
 KVL = 512
@@ -15,7 +18,7 @@
     return (((yh * 4 + z) * 4 + x) * 2 + yl) * 2 + core
 
 
-def shift_pairs(core_axes, offset):
+def partners(axes, flips):
     pairs = []
     for yh in range(2):
         for z in range(4):
@@ -23,37 +26,51 @@
                 for yl in range(2):
                     for core in range(2):
                         spot = {"x": x, "y": yh * 2 + yl, "z": z}
-                        axis = core_axes[core]
-                        spot[axis] = (spot[axis] + offset) % 4
+                        spot[axes[core]] ^= flips[core]
                         there = place(spot["y"] // 2, spot["z"], spot["x"], spot["y"] % 2, core)
-                        pairs.append((there, place(yh, z, x, yl, core)))
+                        pairs.append((place(yh, z, x, yl, core), there))
     return pairs
 
 
 AXIS = {"a": ("x", "z"), "b": ("z", "x"), "y": ("y", "y")}
-
-
-def shift(values, axis, offset):
-    return lax.ppermute(values, AXES, shift_pairs(AXIS[axis], offset))
+SAME, TURNED, SPLIT = ((1, 1), (3, 3)), ((3, 3), (1, 1)), ((1, 3), (3, 1))
+FAR = (2, 2)
+
+
+def flip(values, axis, flips):
+    return lax.ppermute(values, AXES, partners(AXIS[axis], flips))
 
 
 def swap_cores(values):
     return lax.ppermute(values, AXES, [(d, d ^ 1) for d in range(128)])
 
 
-def gather(values, axis):
-    near = shift(values, axis, 1)
-    back = shift(values, axis, 3)
-    far = shift(values, axis, 2)
-    return [values, near, far, back]
-
-
-def reduce(blocks, axis):
-    near = shift(blocks[1], axis, 3)
-    back = shift(blocks[3], axis, 1)
-    far = shift(blocks[2], axis, 2)
+def gather(values, axis, order):
+    far = flip(values, axis, FAR)
+    return [values, flip(values, axis, order[0]), flip(values, axis, order[1]), far]
+
+
+def gather_forward(values, axis, order):
+    near = flip(values, axis, order[0])
+    back = flip(values, axis, order[1])
+    return [values, near, back, flip(near, axis, order[1])]
+
+
+def reduce(blocks, axis, order):
     f = jnp.float32
+    far = flip(blocks[3], axis, FAR)
+    near = flip(blocks[1], axis, order[0])
+    back = flip(blocks[2], axis, order[1])
     return blocks[0].astype(f) + near.astype(f) + back.astype(f) + far.astype(f)
+
+
+def reduce_forward(blocks, axis, order):
+    f = jnp.float32
+    far = flip(blocks[3], axis, order[1])
+    back = flip(blocks[2], axis, order[1])
+    near = (blocks[1].astype(f) + far.astype(f)).astype(blocks[1].dtype)
+    near = flip(near, axis, order[0])
+    return blocks[0].astype(f) + back.astype(f) + near.astype(f)
 
 
 def normalize(values):
@@ -126,62 +143,143 @@
     return mixed.astype(jnp.bfloat16)
 
 
+STEP = 512
+TURN = (0, 2, 1, 3)
+
+
+def lift_kernel(steps, *refs):
+    x1, x2, x3, gate_cells = refs[0:4], refs[4:8], refs[8:12], refs[12:16]
+    slabs, picks, straight, turned, acc, late = refs[16:20], refs[20], refs[21], refs[22], refs[23], refs[24]
+    one, two, three = steps
+    k = pl.program_id(0)
+    f32 = jnp.float32
+
+    def add(target, parts, fresh):
+        rows = jnp.concatenate([part[...] for part in parts], axis=0)
+        for i, slab in enumerate(slabs):
+            cols = pl.ds(i * 256, 256)
+            product = jnp.dot(rows, slab[0], preferred_element_type=f32)
+            target[:, cols] = product if fresh else target[:, cols] + product
+
+    pl.when(k == 0)(lambda: add(acc, x1, True))
+    pl.when((k > 0) & (k < one))(lambda: add(acc, x1, False))
+    pl.when((k >= one) & (k < one + two))(lambda: add(acc, [x2[i] for i in TURN], False))
+    pl.when(k == one + two)(lambda: add(late, x3, True))
+    pl.when(k > one + two)(lambda: add(late, x3, False))
+
+    @pl.when(k == one + two + three - 1)
+    def _():
+        count = acc.shape[0]
+
+        def turn(values):
+            cells = values.reshape(4, 4, 4, count // 64, values.shape[-1])
+            return jnp.transpose(cells, (2, 1, 0, 3, 4)).reshape(values.shape)
+
+        cells = jnp.concatenate([cell[...] for cell in gate_cells], axis=0).astype(f32)
+        for i in range(2):
+            weight = turn(cells * picks[pl.ds(i, 1), :])
+            weight = jnp.sum(weight, axis=1, keepdims=True)
+            gated = acc[:, pl.ds(512 * i, 256)] + turn(late[:, pl.ds(512 * i, 256)])
+            lifted = acc[:, pl.ds(512 * i + 256, 256)] + turn(late[:, pl.ds(512 * i + 256, 256)])
+            inner = gated / (1.0 + jnp.exp(-gated)) * lifted * weight
+            straight[:, pl.ds(256 * i, 256)] = inner.astype(straight.dtype)
+            turned[:, pl.ds(256 * i, 256)] = turn(inner).astype(turned.dtype)
+
+
+def lift(x1, x2, x3, slabs, picks):
+    steps = x1[0].shape[1] // STEP, x2[0].shape[1] // STEP, (x3[0].shape[1] - LANES) // STEP
+    one, two, three = steps
+    part = x1[0].shape[0]
+    count = 4 * part
+
+    def clamp(start, n):
+        return lambda k: (0, jnp.clip(k - start, 0, n - 1))
+
+    cell = lambda k: (0, three * STEP // LANES)
+    in_specs = (
+        [pl.BlockSpec((part, STEP), clamp(0, one))] * 4
+        + [pl.BlockSpec((part, STEP), clamp(one, two))] * 4
+        + [pl.BlockSpec((part, STEP), clamp(one + two, three))] * 4
+        + [pl.BlockSpec((part, LANES), cell)] * 4
+        + [pl.BlockSpec((1, STEP, 256), lambda k: (0, k, 0))] * 4
+        + [pl.BlockSpec((8, LANES), lambda k: (0, 0))]
+    )
+    out = pl.BlockSpec((count, 512), lambda k: (0, 0))
+    return pl.pallas_call(
+        functools.partial(lift_kernel, steps),
+        grid=(sum(steps),),
+        in_specs=in_specs,
+        out_specs=[out, out],
+        out_shape=[jax.ShapeDtypeStruct((count, 512), jnp.bfloat16)] * 2,
+        scratch_shapes=[pltpu.VMEM((count, 1024), jnp.float32)] * 2,
+        compiler_params=pltpu.CompilerParams(vmem_limit_bytes=40 << 20),
+    )(*x1, *x2, *x3, *x3, *slabs, picks)
+
+
+def lower_kernel(inner, own, other, *outs):
+    rows = inner.shape[0] // 4
+    product = jnp.dot(inner[:, :256], own[0], preferred_element_type=jnp.float32)
+    product += jnp.dot(inner[:, 256:], other[0], preferred_element_type=jnp.float32)
+    for i, out in enumerate(outs):
+        out[...] = product[i * rows : (i + 1) * rows].astype(out.dtype)
+
+
+def lower(inner, own, other, start, width):
+    rows = inner.shape[0] // 4
+    slab = pl.BlockSpec((1, 256, STEP), lambda n: (0, 0, n + start // STEP))
+    return pl.pallas_call(
+        lower_kernel,
+        grid=(width // STEP,),
+        in_specs=[pl.BlockSpec(inner.shape, lambda n: (0, 0)), slab, slab],
+        out_specs=[pl.BlockSpec((rows, STEP), lambda n: (0, n))] * 4,
+        out_shape=[jax.ShapeDtypeStruct((rows, width), jnp.bfloat16)] * 4,
+        compiler_params=pltpu.CompilerParams(vmem_limit_bytes=30 << 20),
+    )(inner, own, other)
+
+
 def body(hidden, router, routes, w_gate, w_up, w_down, w_latent, lengths, latent_cache, queries):
     bf, f32 = jnp.bfloat16, jnp.float32
     rows, width = hidden.shape
     experts = router.shape[1]
-    cut = width // LANES * 2 // 3 // 2 * 2 * LANES + 2 * LANES
-    cut = 38 * LANES if width == 7168 else cut
+    third = 2560
+    cut = 2 * third
     rest = width - cut
     mine = lax.rem(lax.axis_index("dev"), experts)
-
+    other = mine + 1 - 2 * lax.rem(mine, 2)
+
+    other_gate, other_up = swap_cores(w_gate), swap_cores(w_up)
     normed, gates = prepare(router, routes, hidden)
-    other_gate, other_up, other_down = swap_cores(w_gate[0]), swap_cores(w_up[0]), swap_cores(w_down[0])
-
-    first = jnp.stack(gather(normed[:, :cut], "y"))
-    second = jnp.stack(gather(jnp.concatenate([normed[:, cut:], gates], axis=1), "a"))
-    both = gather(jnp.concatenate([first, second], axis=2), "b")
-    first = jnp.stack([block[:, :, :cut] for block in both])
-    second = jnp.stack([block[:, :, cut:] for block in both])
-    firsts = gather(first, "a")
-    seconds = gather(second, "y")
-
-    gates_all = jnp.stack([block[..., rest:] for block in seconds]).astype(f32)
-    gates_all = gates_all[..., :experts] + gates_all[..., experts : 2 * experts]
-    labels = jnp.arange(experts)
-    gate_own = jnp.sum(jnp.where(labels == mine, gates_all, 0.0), axis=-1)
-    gate_other = jnp.sum(jnp.where(labels == mine + 1 - 2 * (mine % 2), gates_all, 0.0), axis=-1)
-    gate_own, gate_other = [
-        jnp.transpose(g, (2, 1, 0, 3)).reshape(-1, 1) for g in (gate_own, gate_other)
-    ]
-
-    count = 64 * rows
-    left = jnp.stack(firsts).reshape(count, cut)
-    right = jnp.transpose(jnp.stack([block[..., :rest] for block in seconds]), (2, 1, 0, 3, 4))
-    right = right.reshape(count, rest)
-
-    def lift(slab):
-        return jnp.dot(left, slab[:cut], preferred_element_type=f32) + jnp.dot(
-            right, slab[cut:], preferred_element_type=f32
-        )
-
-    inner = jnp.concatenate(
-        [
-            (jax.nn.silu(lift(w_gate[0])) * lift(w_up[0]) * gate_own).astype(bf),
-            (jax.nn.silu(lift(other_gate)) * lift(other_up) * gate_other).astype(bf),
-        ],
-        axis=1,
-    )
-    down = jnp.concatenate([w_down[0], other_down], axis=0)
-    inner_turned = jnp.transpose(inner.reshape(4, 4, 4, rows, -1), (2, 1, 0, 3, 4)).reshape(count, -1)
-    first = jnp.dot(inner, down[:, :cut], preferred_element_type=f32).astype(bf)
-    second = jnp.dot(inner_turned, down[:, cut:], preferred_element_type=f32).astype(bf)
-
-    first = reduce(first.reshape(4, 4, 4, rows, cut), "a")
-    second = reduce(second.reshape(4, 4, 4, rows, rest), "y")
-    both = reduce(jnp.concatenate([first, second], axis=3).astype(bf), "b").astype(bf)
-    first = reduce(both[..., :cut], "y")
-    second = reduce(both[..., cut:], "a")
+
+    first = jnp.stack(gather(normed[:, :cut], "y", SPLIT))
+    second = jnp.stack(gather(jnp.concatenate([normed[:, cut:], gates], axis=1), "a", SAME))
+    both, other_gate, other_up = lax.optimization_barrier(
+        (jnp.concatenate([first, second], axis=2), other_gate, other_up)
+    )
+    other_down = swap_cores(w_down)
+    both = jnp.stack(gather(both, "b", SAME))
+    both, other_down = lax.optimization_barrier((both, other_down))
+    flat = (16 * rows, -1)
+    x1 = gather_forward(both[..., :third].reshape(flat), "a", SAME)
+    x2 = gather_forward(both[..., third:cut].reshape(flat), "a", TURNED)
+    x3 = gather_forward(both[..., cut:].reshape(flat), "y", SPLIT)
+
+    spots = jnp.arange(LANES)
+    marks = jnp.stack([(spots == e) | (spots == e + experts) for e in (mine, other)]).astype(f32)
+    picks = jnp.concatenate([marks, jnp.zeros((6, LANES), f32)])
+    straight, turned = lift(x1, x2, x3, (w_gate, w_up, other_gate, other_up), picks)
+    y1 = lower(straight, w_down, other_down, 0, third)
+    y2 = lower(straight, w_down, other_down, third, third)
+    y3 = lower(turned, w_down, other_down, cut, rest)
+    y2 = [y2[i] for i in TURN]
+
+    y1 = reduce_forward(y1, "a", SAME).astype(bf)
+    y2 = reduce_forward(y2, "a", TURNED).astype(bf)
+    y3 = reduce_forward(y3, "y", SPLIT).astype(bf)
+    both = jnp.concatenate([y1, y2, y3], axis=1).reshape(4, 4, rows, width)
+    both = reduce([both[i] for i in range(4)], "b", SAME).astype(bf)
+    first, second = both[..., :cut], both[..., cut:]
+    first = reduce([first[i] for i in range(4)], "y", SPLIT)
+    second = reduce([second[i] for i in range(4)], "a", SAME)
     mixture = jnp.concatenate([first, second], axis=1)
     layer_out = (hidden.astype(f32) + mixture).astype(bf)
 

time: 207 us -> 192 us (0.928)
  Pallas kernels: 0 us -> 28.6 us
  matrix products: 30.8 us -> 7.21 us
  waiting for transfers between devices: 104 us -> 95.7 us
  other arithmetic: 11.8 us -> 6.1 us
  starting transfers between devices: 52.8 us -> 48.4 us
    pallas_call x0 -> x4, Pallas kernels: none -> 28.6 us  [the longest x1 16.4 us: lift(): pl.pallas_call(functools.partial(lift_kernel, steps), grid=(sum(steps),),...]
    dot_general x10 -> x0, matrix products: 23.6 us -> none  [the longest x4 9.51 us: lift(): jnp.dot(left, slab[:cut], preferred_element_type=f32)]
    ppermute x30 -> x36, waiting for transfers between devices: 104 us -> 95.7 us  [flip(): return lax.ppermute(values, AXES, partners(AXIS[axis], flips))]
    another operation x9 -> x3, other arithmetic: 6.7 us -> 0.41 us  [the longest x1 0.28 us: body(): both = jnp.stack(gather(both, 'b', SAME))]
    ppermute x30 -> x36, starting transfers between devices: 52.1 us -> 47.7 us  [flip(): return lax.ppermute(values, AXES, partners(AXIS[axis], flips))]
    another operation x15 -> x1, local copies, waits for them, and re-layouts: 2.86 us -> 0.01 us  [body(): first = jnp.stack(gather(normed[:, :cut], 'y', SPLIT))]
    unnamed x18 -> x22, local copies, waits for them, and re-layouts: 1.43 us -> 3.94 us
  transfers between devices with their start and end apart: 33 -> 39, of which waited for: 18 -> 22; matrix products, arithmetic and copies ran while one was open for 16% -> 4% of each run, Pallas kernels for 0% -> 5%
where the time goes in v2:
time: 192 us; the launch traced here: 191 us
  waiting for transfers between devices  95.7 us (50%)
  starting transfers between devices  48.4 us (25%)
  Pallas kernels  28.6 us (15%)
  matrix products  7.21 us (4%)
  other arithmetic  6.1 us (3%)
  local copies, waits for them, and re-layouts  4.32 us (2%)
    ppermute x36, waiting for transfers between devices, flip(): return lax.ppermute(values, AXES, partners(AXIS[axis], flips))  95.7 us
    ppermute x36, starting transfers between devices, flip(): return lax.ppermute(values, AXES, partners(AXIS[axis], flips))  47.7 us
    pallas_call x1, Pallas kernels, lift(): pl.pallas_call(functools.partial(lift_kernel, steps), grid=(sum(steps),),...  16.4 us
    pallas_call x3, Pallas kernels, lower(): pl.pallas_call(lower_kernel, grid=(width // STEP,), in_specs=[pl.BlockSpe...  12.2 us
    unnamed x22, local copies, waits for them, and re-layouts  3.94 us
  transfers between devices with their start and end apart: 39, of which 22 were waited for; matrix products, arithmetic and copies ran while one was open for 4% of the time, Pallas kernels for 5%

profile of v2, /device:TPU:0, one launch (start us, length us, event | category | flops | bytes accessed | tf_op | source)
XLA Modules:
  0.0 191.4 jit_solution(9063913653388147871)
XLA Ops:
  9.7 2.8 %collective-permute-start.4 = (bf16[8,2176]{1,0:T(8,128)(2,1)S(1)}, bf16[8,2176]{1,0:T(8,128)(2,1)S(1)}, u32[]{:S(2)}, u32[]{:S(2)}) collective-permute-start(bf16[8,2176]{1,0:T(8,128)(2,1)S(1)} %concatenate.23), channel_id=1, source_target_pairs={{0,12},{1,49},{2,14},{3,51},{4,8},{5,53},{6,10},{7,55},{8,4},{9,57... | collective-permute-start | bytes 104456 | tf_op jit(solution)/shard_map/ppermute | solution.py:41
  12.5 2.3 %collective-permute-done.4 = bf16[8,2176]{1,0:T(8,128)(2,1)S(1)} collective-permute-done((bf16[8,2176]{1,0:T(8,128)(2,1)S(1)}, bf16[8,2176]{1,0:T(8,128)(2,1)S(1)}, u32[]{:S(2)}, u32[]{:S(2)}) %collective-permute-start.4) | collective-permute-done | bytes 34848 | tf_op jit(solution)/shard_map/ppermute | solution.py:41
  14.8 1.9 collective-permute-start.5
  16.7 3.5 %collective-permute-done.5 = bf16[8,2176]{1,0:T(8,128)(2,1)S(1)} collective-permute-done((bf16[8,2176]{1,0:T(8,128)(2,1)S(1)}, bf16[8,2176]{1,0:T(8,128)(2,1)S(1)}, u32[]{:S(2)}, u32[]{:S(2)}) %collective-permute-start.5) | collective-permute-done | bytes 34848 | tf_op jit(solution)/shard_map/ppermute | solution.py:41
  20.3 3.1 %collective-permute-start.1 = (bf16[8,5120]{1,0:T(8,128)(2,1)S(1)}, bf16[8,5120]{1,0:T(8,128)(2,1)S(1)}, u32[]{:S(2)}, u32[]{:S(2)}) collective-permute-start(bf16[8,5120]{1,0:T(8,128)(2,1)S(1)} %get-tuple-element.56), channel_id=1, source_target_pairs={{0,66},{1,3},{2,64},{3,1},{4,70},{5,7},{6,68},{7,5},{8,74},{9,11},... | collective-permute-start | bytes 245768 | tf_op jit(solution)/shard_map/ppermute | solution.py:41
  24.0 2.2 %collective-permute-done.1 = bf16[8,5120]{1,0:T(8,128)(2,1)S(1)} collective-permute-done((bf16[8,5120]{1,0:T(8,128)(2,1)S(1)}, bf16[8,5120]{1,0:T(8,128)(2,1)S(1)}, u32[]{:S(2)}, u32[]{:S(2)}) %collective-permute-start.1) | collective-permute-done | bytes 81952 | tf_op jit(solution)/shard_map/ppermute | solution.py:41
  26.2 3.1 %collective-permute-done.2 = bf16[8,5120]{1,0:T(8,128)(2,1)S(1)} collective-permute-done((bf16[8,5120]{1,0:T(8,128)(2,1)S(1)}, bf16[8,5120]{1,0:T(8,128)(2,1)S(1)}, u32[]{:S(2)}, u32[]{:S(2)}) %collective-permute-start.2) | collective-permute-done | bytes 81952 | tf_op jit(solution)/shard_map/ppermute | solution.py:41
  29.4 4.1 %collective-permute-start.9 = (bf16[4,8,7296]{2,1,0:T(8,128)(2,1)S(1)}, bf16[4,8,7296]{2,1,0:T(8,128)(2,1)S(1)}, u32[]{:S(2)}, u32[]{:S(2)}) collective-permute-start(bf16[4,8,7296]{2,1,0:T(8,128)(2,1)S(1)} %maximum_maximum_fusion), channel_id=1, source_target_pairs={{0,48},{1,13},{2,50},{3,15},{4,52},{5,9},{6,54},{7,11},{8,56},{9,5... | collective-permute-start | bytes 1400840 | tf_op jit(solution)/shard_map/ppermute | solution.py:41
  34.5 11.3 %collective-permute-done.9 = bf16[4,8,7296]{2,1,0:T(8,128)(2,1)S(1)} collective-permute-done((bf16[4,8,7296]{2,1,0:T(8,128)(2,1)S(1)}, bf16[4,8,7296]{2,1,0:T(8,128)(2,1)S(1)}, u32[]{:S(2)}, u32[]{:S(2)}) %collective-permute-start.9) | collective-permute-done | bytes 466976 | tf_op jit(solution)/shard_map/ppermute | solution.py:41
  45.8 3.5 %collective-permute-done.8 = bf16[4,8,7296]{2,1,0:T(8,128)(2,1)S(1)} collective-permute-done((bf16[4,8,7296]{2,1,0:T(8,128)(2,1)S(1)}, bf16[4,8,7296]{2,1,0:T(8,128)(2,1)S(1)}, u32[]{:S(2)}, u32[]{:S(2)}) %collective-permute-start.8) | collective-permute-done | bytes 466976 | tf_op jit(solution)/shard_map/ppermute | solution.py:41
  49.7 2.8 %collective-permute-start.15 = (bf16[128,2560]{1,0:T(8,128)(2,1)S(1)}, bf16[128,2560]{1,0:T(8,128)(2,1)}, u32[]{:S(2)}, u32[]{:S(2)}) collective-permute-start(bf16[128,2560]{1,0:T(8,128)(2,1)S(1)} %bitcast.63), channel_id=1, source_target_pairs={{0,12},{1,49},{2,14},{3,51},{4,8},{5,53},{6,10},{7,55},{8,4},{9,57... | collective-permute-start | bytes 1966088 | tf_op jit(solution)/shard_map/ppermute | solution.py:41
  53.3 11.6 %collective-permute-done.18.refs_9_.refs_13_ = bf16[128,2176]{1,0:T(8,128)(2,1)} collective-permute-done((bf16[128,2176]{1,0:T(8,128)(2,1)S(1)}, bf16[128,2176]{1,0:T(8,128)(2,1)}, u32[]{:S(2)}, u32[]{:S(2)}) %collective-permute-start.18) | collective-permute-done | bytes 557088 | tf_op jit(solution)/shard_map/ppermute | solution.py:41
  65.0 2.4 %collective-permute-start.16 = (bf16[128,2560]{1,0:T(8,128)(2,1)S(1)}, bf16[128,2560]{1,0:T(8,128)(2,1)}, u32[]{:S(2)}, u32[]{:S(2)}) collective-permute-start(bf16[128,2560]{1,0:T(8,128)(2,1)S(1)} %bitcast.64), channel_id=1, source_target_pairs={{0,4},{1,17},{2,6},{3,19},{4,0},{5,21},{6,2},{7,23},{8,12},{9,25},... | collective-permute-start | bytes 1966088 | tf_op jit(solution)/shard_map/ppermute | solution.py:41
  68.7 7.3 %collective-permute-done.16.refs_6_ = bf16[128,2560]{1,0:T(8,128)(2,1)} collective-permute-done((bf16[128,2560]{1,0:T(8,128)(2,1)S(1)}, bf16[128,2560]{1,0:T(8,128)(2,1)}, u32[]{:S(2)}, u32[]{:S(2)}) %collective-permute-start.16) | collective-permute-done | bytes 655392 | tf_op jit(solution)/shard_map/ppermute | solution.py:41
  76.0 3.3 %collective-permute-done.20.refs_11_.refs_15_ = bf16[128,2176]{1,0:T(8,128)(2,1)} collective-permute-done((bf16[128,2176]{1,0:T(8,128)(2,1)}, bf16[128,2176]{1,0:T(8,128)(2,1)}, u32[]{:S(2)}, u32[]{:S(2)}) %collective-permute-start.20) | collective-permute-done | bytes 557088 | tf_op jit(solution)/shard_map/ppermute | solution.py:41
  79.5 3.6 %collective-permute-done.17.refs_7_ = bf16[128,2560]{1,0:T(8,128)(2,1)} collective-permute-done((bf16[128,2560]{1,0:T(8,128)(2,1)}, bf16[128,2560]{1,0:T(8,128)(2,1)}, u32[]{:S(2)}, u32[]{:S(2)}) %collective-permute-start.17) | collective-permute-done | bytes 655392 | tf_op jit(solution)/shard_map/ppermute | solution.py:41
  83.0 2.0 %copy-done.2 = bf16[1,7168,256]{2,1,0:T(8,128)(2,1)S(1)} copy-done((bf16[1,7168,256]{2,1,0:T(8,128)(2,1)S(1)}, bf16[1,7168,256]{2,1,0:T(8,128)(2,1)}, u32[]{:S(2)}) %copy-start.2) | copy-done | bytes 3670040
  86.1 16.4 %shard_map.113 = (bf16[512,512]{1,0:T(8,128)(2,1)S(1)}, bf16[512,512]{1,0:T(8,128)(2,1)S(1)}) custom-call(bf16[128,2560]{1,0:T(8,128)(2,1)S(1)} %bitcast.68, bf16[128,2560]{1,0:T(8,128)(2,1)} %collective-permute-done.12.refs_1_, bf16[128,2560]{1,0:T(8,128)(2,1)} %collective-permute-done.13.refs_2_, bf16[128,2560]{1,0:T(8,128)(2,1)} %collective-permute-done.14.refs_3_, ...), custom_call_target="tpu_custom_call" | custom-call | tf_op jit(solution)/shard_map/pallas_call | solution.py:208
  102.6 3.5 %shard_map.116 = (bf16[128,2048]{1,0:T(8,128)(2,1)S(1)}, bf16[128,2048]{1,0:T(8,128)(2,1)S(1)}, bf16[128,2048]{1,0:T(8,128)(2,1)S(1)}, bf16[128,2048]{1,0:T(8,128)(2,1)S(1)}) custom-call(bf16[512,512]{1,0:T(8,128)(2,1)S(1)} %get-tuple-element.35.inner, bf16[1,256,7168]{2,1,0:T(8,128)(2,1)S(1)} %copy-done.1, bf16[1,256,7168]{2,1,0:T(8,128)(2,1)} %collective-permute-done.11.other), custom_call_target="tpu_custom_call" | custom-call | tf_op jit(solution)/shard_map/pallas_call | solution.py:230
  106.1 4.4 %shard_map.114 = (bf16[128,2560]{1,0:T(8,128)(2,1)S(1)}, bf16[128,2560]{1,0:T(8,128)(2,1)S(1)}, bf16[128,2560]{1,0:T(8,128)(2,1)S(1)}, bf16[128,2560]{1,0:T(8,128)(2,1)S(1)}) custom-call(bf16[512,512]{1,0:T(8,128)(2,1)S(1)} %get-tuple-element.25.inner, bf16[1,256,7168]{2,1,0:T(8,128)(2,1)S(1)} %copy-done.1, bf16[1,256,7168]{2,1,0:T(8,128)(2,1)} %collective-permute-done.11.other), custom_call_target="tpu_custom_call" | custom-call | tf_op jit(solution)/shard_map/pallas_call | solution.py:230
  110.7 4.4 %shard_map.115 = (bf16[128,2560]{1,0:T(8,128)(2,1)S(1)}, bf16[128,2560]{1,0:T(8,128)(2,1)S(1)}, bf16[128,2560]{1,0:T(8,128)(2,1)S(1)}, bf16[128,2560]{1,0:T(8,128)(2,1)S(1)}) custom-call(bf16[512,512]{1,0:T(8,128)(2,1)S(1)} %get-tuple-element.25.inner, bf16[1,256,7168]{2,1,0:T(8,128)(2,1)S(1)} %copy-done.1, bf16[1,256,7168]{2,1,0:T(8,128)(2,1)} %collective-permute-done.11.other), custom_call_target="tpu_custom_call" | custom-call | tf_op jit(solution)/shard_map/pallas_call | solution.py:230
  115.1 3.3 %collective-permute-start.21 = (bf16[128,2560]{1,0:T(8,128)(2,1)S(1)}, bf16[128,2560]{1,0:T(8,128)(2,1)S(1)}, u32[]{:S(2)}, u32[]{:S(2)}) collective-permute-start(bf16[128,2560]{1,0:T(8,128)(2,1)S(1)} %get-tuple-element.28), channel_id=1, source_target_pairs={{0,12},{1,49},{2,14},{3,51},{4,8},{5,53},{6,10},{7,55},{8,4},{9,57... | collective-permute-start | bytes 1966088 | tf_op jit(solution)/shard_map/ppermute | solution.py:41
  121.3 2.2 %collective-permute-start.27 = (bf16[128,2048]{1,0:T(8,128)(2,1)S(1)}, bf16[128,2048]{1,0:T(8,128)(2,1)S(1)}, u32[]{:S(2)}, u32[]{:S(2)}) collective-permute-start(bf16[128,2048]{1,0:T(8,128)(2,1)S(1)} %get-tuple-element.37), channel_id=1, source_target_pairs={{0,66},{1,3},{2,64},{3,1},{4,70},{5,7},{6,68},{7,5},{8,74},{9,11},... | collective-permute-start | bytes 1572872 | tf_op jit(solution)/shard_map/ppermute | solution.py:41
  124.0 5.0 %collective-permute-done.25 = bf16[128,2560]{1,0:T(8,128)(2,1)S(1)} collective-permute-done((bf16[128,2560]{1,0:T(8,128)(2,1)S(1)}, bf16[128,2560]{1,0:T(8,128)(2,1)S(1)}, u32[]{:S(2)}, u32[]{:S(2)}) %collective-permute-start.25) | collective-permute-done | bytes 655392 | tf_op jit(solution)/shard_map/ppermute | solution.py:41
  133.3 19.6 %collective-permute-done.23 = bf16[128,2560]{1,0:T(8,128)(2,1)S(1)} collective-permute-done((bf16[128,2560]{1,0:T(8,128)(2,1)S(1)}, bf16[128,2560]{1,0:T(8,128)(2,1)S(1)}, u32[]{:S(2)}, u32[]{:S(2)}) %collective-permute-start.23) | collective-permute-done | bytes 655392 | tf_op jit(solution)/shard_map/ppermute | solution.py:41
  155.2 4.3 %collective-permute-start.31 = (bf16[4,8,7168]{2,1,0:T(8,128)(2,1)S(1)}, bf16[4,8,7168]{2,1,0:T(8,128)(2,1)S(1)}, u32[]{:S(2)}, u32[]{:S(2)}) collective-permute-start(bf16[4,8,7168]{2,1,0:T(8,128)(2,1)S(1)} %get-tuple-element.48), channel_id=1, source_target_pairs={{0,48},{1,13},{2,50},{3,15},{4,52},{5,9},{6,54},{7,11},{8,56},{9,5... | collective-permute-start | bytes 1376264 | tf_op jit(solution)/shard_map/ppermute | solution.py:41
  162.6 7.8 %collective-permute-done.31 = bf16[4,8,7168]{2,1,0:T(8,128)(2,1)S(1)} collective-permute-done((bf16[4,8,7168]{2,1,0:T(8,128)(2,1)S(1)}, bf16[4,8,7168]{2,1,0:T(8,128)(2,1)S(1)}, u32[]{:S(2)}, u32[]{:S(2)}) %collective-permute-start.31) | collective-permute-done | bytes 458784 | tf_op jit(solution)/shard_map/ppermute | solution.py:41
  173.4 3.3 %collective-permute-start.38 = (bf16[8,2048]{1,0:T(8,128)(2,1)S(1)}, bf16[8,2048]{1,0:T(8,128)(2,1)S(1)}, u32[]{:S(2)}, u32[]{:S(2)}) collective-permute-start(bf16[8,2048]{1,0:T(8,128)(2,1)S(1)} %get-tuple-element.53), channel_id=1, source_target_pairs={{0,8},{1,33},{2,10},{3,35},{4,12},{5,37},{6,14},{7,39},{8,0},{9,41... | collective-permute-start | bytes 98312 | tf_op jit(solution)/shard_map/ppermute | solution.py:41
  176.8 3.3 %collective-permute-start.34 = (bf16[8,5120]{1,0:T(8,128)(2,1)S(1)}, bf16[8,5120]{1,0:T(8,128)(2,1)S(1)}, u32[]{:S(2)}, u32[]{:S(2)}) collective-permute-start(bf16[8,5120]{1,0:T(8,128)(2,1)S(1)} %get-tuple-element.51), channel_id=1, source_target_pairs={{0,66},{1,3},{2,64},{3,1},{4,70},{5,7},{6,68},{7,5},{8,74},{9,11},... | collective-permute-start | bytes 245768 | tf_op jit(solution)/shard_map/ppermute | solution.py:41
  182.5 3.5 %collective-permute-done.35 = bf16[8,5120]{1,0:T(8,128)(2,1)S(1)} collective-permute-done((bf16[8,5120]{1,0:T(8,128)(2,1)S(1)}, bf16[8,5120]{1,0:T(8,128)(2,1)S(1)}, u32[]{:S(2)}, u32[]{:S(2)}) %collective-permute-start.35) | collective-permute-done | bytes 81952 | tf_op jit(solution)/shard_map/ppermute | solution.py:41
  186.3 2.2 %fusion.18 = f32[8,576]{1,0:T(8,128)S(1)} fusion(bf16[7168,576]{0,1:T(8,128)(2,1)S(1)} %bitcast.70, bf16[8,7168]{1,0:T(8,128)(2,1)S(1)} %get-tuple-element.43, f32[8]{0:T(128)S(1)} %add_rsqrt_fusion.1), kind=kOutput, calls=%fused_computation.42 | convolution fusion | flops 66232320 | bytes 8390688 | tf_op jit(solution)/shard_map/dot_general | solution.py:129
  189.2 2.2 %add_convert_fusion = bf16[8,128,512]{2,1,0:T(8,128)(2,1)} fusion(bf16[8,384,576]{1,2,0:T(8,128)(2,1)S(1)} %copy-done.5, f32[8,512]{1,0:T(8,128)S(1)} %get-tuple-element.40, f32[8,128]{1,0:T(8,128)S(1)} %get-tuple-element.60, f32[8,128]{1,0:T(8,128)S(1)} %get-tuple-element.59, f32[8,128,384]{2,1,0:T(8,128)S(1)} %get-tuple-element.66, ...), kind=kOutput, calls=%fused_computation.2 | convolution fusion | flops 405929984 | bytes 5798912 | tf_op jit(solution)/shard_map/rhj,rjc->rhc/dot_general | solution.py:121
  (119 shorter events, 34.1 us)
Async XLA Ops:
  0.6 28.7 %collective-permute-start.6 = (bf16[1,7168,256]{2,1,0:T(8,128)(2,1)}, bf16[1,7168,256]{2,1,0:T(8,128)(2,1)}, u32[]{:S(2)}, u32[]{:S(2)}) collective-permute-start(bf16[1,7168,256]{2,1,0:T(8,128)(2,1)} %refs_16_.1), channel_id=1, source_target_pairs={{0,1},{1,0},{2,3},{3,2},{4,5},{5,4},{6,7},{7,6},{8,9},{9,8},{10,11... | collective-permute-start | bytes 11010056 | tf_op jit(solution)/shard_map/ppermute | solution.py:45
  0.7 28.6 %collective-permute-start.7 = (bf16[1,7168,256]{2,1,0:T(8,128)(2,1)}, bf16[1,7168,256]{2,1,0:T(8,128)(2,1)}, u32[]{:S(2)}, u32[]{:S(2)}) collective-permute-start(bf16[1,7168,256]{2,1,0:T(8,128)(2,1)} %refs_17_.1), channel_id=1, source_target_pairs={{0,1},{1,0},{2,3},{3,2},{4,5},{5,4},{6,7},{7,6},{8,9},{9,8},{10,11... | collective-permute-start | bytes 11010056 | tf_op jit(solution)/shard_map/ppermute | solution.py:45
  1.2 48.3 %collective-permute-start.11 = (bf16[1,256,7168]{2,1,0:T(8,128)(2,1)}, bf16[1,256,7168]{2,1,0:T(8,128)(2,1)}, u32[]{:S(2)}, u32[]{:S(2)}) collective-permute-start(bf16[1,256,7168]{2,1,0:T(8,128)(2,1)} %own.5), channel_id=1, source_target_pairs={{0,1},{1,0},{2,3},{3,2},{4,5},{5,4},{6,7},{7,6},{8,9},{9,8},{10,11... | collective-permute-start | bytes 11010056 | tf_op jit(solution)/shard_map/ppermute | solution.py:45
  7.3 16.0 %collective-permute-start = (bf16[8,5120]{1,0:T(8,128)(2,1)S(1)}, bf16[8,5120]{1,0:T(8,128)(2,1)S(1)}, u32[]{:S(2)}, u32[]{:S(2)}) collective-permute-start(bf16[8,5120]{1,0:T(8,128)(2,1)S(1)} %get-tuple-element.56), channel_id=1, source_target_pairs={{0,2},{1,67},{2,0},{3,65},{4,6},{5,71},{6,4},{7,69},{8,10},{9,75},... | collective-permute-start | bytes 245768 | tf_op jit(solution)/shard_map/ppermute | solution.py:41
  20.3 6.0 %collective-permute-start.1 = (bf16[8,5120]{1,0:T(8,128)(2,1)S(1)}, bf16[8,5120]{1,0:T(8,128)(2,1)S(1)}, u32[]{:S(2)}, u32[]{:S(2)}) collective-permute-start(bf16[8,5120]{1,0:T(8,128)(2,1)S(1)} %get-tuple-element.56), channel_id=1, source_target_pairs={{0,66},{1,3},{2,64},{3,1},{4,70},{5,7},{6,68},{7,5},{8,74},{9,11},... | collective-permute-start | bytes 245768 | tf_op jit(solution)/shard_map/ppermute | solution.py:41
  29.4 16.4 %collective-permute-start.9 = (bf16[4,8,7296]{2,1,0:T(8,128)(2,1)S(1)}, bf16[4,8,7296]{2,1,0:T(8,128)(2,1)S(1)}, u32[]{:S(2)}, u32[]{:S(2)}) collective-permute-start(bf16[4,8,7296]{2,1,0:T(8,128)(2,1)S(1)} %maximum_maximum_fusion), channel_id=1, source_target_pairs={{0,48},{1,13},{2,50},{3,15},{4,52},{5,9},{6,54},{7,11},{8,56},{9,5... | collective-permute-start | bytes 1400840 | tf_op jit(solution)/shard_map/ppermute | solution.py:41
  33.5 12.2 %collective-permute-start.10 = (bf16[4,8,7296]{2,1,0:T(8,128)(2,1)S(1)}, bf16[4,8,7296]{2,1,0:T(8,128)(2,1)S(1)}, u32[]{:S(2)}, u32[]{:S(2)}) collective-permute-start(bf16[4,8,7296]{2,1,0:T(8,128)(2,1)S(1)} %maximum_maximum_fusion), channel_id=1, source_target_pairs={{0,32},{1,9},{2,34},{3,11},{4,36},{5,13},{6,38},{7,15},{8,40},{9,1... | collective-permute-start | bytes 1400840 | tf_op jit(solution)/shard_map/ppermute | solution.py:41
  33.5 15.7 %collective-permute-start.8 = (bf16[4,8,7296]{2,1,0:T(8,128)(2,1)S(1)}, bf16[4,8,7296]{2,1,0:T(8,128)(2,1)S(1)}, u32[]{:S(2)}, u32[]{:S(2)}) collective-permute-start(bf16[4,8,7296]{2,1,0:T(8,128)(2,1)S(1)} %maximum_maximum_fusion), channel_id=1, source_target_pairs={{0,16},{1,5},{2,18},{3,7},{4,20},{5,1},{6,22},{7,3},{8,24},{9,13},... | collective-permute-start | bytes 1400840 | tf_op jit(solution)/shard_map/ppermute | solution.py:41
  49.6 17.7 %collective-permute-start.12 = (bf16[128,2560]{1,0:T(8,128)(2,1)S(1)}, bf16[128,2560]{1,0:T(8,128)(2,1)}, u32[]{:S(2)}, u32[]{:S(2)}) collective-permute-start(bf16[128,2560]{1,0:T(8,128)(2,1)S(1)} %bitcast.66), channel_id=1, source_target_pairs={{0,4},{1,17},{2,6},{3,19},{4,0},{5,21},{6,2},{7,23},{8,12},{9,25},... | collective-permute-start | bytes 1966088 | tf_op jit(solution)/shard_map/ppermute | solution.py:41
  49.7 17.6 %collective-permute-start.15 = (bf16[128,2560]{1,0:T(8,128)(2,1)S(1)}, bf16[128,2560]{1,0:T(8,128)(2,1)}, u32[]{:S(2)}, u32[]{:S(2)}) collective-permute-start(bf16[128,2560]{1,0:T(8,128)(2,1)S(1)} %bitcast.63), channel_id=1, source_target_pairs={{0,12},{1,49},{2,14},{3,51},{4,8},{5,53},{6,10},{7,55},{8,4},{9,57... | collective-permute-start | bytes 1966088 | tf_op jit(solution)/shard_map/ppermute | solution.py:41
  52.6 12.4 %collective-permute-start.18 = (bf16[128,2176]{1,0:T(8,128)(2,1)S(1)}, bf16[128,2176]{1,0:T(8,128)(2,1)}, u32[]{:S(2)}, u32[]{:S(2)}) collective-permute-start(bf16[128,2176]{1,0:T(8,128)(2,1)S(1)} %bitcast.59), channel_id=1, source_target_pairs={{0,2},{1,67},{2,0},{3,65},{4,6},{5,71},{6,4},{7,69},{8,10},{9,75},... | collective-permute-start | bytes 1671176 | tf_op jit(solution)/shard_map/ppermute | solution.py:41
  52.7 14.8 %collective-permute-start.19 = (bf16[128,2176]{1,0:T(8,128)(2,1)S(1)}, bf16[128,2176]{1,0:T(8,128)(2,1)S(1)}, u32[]{:S(2)}, u32[]{:S(2)}) collective-permute-start(bf16[128,2176]{1,0:T(8,128)(2,1)S(1)} %bitcast.60), channel_id=1, source_target_pairs={{0,66},{1,3},{2,64},{3,1},{4,70},{5,7},{6,68},{7,5},{8,74},{9,11},... | collective-permute-start | bytes 1671176 | tf_op jit(solution)/shard_map/ppermute | solution.py:41
  52.8 15.9 %collective-permute-start.13 = (bf16[128,2560]{1,0:T(8,128)(2,1)S(1)}, bf16[128,2560]{1,0:T(8,128)(2,1)}, u32[]{:S(2)}, u32[]{:S(2)}) collective-permute-start(bf16[128,2560]{1,0:T(8,128)(2,1)S(1)} %bitcast.67), channel_id=1, source_target_pairs={{0,12},{1,49},{2,14},{3,51},{4,8},{5,53},{6,10},{7,55},{8,4},{9,57... | collective-permute-start | bytes 1966088 | tf_op jit(solution)/shard_map/ppermute | solution.py:41
  65.0 11.0 %collective-permute-start.16 = (bf16[128,2560]{1,0:T(8,128)(2,1)S(1)}, bf16[128,2560]{1,0:T(8,128)(2,1)}, u32[]{:S(2)}, u32[]{:S(2)}) collective-permute-start(bf16[128,2560]{1,0:T(8,128)(2,1)S(1)} %bitcast.64), channel_id=1, source_target_pairs={{0,4},{1,17},{2,6},{3,19},{4,0},{5,21},{6,2},{7,23},{8,12},{9,25},... | collective-permute-start | bytes 1966088 | tf_op jit(solution)/shard_map/ppermute | solution.py:41
  67.3 12.1 %collective-permute-start.14 = (bf16[128,2560]{1,0:T(8,128)(2,1)}, bf16[128,2560]{1,0:T(8,128)(2,1)}, u32[]{:S(2)}, u32[]{:S(2)}) collective-permute-start(bf16[128,2560]{1,0:T(8,128)(2,1)} %collective-permute-done.12.refs_1_), channel_id=1, source_target_pairs={{0,12},{1,49},{2,14},{3,51},{4,8},{5,53},{6,10},{7,55},{8,4},{9,57... | collective-permute-start | bytes 1966088 | tf_op jit(solution)/shard_map/ppermute | solution.py:41
  67.3 15.7 %collective-permute-start.17 = (bf16[128,2560]{1,0:T(8,128)(2,1)}, bf16[128,2560]{1,0:T(8,128)(2,1)}, u32[]{:S(2)}, u32[]{:S(2)}) collective-permute-start(bf16[128,2560]{1,0:T(8,128)(2,1)} %collective-permute-done.15.refs_5_), channel_id=1, source_target_pairs={{0,4},{1,17},{2,6},{3,19},{4,0},{5,21},{6,2},{7,23},{8,12},{9,25},... | collective-permute-start | bytes 1966088 | tf_op jit(solution)/shard_map/ppermute | solution.py:41
  68.3 11.1 %collective-permute-start.20 = (bf16[128,2176]{1,0:T(8,128)(2,1)}, bf16[128,2176]{1,0:T(8,128)(2,1)}, u32[]{:S(2)}, u32[]{:S(2)}) collective-permute-start(bf16[128,2176]{1,0:T(8,128)(2,1)} %collective-permute-done.18.refs_9_.refs_13_), channel_id=1, source_target_pairs={{0,66},{1,3},{2,64},{3,1},{4,70},{5,7},{6,68},{7,5},{8,74},{9,11},... | collective-permute-start | bytes 1671176 | tf_op jit(solution)/shard_map/ppermute | solution.py:41
  106.0 15.3 %collective-permute-start.28 = (bf16[128,2048]{1,0:T(8,128)(2,1)S(1)}, bf16[128,2048]{1,0:T(8,128)(2,1)S(1)}, u32[]{:S(2)}, u32[]{:S(2)}) collective-permute-start(bf16[128,2048]{1,0:T(8,128)(2,1)S(1)} %get-tuple-element.39), channel_id=1, source_target_pairs={{0,66},{1,3},{2,64},{3,1},{4,70},{5,7},{6,68},{7,5},{8,74},{9,11},... | collective-permute-start | bytes 1572872 | tf_op jit(solution)/shard_map/ppermute | solution.py:41
  110.5 13.2 %collective-permute-start.22 = (bf16[128,2560]{1,0:T(8,128)(2,1)S(1)}, bf16[128,2560]{1,0:T(8,128)(2,1)S(1)}, u32[]{:S(2)}, u32[]{:S(2)}) collective-permute-start(bf16[128,2560]{1,0:T(8,128)(2,1)S(1)} %get-tuple-element.30), channel_id=1, source_target_pairs={{0,12},{1,49},{2,14},{3,51},{4,8},{5,53},{6,10},{7,55},{8,4},{9,57... | collective-permute-start | bytes 1966088 | tf_op jit(solution)/shard_map/ppermute | solution.py:41
  115.1 18.2 %collective-permute-start.21 = (bf16[128,2560]{1,0:T(8,128)(2,1)S(1)}, bf16[128,2560]{1,0:T(8,128)(2,1)S(1)}, u32[]{:S(2)}, u32[]{:S(2)}) collective-permute-start(bf16[128,2560]{1,0:T(8,128)(2,1)S(1)} %get-tuple-element.28), channel_id=1, source_target_pairs={{0,12},{1,49},{2,14},{3,51},{4,8},{5,53},{6,10},{7,55},{8,4},{9,57... | collective-permute-start | bytes 1966088 | tf_op jit(solution)/shard_map/ppermute | solution.py:41
  118.4 10.6 %collective-permute-start.25 = (bf16[128,2560]{1,0:T(8,128)(2,1)S(1)}, bf16[128,2560]{1,0:T(8,128)(2,1)S(1)}, u32[]{:S(2)}, u32[]{:S(2)}) collective-permute-start(bf16[128,2560]{1,0:T(8,128)(2,1)S(1)} %get-tuple-element.34), channel_id=1, source_target_pairs={{0,4},{1,17},{2,6},{3,19},{4,0},{5,21},{6,2},{7,23},{8,12},{9,25},... | collective-permute-start | bytes 1966088 | tf_op jit(solution)/shard_map/ppermute | solution.py:41
  119.2 33.9 %collective-permute-start.24 = (bf16[128,2560]{1,0:T(8,128)(2,1)S(1)}, bf16[128,2560]{1,0:T(8,128)(2,1)S(1)}, u32[]{:S(2)}, u32[]{:S(2)}) collective-permute-start(bf16[128,2560]{1,0:T(8,128)(2,1)S(1)} %get-tuple-element.32), channel_id=1, source_target_pairs={{0,4},{1,17},{2,6},{3,19},{4,0},{5,21},{6,2},{7,23},{8,12},{9,25},... | collective-permute-start | bytes 1966088 | tf_op jit(solution)/shard_map/ppermute | solution.py:41
  121.3 10.4 %collective-permute-start.27 = (bf16[128,2048]{1,0:T(8,128)(2,1)S(1)}, bf16[128,2048]{1,0:T(8,128)(2,1)S(1)}, u32[]{:S(2)}, u32[]{:S(2)}) collective-permute-start(bf16[128,2048]{1,0:T(8,128)(2,1)S(1)} %get-tuple-element.37), channel_id=1, source_target_pairs={{0,66},{1,3},{2,64},{3,1},{4,70},{5,7},{6,68},{7,5},{8,74},{9,11},... | collective-permute-start | bytes 1572872 | tf_op jit(solution)/shard_map/ppermute | solution.py:41
  123.7 9.3 %collective-permute-start.29 = (bf16[128,2048]{1,0:T(8,128)(2,1)S(1)}, bf16[128,2048]{1,0:T(8,128)(2,1)S(1)}, u32[]{:S(2)}, u32[]{:S(2)}) collective-permute-start(bf16[128,2048]{1,0:T(8,128)(2,1)S(1)} %add_convert_fusion.6), channel_id=1, source_target_pairs={{0,2},{1,67},{2,0},{3,65},{4,6},{5,71},{6,4},{7,69},{8,10},{9,75},... | collective-permute-start | bytes 1572872 | tf_op jit(solution)/shard_map/ppermute | solution.py:41
  129.0 23.9 %collective-permute-start.23 = (bf16[128,2560]{1,0:T(8,128)(2,1)S(1)}, bf16[128,2560]{1,0:T(8,128)(2,1)S(1)}, u32[]{:S(2)}, u32[]{:S(2)}) collective-permute-start(bf16[128,2560]{1,0:T(8,128)(2,1)S(1)} %add_convert_fusion.4), channel_id=1, source_target_pairs={{0,4},{1,17},{2,6},{3,19},{4,0},{5,21},{6,2},{7,23},{8,12},{9,25},... | collective-permute-start | bytes 1966088 | tf_op jit(solution)/shard_map/ppermute | solution.py:41
  131.7 21.3 %collective-permute-start.26 = (bf16[128,2560]{1,0:T(8,128)(2,1)S(1)}, bf16[128,2560]{1,0:T(8,128)(2,1)S(1)}, u32[]{:S(2)}, u32[]{:S(2)}) collective-permute-start(bf16[128,2560]{1,0:T(8,128)(2,1)S(1)} %add_convert_fusion.2), channel_id=1, source_target_pairs={{0,12},{1,49},{2,14},{3,51},{4,8},{5,53},{6,10},{7,55},{8,4},{9,57... | collective-permute-start | bytes 1966088 | tf_op jit(solution)/shard_map/ppermute | solution.py:41
  153.6 9.0 %collective-permute-start.30 = (bf16[4,8,7168]{2,1,0:T(8,128)(2,1)S(1)}, bf16[4,8,7168]{2,1,0:T(8,128)(2,1)S(1)}, u32[]{:S(2)}, u32[]{:S(2)}) collective-permute-start(bf16[4,8,7168]{2,1,0:T(8,128)(2,1)S(1)} %get-tuple-element.46), channel_id=1, source_target_pairs={{0,16},{1,5},{2,18},{3,7},{4,20},{5,1},{6,22},{7,3},{8,24},{9,13},... | collective-permute-start | bytes 1376264 | tf_op jit(solution)/shard_map/ppermute | solution.py:41
  155.2 15.2 %collective-permute-start.31 = (bf16[4,8,7168]{2,1,0:T(8,128)(2,1)S(1)}, bf16[4,8,7168]{2,1,0:T(8,128)(2,1)S(1)}, u32[]{:S(2)}, u32[]{:S(2)}) collective-permute-start(bf16[4,8,7168]{2,1,0:T(8,128)(2,1)S(1)} %get-tuple-element.48), channel_id=1, source_target_pairs={{0,48},{1,13},{2,50},{3,15},{4,52},{5,9},{6,54},{7,11},{8,56},{9,5... | collective-permute-start | bytes 1376264 | tf_op jit(solution)/shard_map/ppermute | solution.py:41
  159.5 12.7 %collective-permute-start.32 = (bf16[4,8,7168]{2,1,0:T(8,128)(2,1)S(1)}, bf16[4,8,7168]{2,1,0:T(8,128)(2,1)S(1)}, u32[]{:S(2)}, u32[]{:S(2)}) collective-permute-start(bf16[4,8,7168]{2,1,0:T(8,128)(2,1)S(1)} %get-tuple-element.47), channel_id=1, source_target_pairs={{0,32},{1,9},{2,34},{3,11},{4,36},{5,13},{6,38},{7,15},{8,40},{9,1... | collective-permute-start | bytes 1376264 | tf_op jit(solution)/shard_map/ppermute | solution.py:41
  172.5 7.6 %collective-permute-start.36 = (bf16[8,2048]{1,0:T(8,128)(2,1)S(1)}, bf16[8,2048]{1,0:T(8,128)(2,1)S(1)}, u32[]{:S(2)}, u32[]{:S(2)}) collective-permute-start(bf16[8,2048]{1,0:T(8,128)(2,1)S(1)} %get-tuple-element.52), channel_id=1, source_target_pairs={{0,4},{1,17},{2,6},{3,19},{4,0},{5,21},{6,2},{7,23},{8,12},{9,25},... | collective-permute-start | bytes 98312 | tf_op jit(solution)/shard_map/ppermute | solution.py:41
  172.6 8.9 %collective-permute-start.37 = (bf16[8,2048]{1,0:T(8,128)(2,1)S(1)}, bf16[8,2048]{1,0:T(8,128)(2,1)S(1)}, u32[]{:S(2)}, u32[]{:S(2)}) collective-permute-start(bf16[8,2048]{1,0:T(8,128)(2,1)S(1)} %get-tuple-element.54), channel_id=1, source_target_pairs={{0,12},{1,49},{2,14},{3,51},{4,8},{5,53},{6,10},{7,55},{8,4},{9,57... | collective-permute-start | bytes 98312 | tf_op jit(solution)/shard_map/ppermute | solution.py:41
  173.4 8.1 %collective-permute-start.38 = (bf16[8,2048]{1,0:T(8,128)(2,1)S(1)}, bf16[8,2048]{1,0:T(8,128)(2,1)S(1)}, u32[]{:S(2)}, u32[]{:S(2)}) collective-permute-start(bf16[8,2048]{1,0:T(8,128)(2,1)S(1)} %get-tuple-element.53), channel_id=1, source_target_pairs={{0,8},{1,33},{2,10},{3,35},{4,12},{5,37},{6,14},{7,39},{8,0},{9,41... | collective-permute-start | bytes 98312 | tf_op jit(solution)/shard_map/ppermute | solution.py:41
  (18 other events, 315.2 us)

commit v3 on v1

--- a/solution.py
+++ b/solution.py
@@ -1,8 +1,11 @@
+import functools
 import math
 
 import jax
 import jax.numpy as jnp
 from jax import lax
+from jax.experimental import pallas as pl
+from jax.experimental.pallas import tpu as pltpu
 from jax.sharding import PartitionSpec as P
 
 KVL = 512
@@ -15,7 +18,7 @@
     return (((yh * 4 + z) * 4 + x) * 2 + yl) * 2 + core
 
 
-def shift_pairs(core_axes, offset):
+def partners(axes, flips):
     pairs = []
     for yh in range(2):
         for z in range(4):
@@ -23,37 +26,48 @@
                 for yl in range(2):
                     for core in range(2):
                         spot = {"x": x, "y": yh * 2 + yl, "z": z}
-                        axis = core_axes[core]
-                        spot[axis] = (spot[axis] + offset) % 4
+                        spot[axes[core]] ^= flips[core]
                         there = place(spot["y"] // 2, spot["z"], spot["x"], spot["y"] % 2, core)
-                        pairs.append((there, place(yh, z, x, yl, core)))
+                        pairs.append((place(yh, z, x, yl, core), there))
     return pairs
 
 
 AXIS = {"a": ("x", "z"), "b": ("z", "x"), "y": ("y", "y")}
-
-
-def shift(values, axis, offset):
-    return lax.ppermute(values, AXES, shift_pairs(AXIS[axis], offset))
+SAME, TURNED, SPLIT = ((1, 1), (3, 3)), ((3, 3), (1, 1)), ((1, 3), (3, 1))
+FAR = (2, 2)
+
+
+def flip(values, axis, flips):
+    return lax.ppermute(values, AXES, partners(AXIS[axis], flips))
 
 
 def swap_cores(values):
     return lax.ppermute(values, AXES, [(d, d ^ 1) for d in range(128)])
 
 
-def gather(values, axis):
-    near = shift(values, axis, 1)
-    back = shift(values, axis, 3)
-    far = shift(values, axis, 2)
-    return [values, near, far, back]
-
-
-def reduce(blocks, axis):
-    near = shift(blocks[1], axis, 3)
-    back = shift(blocks[3], axis, 1)
-    far = shift(blocks[2], axis, 2)
+def gather(values, axis, order):
+    far = flip(values, axis, FAR)
+    return [values, flip(values, axis, order[0]), flip(values, axis, order[1]), far]
+
+
+def gather_pairs(values, axis, order):
+    own = jnp.concatenate([values, flip(values, axis, order[0])], axis=0)
+    return own, flip(own, axis, order[1])
+
+
+def reduce(blocks, axis, order):
     f = jnp.float32
+    far = flip(blocks[3], axis, FAR)
+    near = flip(blocks[1], axis, order[0])
+    back = flip(blocks[2], axis, order[1])
     return blocks[0].astype(f) + near.astype(f) + back.astype(f) + far.astype(f)
+
+
+def reduce_pairs(keep, send, axis, order):
+    f = jnp.float32
+    total = keep.astype(f) + flip(send, axis, order[1]).astype(f)
+    half = keep.shape[0] // 2
+    return total[:half] + flip(total[half:].astype(keep.dtype), axis, order[0]).astype(f)
 
 
 def normalize(values):
@@ -126,62 +140,238 @@
     return mixed.astype(jnp.bfloat16)
 
 
+HIDDEN = 256
+
+
+def copy_in(pairs, sems):
+    copies = [pltpu.make_async_copy(src, dst, sems.at[i]) for i, (src, dst) in enumerate(pairs)]
+    for copy in copies:
+        copy.start()
+    return copies
+
+
+def spans(widths):
+    starts = [sum(widths[:i]) for i in range(len(widths))]
+    return list(zip(starts, widths))
+
+
+def slab_pairs(slabs, held, widths):
+    return [
+        (slab.at[0, pl.ds(start, width)], held.at[i, pl.ds(start, width)])
+        for start, width in spans(widths)
+        for i, slab in enumerate(slabs)
+    ]
+
+
+def multiply(copies, held, rows, widths, store):
+    for part, (start, width) in enumerate(spans(widths)):
+        for i in range(4):
+            copies[part * 4 + i].wait()
+            store(
+                part,
+                i,
+                jnp.dot(
+                    rows[part][:, :width],
+                    held[i, pl.ds(start, width)],
+                    preferred_element_type=jnp.float32,
+                ),
+            )
+
+
+def early_kernel(widths, x1, x2, x3, s1, s2, s3, s4, h1, h2, h3, held, sems):
+    copies = copy_in(slab_pairs((s1, s2, s3, s4), held, widths), sems)
+    outs = (h1, h2, h3)
+
+    def store(part, i, product):
+        outs[part][:, pl.ds(i * HIDDEN, HIDDEN)] = product
+
+    multiply(copies, held, (x1, x2, x3), widths, store)
+
+
+def early(rows, slabs, widths):
+    count = rows[0].shape[0]
+    vmem, any_ = pl.BlockSpec(memory_space=pltpu.VMEM), pl.BlockSpec(memory_space=pl.ANY)
+    return pl.pallas_call(
+        functools.partial(early_kernel, widths),
+        in_specs=[vmem] * 3 + [any_] * 4,
+        out_specs=[vmem] * 3,
+        out_shape=[jax.ShapeDtypeStruct((count, 4 * HIDDEN), jnp.float32)] * 3,
+        scratch_shapes=[
+            pltpu.VMEM((4, sum(widths), HIDDEN), jnp.bfloat16),
+            pltpu.SemaphoreType.DMA((12,)),
+        ],
+        compiler_params=pltpu.CompilerParams(vmem_limit_bytes=34 << 20),
+    )(*rows, *slabs)
+
+
+def late_kernel(widths, x1, x2, x3, h1, h2, h3, before, picks, s1, s2, s3, s4, own, other, o1, o2, o3, straight, turned, g1, g2, g3, held, low, out1, out2, out3, sems, low_sems, out_sems):
+    f32, bf = jnp.float32, jnp.bfloat16
+    copies = copy_in(slab_pairs((s1, s2, s3, s4), held, widths), sems)
+    low_copies = copy_in(
+        [
+            (slab.at[0, :, pl.ds(start, width)], low.at[pl.ds(i * HIDDEN, HIDDEN), pl.ds(start, width)])
+            for start, width in spans(widths)
+            for i, slab in enumerate((own, other))
+        ],
+        low_sems,
+    )
+    fresh = (g1, g2, g3)
+
+    def store(part, i, product):
+        fresh[part][:, pl.ds(i * HIDDEN, HIDDEN)] = product
+
+    multiply(copies, held, (x1, x2, x3), widths, store)
+    half = x1.shape[0]
+    count, block = 2 * half, half // 2
+
+    def turn(values):
+        cells = values.reshape(4, 4, 4, count // 64, values.shape[-1])
+        return jnp.transpose(cells, (2, 1, 0, 3, 4)).reshape(values.shape)
+
+    def whole(i):
+        cols = pl.ds(i * HIDDEN, HIDDEN)
+        first = jnp.concatenate([h1[:, cols], g1[:, cols]], axis=0)
+        second = jnp.concatenate(
+            [h2[:block, cols], g2[:block, cols], h2[block:, cols], g2[block:, cols]], axis=0
+        )
+        third = jnp.concatenate([h3[:, cols], g3[:, cols]], axis=0)
+        return first + second + turn(third)
+
+    cells = jnp.concatenate([before[...], x3[:, pl.ds(widths[2], LANES)]], axis=0).astype(f32)
+    for i in range(2):
+        weight = turn(cells * picks[pl.ds(i, 1), :])
+        weight = jnp.sum(weight, axis=1, keepdims=True)
+        gated = whole(2 * i)
+        inner = gated / (1.0 + jnp.exp(-gated)) * whole(2 * i + 1) * weight
+        straight[:, pl.ds(HIDDEN * i, HIDDEN)] = inner.astype(bf)
+        turned[:, pl.ds(HIDDEN * i, HIDDEN)] = turn(inner).astype(bf)
+
+    leaving = (
+        straight[half:, :],
+        jnp.concatenate([straight[block:half, :], straight[half + block :, :]], axis=0),
+        turned[half:, :],
+    )
+    out_copies = []
+    for part, (start, width) in enumerate(spans(widths)):
+        low_copies[2 * part].wait()
+        low_copies[2 * part + 1].wait()
+        buffer, out = (out1, out2, out3)[part], (o1, o2, o3)[part]
+        buffer[...] = jnp.dot(leaving[part], low[:, pl.ds(start, width)], preferred_element_type=f32).astype(bf)
+        copy = pltpu.make_async_copy(buffer, out, out_sems.at[part])
+        copy.start()
+        out_copies.append(copy)
+    for copy in out_copies:
+        copy.wait()
+
+
+def late(rows, partial, before, picks, slabs, lows, widths):
+    bf, f32 = jnp.bfloat16, jnp.float32
+    count = rows[0].shape[0]
+    vmem, any_ = pl.BlockSpec(memory_space=pltpu.VMEM), pl.BlockSpec(memory_space=pl.ANY)
+    return pl.pallas_call(
+        functools.partial(late_kernel, widths),
+        in_specs=[vmem] * 8 + [any_] * 6,
+        out_specs=[any_] * 3 + [vmem] * 2,
+        out_shape=[jax.ShapeDtypeStruct((count, width), bf) for width in widths]
+        + [jax.ShapeDtypeStruct((2 * count, 2 * HIDDEN), bf)] * 2,
+        scratch_shapes=[pltpu.VMEM((count, 4 * HIDDEN), f32)] * 3
+        + [
+            pltpu.VMEM((4, sum(widths), HIDDEN), bf),
+            pltpu.VMEM((2 * HIDDEN, sum(widths)), bf),
+        ]
+        + [pltpu.VMEM((count, width), bf) for width in widths]
+        + [
+            pltpu.SemaphoreType.DMA((12,)),
+            pltpu.SemaphoreType.DMA((6,)),
+            pltpu.SemaphoreType.DMA((3,)),
+        ],
+        compiler_params=pltpu.CompilerParams(vmem_limit_bytes=52 << 20),
+    )(*rows, *partial, before, picks, *slabs, *lows)
+
+
+def stay_kernel(widths, straight, turned, own, other, o1, o2, o3, low, sems):
+    copies = copy_in(
+        [
+            (slab.at[0, :, pl.ds(start, width)], low.at[pl.ds(i * HIDDEN, HIDDEN), pl.ds(start, width)])
+            for start, width in spans(widths)
+            for i, slab in enumerate((own, other))
+        ],
+        sems,
+    )
+    half = straight.shape[0] // 2
+    block = half // 2
+    staying = (
+        straight[:half, :],
+        jnp.concatenate([straight[:block, :], straight[half : half + block, :]], axis=0),
+        turned[:half, :],
+    )
+    for part, (start, width) in enumerate(spans(widths)):
+        copies[2 * part].wait()
+        copies[2 * part + 1].wait()
+        product = jnp.dot(staying[part], low[:, pl.ds(start, width)], preferred_element_type=jnp.float32)
+        (o1, o2, o3)[part][...] = product.astype(jnp.bfloat16)
+
+
+def stay(straight, turned, lows, widths):
+    vmem, any_ = pl.BlockSpec(memory_space=pltpu.VMEM), pl.BlockSpec(memory_space=pl.ANY)
+    count = straight.shape[0] // 2
+    return pl.pallas_call(
+        functools.partial(stay_kernel, widths),
+        in_specs=[vmem] * 2 + [any_] * 2,
+        out_specs=[vmem] * 3,
+        out_shape=[jax.ShapeDtypeStruct((count, width), jnp.bfloat16) for width in widths],
+        scratch_shapes=[
+            pltpu.VMEM((2 * HIDDEN, sum(widths)), jnp.bfloat16),
+            pltpu.SemaphoreType.DMA((6,)),
+        ],
+        compiler_params=pltpu.CompilerParams(vmem_limit_bytes=20 << 20),
+    )(straight, turned, *lows)
+
+
 def body(hidden, router, routes, w_gate, w_up, w_down, w_latent, lengths, latent_cache, queries):
     bf, f32 = jnp.bfloat16, jnp.float32
     rows, width = hidden.shape
     experts = router.shape[1]
-    cut = width // LANES * 2 // 3 // 2 * 2 * LANES + 2 * LANES
-    cut = 38 * LANES if width == 7168 else cut
-    rest = width - cut
+    third = 2560
+    cut = 2 * third
+    widths = (third, third, width - cut)
     mine = lax.rem(lax.axis_index("dev"), experts)
-
+    other = mine + 1 - 2 * lax.rem(mine, 2)
+
+    other_gate, other_up = swap_cores(w_gate), swap_cores(w_up)
     normed, gates = prepare(router, routes, hidden)
-    other_gate, other_up, other_down = swap_cores(w_gate[0]), swap_cores(w_up[0]), swap_cores(w_down[0])
-
-    first = jnp.stack(gather(normed[:, :cut], "y"))
-    second = jnp.stack(gather(jnp.concatenate([normed[:, cut:], gates], axis=1), "a"))
-    both = gather(jnp.concatenate([first, second], axis=2), "b")
-    first = jnp.stack([block[:, :, :cut] for block in both])
-    second = jnp.stack([block[:, :, cut:] for block in both])
-    firsts = gather(first, "a")
-    seconds = gather(second, "y")
-
-    gates_all = jnp.stack([block[..., rest:] for block in seconds]).astype(f32)
-    gates_all = gates_all[..., :experts] + gates_all[..., experts : 2 * experts]
-    labels = jnp.arange(experts)
-    gate_own = jnp.sum(jnp.where(labels == mine, gates_all, 0.0), axis=-1)
-    gate_other = jnp.sum(jnp.where(labels == mine + 1 - 2 * (mine % 2), gates_all, 0.0), axis=-1)
-    gate_own, gate_other = [
-        jnp.transpose(g, (2, 1, 0, 3)).reshape(-1, 1) for g in (gate_own, gate_other)
-    ]
-
-    count = 64 * rows
-    left = jnp.stack(firsts).reshape(count, cut)
-    right = jnp.transpose(jnp.stack([block[..., :rest] for block in seconds]), (2, 1, 0, 3, 4))
-    right = right.reshape(count, rest)
-
-    def lift(slab):
-        return jnp.dot(left, slab[:cut], preferred_element_type=f32) + jnp.dot(
-            right, slab[cut:], preferred_element_type=f32
-        )
-
-    inner = jnp.concatenate(
-        [
-            (jax.nn.silu(lift(w_gate[0])) * lift(w_up[0]) * gate_own).astype(bf),
-            (jax.nn.silu(lift(other_gate)) * lift(other_up) * gate_other).astype(bf),
-        ],
-        axis=1,
-    )
-    down = jnp.concatenate([w_down[0], other_down], axis=0)
-    inner_turned = jnp.transpose(inner.reshape(4, 4, 4, rows, -1), (2, 1, 0, 3, 4)).reshape(count, -1)
-    first = jnp.dot(inner, down[:, :cut], preferred_element_type=f32).astype(bf)
-    second = jnp.dot(inner_turned, down[:, cut:], preferred_element_type=f32).astype(bf)
-
-    first = reduce(first.reshape(4, 4, 4, rows, cut), "a")
-    second = reduce(second.reshape(4, 4, 4, rows, rest), "y")
-    both = reduce(jnp.concatenate([first, second], axis=3).astype(bf), "b").astype(bf)
-    first = reduce(both[..., :cut], "y")
-    second = reduce(both[..., cut:], "a")
+
+    first = gather_pairs(normed[None, :, :cut], "y", SPLIT)
+    second = gather_pairs(jnp.concatenate([normed[:, cut:], gates], axis=1)[None], "a", SAME)
+    both = jnp.concatenate([jnp.concatenate(first), jnp.concatenate(second)], axis=2)
+    both, other_gate, other_up = lax.optimization_barrier((both, other_gate, other_up))
+    other_down = swap_cores(w_down)
+    both = jnp.stack(gather(both, "b", SAME))
+    both, other_down = lax.optimization_barrier((both, other_down))
+    flat = (16 * rows, -1)
+    x1 = gather_pairs(both[..., :third].reshape(flat), "a", SAME)
+    x2 = gather_pairs(both[..., third:cut].reshape(flat), "a", TURNED)
+    x3 = gather_pairs(both[..., cut:].reshape(flat), "y", SPLIT)
+
+    spots = jnp.arange(LANES)
+    marks = jnp.stack([(spots == e) | (spots == e + experts) for e in (mine, other)]).astype(f32)
+    picks = jnp.concatenate([marks, jnp.zeros((6, LANES), f32)])
+    slabs, lows = (w_gate, w_up, other_gate, other_up), (w_down, other_down)
+    partial = early((x1[0], x2[0], x3[0]), slabs, widths)
+    before = x3[0][:, widths[2] :]
+    *leaving, straight, turned = late(
+        (x1[1], x2[1], x3[1]), partial, before, picks, slabs, lows, widths
+    )
+    staying = stay(straight, turned, lows, widths)
+
+    y1 = reduce_pairs(staying[0], leaving[0], "a", SAME).astype(bf)
+    y2 = reduce_pairs(staying[1], leaving[1], "a", TURNED).astype(bf)
+    y3 = reduce_pairs(staying[2], leaving[2], "y", SPLIT).astype(bf)
+    both = jnp.concatenate([y1, y2, y3], axis=1).reshape(4, 4, rows, width)
+    both = reduce([both[i] for i in range(4)], "b", SAME).astype(bf)
+    first, second = both[..., :cut], both[..., cut:]
+    first = reduce([first[i] for i in range(4)], "y", SPLIT)
+    second = reduce([second[i] for i in range(4)], "a", SAME)
     mixture = jnp.concatenate([first, second], axis=1)
     layer_out = (hidden.astype(f32) + mixture).astype(bf)
 

time: 207 us -> 173 us (0.84)
  Pallas kernels: 0 us -> 32.9 us
  waiting for transfers between devices: 104 us -> 74.1 us
  matrix products: 30.8 us -> 7.22 us
  starting transfers between devices: 52.8 us -> 39.4 us
  local copies, waits for them, and re-layouts: 5.38 us -> 8.44 us
  other arithmetic: 11.8 us -> 9.53 us
    pallas_call x0 -> x3, Pallas kernels: none -> 32.9 us  [the longest x1 17.5 us: late(): pl.pallas_call(functools.partial(late_kernel, widths), in_specs=[vmem] *...]
    ppermute x30 -> x28, waiting for transfers between devices: 104 us -> 74.1 us  [flip(): return lax.ppermute(values, AXES, partners(AXIS[axis], flips))]
    dot_general x10 -> x0, matrix products: 23.6 us -> none  [the longest x4 9.51 us: lift(): jnp.dot(left, slab[:cut], preferred_element_type=f32)]
    ppermute x30 -> x28, starting transfers between devices: 52.1 us -> 37.6 us  [flip(): return lax.ppermute(values, AXES, partners(AXIS[axis], flips))]
    unnamed x18 -> x28, local copies, waits for them, and re-layouts: 1.43 us -> 7.86 us
    another operation x9 -> x3, other arithmetic: 6.7 us -> 0.41 us  [the longest x1 0.28 us: body(): both = jnp.stack(gather(both, 'b', SAME))]
    concatenate x2 -> x9, other arithmetic: 0.08 us -> 3.37 us  [the longest x6 3.16 us: gather_pairs(): own = jnp.concatenate([values, flip(values, axis, order[0])], axis=0)]
    another operation x15 -> x0, local copies, waits for them, and re-layouts: 2.86 us -> none  [the longest x4 2.72 us: body(): jnp.stack([block[..., :rest] for block in seconds])]
  transfers between devices with their start and end apart: 33 -> 31, of which waited for: 18 -> 18; matrix products, arithmetic and copies ran while one was open for 16% -> 7% of each run, Pallas kernels for 0% -> 9%
where the time goes in v3:
time: 173 us
  waiting for transfers between devices  74.1 us (43%)
  starting transfers between devices  39.4 us (23%)
  Pallas kernels  32.9 us (19%)
  other arithmetic  9.53 us (6%)
  local copies, waits for them, and re-layouts  8.44 us (5%)
  matrix products  7.22 us (4%)
    ppermute x28, waiting for transfers between devices, flip(): return lax.ppermute(values, AXES, partners(AXIS[axis], flips))  74.1 us
    ppermute x28, starting transfers between devices, flip(): return lax.ppermute(values, AXES, partners(AXIS[axis], flips))  37.6 us
    pallas_call x1, Pallas kernels, late(): pl.pallas_call(functools.partial(late_kernel, widths), in_specs=[vmem] *...  17.5 us
    pallas_call x1, Pallas kernels, early(): pl.pallas_call(functools.partial(early_kernel, widths), in_specs=[vmem] *...  11.6 us
    unnamed x28, local copies, waits for them, and re-layouts  7.86 us
    pallas_call x1, Pallas kernels, stay(): pl.pallas_call(functools.partial(stay_kernel, widths), in_specs=[vmem] *...  3.88 us
  transfers between devices with their start and end apart: 31, of which 18 were waited for; matrix products, arithmetic and copies ran while one was open for 7% of the time, Pallas kernels for 9%

profile of v3, /device:TPU:0, one launch (start us, length us, event | category | flops | bytes accessed | tf_op | source)
XLA Modules:
  0.0 172.7 jit_solution(13798198987939937615)
XLA Ops:
  3.3 1.7 %collective-permute-start = (bf16[1,8,5120]{2,1,0:T(8,128)(2,1)S(1)}, bf16[1,8,5120]{2,1,0:T(8,128)(2,1)S(1)}, u32[]{:S(2)}, u32[]{:S(2)}) collective-permute-start(bf16[1,8,5120]{2,1,0:T(8,128)(2,1)S(1)} %slice_bitcast_fusion.8), channel_id=1, source_target_pairs={{0,2},{1,67},{2,0},{3,65},{4,6},{5,71},{6,4},{7,69},{8,10},{9,75},... | collective-permute-start | bytes 245768 | tf_op jit(solution)/shard_map/ppermute | solution.py:41
  12.6 2.8 %collective-permute-start.3 = (bf16[2,8,2176]{2,1,0:T(8,128)(2,1)S(1)}, bf16[2,8,2176]{2,1,0:T(8,128)(2,1)S(1)}, u32[]{:S(2)}, u32[]{:S(2)}) collective-permute-start(bf16[2,8,2176]{2,1,0:T(8,128)(2,1)S(1)} %pad_maximum_fusion.6), channel_id=1, source_target_pairs={{0,12},{1,49},{2,14},{3,51},{4,8},{5,53},{6,10},{7,55},{8,4},{9,57... | collective-permute-start | bytes 208904 | tf_op jit(solution)/shard_map/ppermute | solution.py:41
  15.5 2.8 %collective-permute-done.3 = bf16[2,8,2176]{2,1,0:T(8,128)(2,1)S(1)} collective-permute-done((bf16[2,8,2176]{2,1,0:T(8,128)(2,1)S(1)}, bf16[2,8,2176]{2,1,0:T(8,128)(2,1)S(1)}, u32[]{:S(2)}, u32[]{:S(2)}) %collective-permute-start.3) | collective-permute-done | bytes 69664 | tf_op jit(solution)/shard_map/ppermute | solution.py:41
  18.3 2.0 %collective-permute-start.6 = (bf16[4,8,7296]{2,1,0:T(8,128)(2,1)S(1)}, bf16[4,8,7296]{2,1,0:T(8,128)(2,1)S(1)}, u32[]{:S(2)}, u32[]{:S(2)}) collective-permute-start(bf16[4,8,7296]{2,1,0:T(8,128)(2,1)S(1)} %maximum_maximum_fusion), channel_id=1, source_target_pairs={{0,16},{1,5},{2,18},{3,7},{4,20},{5,1},{6,22},{7,3},{8,24},{9,13},... | collective-permute-start | bytes 1400840 | tf_op jit(solution)/shard_map/ppermute | solution.py:41
  20.3 2.5 %collective-permute-start.7 = (bf16[4,8,7296]{2,1,0:T(8,128)(2,1)S(1)}, bf16[4,8,7296]{2,1,0:T(8,128)(2,1)S(1)}, u32[]{:S(2)}, u32[]{:S(2)}) collective-permute-start(bf16[4,8,7296]{2,1,0:T(8,128)(2,1)S(1)} %maximum_maximum_fusion), channel_id=1, source_target_pairs={{0,48},{1,13},{2,50},{3,15},{4,52},{5,9},{6,54},{7,11},{8,56},{9,5... | collective-permute-start | bytes 1400840 | tf_op jit(solution)/shard_map/ppermute | solution.py:41
  23.9 3.1 %collective-permute-done.6 = bf16[4,8,7296]{2,1,0:T(8,128)(2,1)S(1)} collective-permute-done((bf16[4,8,7296]{2,1,0:T(8,128)(2,1)S(1)}, bf16[4,8,7296]{2,1,0:T(8,128)(2,1)S(1)}, u32[]{:S(2)}, u32[]{:S(2)}) %collective-permute-start.6) | collective-permute-done | bytes 466976 | tf_op jit(solution)/shard_map/ppermute | solution.py:41
  26.9 7.0 %collective-permute-done.7 = bf16[4,8,7296]{2,1,0:T(8,128)(2,1)S(1)} collective-permute-done((bf16[4,8,7296]{2,1,0:T(8,128)(2,1)S(1)}, bf16[4,8,7296]{2,1,0:T(8,128)(2,1)S(1)}, u32[]{:S(2)}, u32[]{:S(2)}) %collective-permute-start.7) | collective-permute-done | bytes 466976 | tf_op jit(solution)/shard_map/ppermute | solution.py:41
  33.9 1.5 collective-permute-done.8
  35.8 2.8 %collective-permute-start.12 = (bf16[128,2560]{1,0:T(8,128)(2,1)S(1)}, bf16[128,2560]{1,0:T(8,128)(2,1)S(1)}, u32[]{:S(2)}, u32[]{:S(2)}) collective-permute-start(bf16[128,2560]{1,0:T(8,128)(2,1)S(1)} %bitcast.60), channel_id=1, source_target_pairs={{0,12},{1,49},{2,14},{3,51},{4,8},{5,53},{6,10},{7,55},{8,4},{9,57... | collective-permute-start | bytes 1966088 | tf_op jit(solution)/shard_map/ppermute | solution.py:41
  38.9 8.8 %collective-permute-done.12 = bf16[128,2560]{1,0:T(8,128)(2,1)S(1)} collective-permute-done((bf16[128,2560]{1,0:T(8,128)(2,1)S(1)}, bf16[128,2560]{1,0:T(8,128)(2,1)S(1)}, u32[]{:S(2)}, u32[]{:S(2)}) %collective-permute-start.12) | collective-permute-done | bytes 655392 | tf_op jit(solution)/shard_map/ppermute | solution.py:41
  55.5 2.0 %copy-done.2 = bf16[1,7168,256]{2,1,0:T(8,128)(2,1)S(1)} copy-done((bf16[1,7168,256]{2,1,0:T(8,128)(2,1)S(1)}, bf16[1,7168,256]{2,1,0:T(8,128)(2,1)}, u32[]{:S(2)}) %copy-start.2) | copy-done | bytes 3670040
  57.5 2.0 %copy-done.3 = bf16[1,7168,256]{2,1,0:T(8,128)(2,1)S(1)} copy-done((bf16[1,7168,256]{2,1,0:T(8,128)(2,1)S(1)}, bf16[1,7168,256]{2,1,0:T(8,128)(2,1)}, u32[]{:S(2)}) %copy-start.3) | copy-done | bytes 3670040
  59.5 11.6 %shard_map.113 = (f32[256,1024]{1,0:T(8,128)S(1)}, f32[256,1024]{1,0:T(8,128)S(1)}, f32[256,1024]{1,0:T(8,128)S(1)}) custom-call(bf16[256,2560]{1,0:T(8,128)(2,1)} %pad_maximum_fusion.2.x1, bf16[256,2560]{1,0:T(8,128)(2,1)S(1)} %pad_maximum_fusion.3.x2, bf16[256,2176]{1,0:T(8,128)(2,1)} %pad_maximum_fusion.4.x3, bf16[1,7168,256]{2,1,0:T(8,128)(2,1)S(1)} %copy-done.2, ...), custom_call_target="tpu_custom_call" | custom-call | tf_op jit(solution)/shard_map/pallas_call | solution.py:194
  74.1 17.5 %shard_map.114 = (bf16[256,2560]{1,0:T(8,128)(2,1)}, bf16[256,2560]{1,0:T(8,128)(2,1)}, bf16[256,2048]{1,0:T(8,128)(2,1)}, bf16[512,512]{1,0:T(8,128)(2,1)S(1)}, bf16[512,512]{1,0:T(8,128)(2,1)S(1)}) custom-call(bf16[256,2560]{1,0:T(8,128)(2,1)} %collective-permute-done.11.x1, bf16[256,2560]{1,0:T(8,128)(2,1)} %collective-permute-done.13.x2, ...), custom_call_target="tpu_custom_call" | custom-call | tf_op jit(solution)/shard_map/pallas_call | solution.py:271
  91.6 2.4 %collective-permute-start.20 = (bf16[256,2048]{1,0:T(8,128)(2,1)}, bf16[256,2048]{1,0:T(8,128)(2,1)S(1)}, u32[]{:S(2)}, u32[]{:S(2)}) collective-permute-start(bf16[256,2048]{1,0:T(8,128)(2,1)} %get-tuple-element.33), channel_id=1, source_target_pairs={{0,66},{1,3},{2,64},{3,1},{4,70},{5,7},{6,68},{7,5},{8,74},{9,11},... | collective-permute-start | bytes 3145736 | tf_op jit(solution)/shard_map/ppermute | solution.py:41
  94.0 1.8 %collective-permute-start.16 = (bf16[256,2560]{1,0:T(8,128)(2,1)}, bf16[256,2560]{1,0:T(8,128)(2,1)S(1)}, u32[]{:S(2)}, u32[]{:S(2)}) collective-permute-start(bf16[256,2560]{1,0:T(8,128)(2,1)} %get-tuple-element.29), channel_id=1, source_target_pairs={{0,12},{1,49},{2,14},{3,51},{4,8},{5,53},{6,10},{7,55},{8,4},{9,57... | collective-permute-start | bytes 3932168 | tf_op jit(solution)/shard_map/ppermute | solution.py:41
  96.2 3.9 %shard_map.115 = (bf16[256,2560]{1,0:T(8,128)(2,1)S(1)}, bf16[256,2560]{1,0:T(8,128)(2,1)S(1)}, bf16[256,2048]{1,0:T(8,128)(2,1)S(1)}) custom-call(bf16[512,512]{1,0:T(8,128)(2,1)S(1)} %get-tuple-element.26.straight, bf16[512,512]{1,0:T(8,128)(2,1)S(1)} %get-tuple-element.27.turned, bf16[1,256,7168]{2,1,0:T(8,128)(2,1)S(1)} %copy-done.1, ...), custom_call_target="tpu_custom_call" | custom-call | tf_op jit(solution)/shard_map/pallas_call | solution.py:318
  100.0 10.6 %collective-permute-done.20 = bf16[256,2048]{1,0:T(8,128)(2,1)S(1)} collective-permute-done((bf16[256,2048]{1,0:T(8,128)(2,1)}, bf16[256,2048]{1,0:T(8,128)(2,1)S(1)}, u32[]{:S(2)}, u32[]{:S(2)}) %collective-permute-start.20) | collective-permute-done | bytes 1048608 | tf_op jit(solution)/shard_map/ppermute | solution.py:41
  111.2 1.8 %collective-permute-done.16 = bf16[256,2560]{1,0:T(8,128)(2,1)S(1)} collective-permute-done((bf16[256,2560]{1,0:T(8,128)(2,1)}, bf16[256,2560]{1,0:T(8,128)(2,1)S(1)}, u32[]{:S(2)}, u32[]{:S(2)}) %collective-permute-start.16) | collective-permute-done | bytes 1310752 | tf_op jit(solution)/shard_map/ppermute | solution.py:41
  115.9 4.5 %collective-permute-done.21 = bf16[128,2048]{1,0:T(8,128)(2,1)S(1)} collective-permute-done((bf16[128,2048]{1,0:T(8,128)(2,1)S(1)}, bf16[128,2048]{1,0:T(8,128)(2,1)S(1)}, u32[]{:S(2)}, u32[]{:S(2)}) %collective-permute-start.21) | collective-permute-done | bytes 524320 | tf_op jit(solution)/shard_map/ppermute | solution.py:41
  120.5 6.8 %collective-permute-done.17 = bf16[128,2560]{1,0:T(8,128)(2,1)S(1)} collective-permute-done((bf16[128,2560]{1,0:T(8,128)(2,1)S(1)}, bf16[128,2560]{1,0:T(8,128)(2,1)S(1)}, u32[]{:S(2)}, u32[]{:S(2)}) %collective-permute-start.17) | collective-permute-done | bytes 655392 | tf_op jit(solution)/shard_map/ppermute | solution.py:41
  127.4 8.7 %collective-permute-done.19 = bf16[128,2560]{1,0:T(8,128)(2,1)S(1)} collective-permute-done((bf16[128,2560]{1,0:T(8,128)(2,1)S(1)}, bf16[128,2560]{1,0:T(8,128)(2,1)S(1)}, u32[]{:S(2)}, u32[]{:S(2)}) %collective-permute-start.19) | collective-permute-done | bytes 655392 | tf_op jit(solution)/shard_map/ppermute | solution.py:41
  136.6 4.5 %collective-permute-start.23 = (bf16[4,8,7168]{2,1,0:T(8,128)(2,1)S(1)}, bf16[4,8,7168]{2,1,0:T(8,128)(2,1)S(1)}, u32[]{:S(2)}, u32[]{:S(2)}) collective-permute-start(bf16[4,8,7168]{2,1,0:T(8,128)(2,1)S(1)} %get-tuple-element.42), channel_id=1, source_target_pairs={{0,48},{1,13},{2,50},{3,15},{4,52},{5,9},{6,54},{7,11},{8,56},{9,5... | collective-permute-start | bytes 1376264 | tf_op jit(solution)/shard_map/ppermute | solution.py:41
  142.8 2.6 %collective-permute-done.22 = bf16[4,8,7168]{2,1,0:T(8,128)(2,1)S(1)} collective-permute-done((bf16[4,8,7168]{2,1,0:T(8,128)(2,1)S(1)}, bf16[4,8,7168]{2,1,0:T(8,128)(2,1)S(1)}, u32[]{:S(2)}, u32[]{:S(2)}) %collective-permute-start.22) | collective-permute-done | bytes 458784 | tf_op jit(solution)/shard_map/ppermute | solution.py:41
  145.4 6.6 %collective-permute-done.23 = bf16[4,8,7168]{2,1,0:T(8,128)(2,1)S(1)} collective-permute-done((bf16[4,8,7168]{2,1,0:T(8,128)(2,1)S(1)}, bf16[4,8,7168]{2,1,0:T(8,128)(2,1)S(1)}, u32[]{:S(2)}, u32[]{:S(2)}) %collective-permute-start.23) | collective-permute-done | bytes 458784 | tf_op jit(solution)/shard_map/ppermute | solution.py:41
  153.8 3.4 %collective-permute-start.30 = (bf16[8,2048]{1,0:T(8,128)(2,1)S(1)}, bf16[8,2048]{1,0:T(8,128)(2,1)S(1)}, u32[]{:S(2)}, u32[]{:S(2)}) collective-permute-start(bf16[8,2048]{1,0:T(8,128)(2,1)S(1)} %get-tuple-element.47), channel_id=1, source_target_pairs={{0,8},{1,33},{2,10},{3,35},{4,12},{5,37},{6,14},{7,39},{8,0},{9,41... | collective-permute-start | bytes 98312 | tf_op jit(solution)/shard_map/ppermute | solution.py:41
  157.3 1.5 collective-permute-start.25
  158.8 2.6 %collective-permute-start.26 = (bf16[8,5120]{1,0:T(8,128)(2,1)S(1)}, bf16[8,5120]{1,0:T(8,128)(2,1)S(1)}, u32[]{:S(2)}, u32[]{:S(2)}) collective-permute-start(bf16[8,5120]{1,0:T(8,128)(2,1)S(1)} %get-tuple-element.45), channel_id=1, source_target_pairs={{0,66},{1,3},{2,64},{3,1},{4,70},{5,7},{6,68},{7,5},{8,74},{9,11},... | collective-permute-start | bytes 245768 | tf_op jit(solution)/shard_map/ppermute | solution.py:41
  161.8 2.7 %collective-permute-done.26 = bf16[8,5120]{1,0:T(8,128)(2,1)S(1)} collective-permute-done((bf16[8,5120]{1,0:T(8,128)(2,1)S(1)}, bf16[8,5120]{1,0:T(8,128)(2,1)S(1)}, u32[]{:S(2)}, u32[]{:S(2)}) %collective-permute-start.26) | collective-permute-done | bytes 81952 | tf_op jit(solution)/shard_map/ppermute | solution.py:41
  164.5 2.9 %collective-permute-done.27 = bf16[8,5120]{1,0:T(8,128)(2,1)S(1)} collective-permute-done((bf16[8,5120]{1,0:T(8,128)(2,1)S(1)}, bf16[8,5120]{1,0:T(8,128)(2,1)S(1)}, u32[]{:S(2)}, u32[]{:S(2)}) %collective-permute-start.27) | collective-permute-done | bytes 81952 | tf_op jit(solution)/shard_map/ppermute | solution.py:41
  167.6 2.2 %fusion.21 = f32[8,576]{1,0:T(8,128)S(1)} fusion(bf16[7168,576]{0,1:T(8,128)(2,1)S(1)} %bitcast.54, bf16[8,7168]{1,0:T(8,128)(2,1)S(1)} %get-tuple-element.37, f32[8]{0:T(128)S(1)} %add_rsqrt_fusion.1), kind=kOutput, calls=%fused_computation.54 | convolution fusion | flops 66232320 | bytes 8390688 | tf_op jit(solution)/shard_map/dot_general | solution.py:126
  170.6 2.2 %add_convert_fusion = bf16[8,128,512]{2,1,0:T(8,128)(2,1)} fusion(bf16[8,384,576]{1,2,0:T(8,128)(2,1)S(1)} %copy-done.7, f32[8,512]{1,0:T(8,128)S(1)} %get-tuple-element.34, f32[8,128]{1,0:T(8,128)S(1)} %get-tuple-element.52, f32[8,128]{1,0:T(8,128)S(1)} %get-tuple-element.51, f32[8,128,384]{2,1,0:T(8,128)S(1)} %get-tuple-element.58, ...), kind=kOutput, calls=%fused_computation.4 | convolution fusion | flops 405929984 | bytes 5798912 | tf_op jit(solution)/shard_map/rhj,rjc->rhc/dot_general | solution.py:118
  (117 shorter events, 31.9 us)
Async XLA Ops:
  0.6 140.5 %copy-start = (bf16[8,128,576]{1,2,0:T(8,128)(2,1)S(1)}, bf16[8,128,576]{1,2,0:T(8,128)(2,1)}, u32[]{:S(2)}) copy-start(bf16[8,128,576]{1,2,0:T(8,128)(2,1)} %param.19) | copy-start | bytes 3538948
  0.6 17.6 %collective-permute-start.4 = (bf16[1,7168,256]{2,1,0:T(8,128)(2,1)}, bf16[1,7168,256]{2,1,0:T(8,128)(2,1)}, u32[]{:S(2)}, u32[]{:S(2)}) collective-permute-start(bf16[1,7168,256]{2,1,0:T(8,128)(2,1)} %s1_.3), channel_id=1, source_target_pairs={{0,1},{1,0},{2,3},{3,2},{4,5},{5,4},{6,7},{7,6},{8,9},{9,8},{10,11... | collective-permute-start | bytes 11010056 | tf_op jit(solution)/shard_map/ppermute | solution.py:45
  0.7 17.5 %collective-permute-start.5 = (bf16[1,7168,256]{2,1,0:T(8,128)(2,1)}, bf16[1,7168,256]{2,1,0:T(8,128)(2,1)}, u32[]{:S(2)}, u32[]{:S(2)}) collective-permute-start(bf16[1,7168,256]{2,1,0:T(8,128)(2,1)} %s2_.3), channel_id=1, source_target_pairs={{0,1},{1,0},{2,3},{3,2},{4,5},{5,4},{6,7},{7,6},{8,9},{9,8},{10,11... | collective-permute-start | bytes 11010056 | tf_op jit(solution)/shard_map/ppermute | solution.py:45
  3.3 6.8 %collective-permute-start = (bf16[1,8,5120]{2,1,0:T(8,128)(2,1)S(1)}, bf16[1,8,5120]{2,1,0:T(8,128)(2,1)S(1)}, u32[]{:S(2)}, u32[]{:S(2)}) collective-permute-start(bf16[1,8,5120]{2,1,0:T(8,128)(2,1)S(1)} %slice_bitcast_fusion.8), channel_id=1, source_target_pairs={{0,2},{1,67},{2,0},{3,65},{4,6},{5,71},{6,4},{7,69},{8,10},{9,75},... | collective-permute-start | bytes 245768 | tf_op jit(solution)/shard_map/ppermute | solution.py:41
  5.1 30.6 %collective-permute-start.9 = (bf16[1,256,7168]{2,1,0:T(8,128)(2,1)}, bf16[1,256,7168]{2,1,0:T(8,128)(2,1)}, u32[]{:S(2)}, u32[]{:S(2)}) collective-permute-start(bf16[1,256,7168]{2,1,0:T(8,128)(2,1)} %own.3), channel_id=1, source_target_pairs={{0,1},{1,0},{2,3},{3,2},{4,5},{5,4},{6,7},{7,6},{8,9},{9,8},{10,11... | collective-permute-start | bytes 11010056 | tf_op jit(solution)/shard_map/ppermute | solution.py:45
  8.7 3.9 %collective-permute-start.2 = (bf16[1,8,2176]{2,1,0:T(8,128)(2,1)S(1)}, bf16[1,8,2176]{2,1,0:T(8,128)(2,1)S(1)}, u32[]{:S(2)}, u32[]{:S(2)}) collective-permute-start(bf16[1,8,2176]{2,1,0:T(8,128)(2,1)S(1)} %bitcast.66), channel_id=1, source_target_pairs={{0,4},{1,17},{2,6},{3,19},{4,0},{5,21},{6,2},{7,23},{8,12},{9,25},... | collective-permute-start | bytes 104456 | tf_op jit(solution)/shard_map/ppermute | solution.py:41
  10.2 8.0 %collective-permute-start.1 = (bf16[2,8,5120]{2,1,0:T(8,128)(2,1)S(1)}, bf16[2,8,5120]{2,1,0:T(8,128)(2,1)S(1)}, u32[]{:S(2)}, u32[]{:S(2)}) collective-permute-start(bf16[2,8,5120]{2,1,0:T(8,128)(2,1)S(1)} %pad_maximum_fusion.5), channel_id=1, source_target_pairs={{0,66},{1,3},{2,64},{3,1},{4,70},{5,7},{6,68},{7,5},{8,74},{9,11},... | collective-permute-start | bytes 491528 | tf_op jit(solution)/shard_map/ppermute | solution.py:41
  12.6 5.6 %collective-permute-start.3 = (bf16[2,8,2176]{2,1,0:T(8,128)(2,1)S(1)}, bf16[2,8,2176]{2,1,0:T(8,128)(2,1)S(1)}, u32[]{:S(2)}, u32[]{:S(2)}) collective-permute-start(bf16[2,8,2176]{2,1,0:T(8,128)(2,1)S(1)} %pad_maximum_fusion.6), channel_id=1, source_target_pairs={{0,12},{1,49},{2,14},{3,51},{4,8},{5,53},{6,10},{7,55},{8,4},{9,57... | collective-permute-start | bytes 208904 | tf_op jit(solution)/shard_map/ppermute | solution.py:41
  18.3 8.6 %collective-permute-start.6 = (bf16[4,8,7296]{2,1,0:T(8,128)(2,1)S(1)}, bf16[4,8,7296]{2,1,0:T(8,128)(2,1)S(1)}, u32[]{:S(2)}, u32[]{:S(2)}) collective-permute-start(bf16[4,8,7296]{2,1,0:T(8,128)(2,1)S(1)} %maximum_maximum_fusion), channel_id=1, source_target_pairs={{0,16},{1,5},{2,18},{3,7},{4,20},{5,1},{6,22},{7,3},{8,24},{9,13},... | collective-permute-start | bytes 1400840 | tf_op jit(solution)/shard_map/ppermute | solution.py:41
  20.3 13.6 %collective-permute-start.7 = (bf16[4,8,7296]{2,1,0:T(8,128)(2,1)S(1)}, bf16[4,8,7296]{2,1,0:T(8,128)(2,1)S(1)}, u32[]{:S(2)}, u32[]{:S(2)}) collective-permute-start(bf16[4,8,7296]{2,1,0:T(8,128)(2,1)S(1)} %maximum_maximum_fusion), channel_id=1, source_target_pairs={{0,48},{1,13},{2,50},{3,15},{4,52},{5,9},{6,54},{7,11},{8,56},{9,5... | collective-permute-start | bytes 1400840 | tf_op jit(solution)/shard_map/ppermute | solution.py:41
  22.8 12.6 %collective-permute-start.8 = (bf16[4,8,7296]{2,1,0:T(8,128)(2,1)S(1)}, bf16[4,8,7296]{2,1,0:T(8,128)(2,1)S(1)}, u32[]{:S(2)}, u32[]{:S(2)}) collective-permute-start(bf16[4,8,7296]{2,1,0:T(8,128)(2,1)S(1)} %maximum_maximum_fusion), channel_id=1, source_target_pairs={{0,32},{1,9},{2,34},{3,11},{4,36},{5,13},{6,38},{7,15},{8,40},{9,1... | collective-permute-start | bytes 1400840 | tf_op jit(solution)/shard_map/ppermute | solution.py:41
  35.8 11.9 %collective-permute-start.12 = (bf16[128,2560]{1,0:T(8,128)(2,1)S(1)}, bf16[128,2560]{1,0:T(8,128)(2,1)S(1)}, u32[]{:S(2)}, u32[]{:S(2)}) collective-permute-start(bf16[128,2560]{1,0:T(8,128)(2,1)S(1)} %bitcast.60), channel_id=1, source_target_pairs={{0,12},{1,49},{2,14},{3,51},{4,8},{5,53},{6,10},{7,55},{8,4},{9,57... | collective-permute-start | bytes 1966088 | tf_op jit(solution)/shard_map/ppermute | solution.py:41
  38.7 10.6 %collective-permute-start.10 = (bf16[128,2560]{1,0:T(8,128)(2,1)S(1)}, bf16[128,2560]{1,0:T(8,128)(2,1)S(1)}, u32[]{:S(2)}, u32[]{:S(2)}) collective-permute-start(bf16[128,2560]{1,0:T(8,128)(2,1)S(1)} %bitcast.58), channel_id=1, source_target_pairs={{0,4},{1,17},{2,6},{3,19},{4,0},{5,21},{6,2},{7,23},{8,12},{9,25},... | collective-permute-start | bytes 1966088 | tf_op jit(solution)/shard_map/ppermute | solution.py:41
  38.7 13.1 %collective-permute-start.14 = (bf16[128,2176]{1,0:T(8,128)(2,1)S(1)}, bf16[128,2176]{1,0:T(8,128)(2,1)S(1)}, u32[]{:S(2)}, u32[]{:S(2)}) collective-permute-start(bf16[128,2176]{1,0:T(8,128)(2,1)S(1)} %bitcast.55), channel_id=1, source_target_pairs={{0,2},{1,67},{2,0},{3,65},{4,6},{5,71},{6,4},{7,69},{8,10},{9,75},... | collective-permute-start | bytes 1671176 | tf_op jit(solution)/shard_map/ppermute | solution.py:41
  47.8 26.3 %collective-permute-start.13 = (bf16[256,2560]{1,0:T(8,128)(2,1)S(1)}, bf16[256,2560]{1,0:T(8,128)(2,1)}, u32[]{:S(2)}, u32[]{:S(2)}) collective-permute-start(bf16[256,2560]{1,0:T(8,128)(2,1)S(1)} %pad_maximum_fusion.3.x2), channel_id=1, source_target_pairs={{0,4},{1,17},{2,6},{3,19},{4,0},{5,21},{6,2},{7,23},{8,12},{9,25},... | collective-permute-start | bytes 3932168 | tf_op jit(solution)/shard_map/ppermute | solution.py:41
  50.4 23.7 %collective-permute-start.11 = (bf16[256,2560]{1,0:T(8,128)(2,1)}, bf16[256,2560]{1,0:T(8,128)(2,1)}, u32[]{:S(2)}, u32[]{:S(2)}) collective-permute-start(bf16[256,2560]{1,0:T(8,128)(2,1)} %pad_maximum_fusion.2.x1), channel_id=1, source_target_pairs={{0,12},{1,49},{2,14},{3,51},{4,8},{5,53},{6,10},{7,55},{8,4},{9,57... | collective-permute-start | bytes 3932168 | tf_op jit(solution)/shard_map/ppermute | solution.py:41
  53.7 20.4 %collective-permute-start.15 = (bf16[256,2176]{1,0:T(8,128)(2,1)}, bf16[256,2176]{1,0:T(8,128)(2,1)}, u32[]{:S(2)}, u32[]{:S(2)}) collective-permute-start(bf16[256,2176]{1,0:T(8,128)(2,1)} %pad_maximum_fusion.4.x3), channel_id=1, source_target_pairs={{0,66},{1,3},{2,64},{3,1},{4,70},{5,7},{6,68},{7,5},{8,74},{9,11},... | collective-permute-start | bytes 3342344 | tf_op jit(solution)/shard_map/ppermute | solution.py:41
  91.6 19.1 %collective-permute-start.20 = (bf16[256,2048]{1,0:T(8,128)(2,1)}, bf16[256,2048]{1,0:T(8,128)(2,1)S(1)}, u32[]{:S(2)}, u32[]{:S(2)}) collective-permute-start(bf16[256,2048]{1,0:T(8,128)(2,1)} %get-tuple-element.33), channel_id=1, source_target_pairs={{0,66},{1,3},{2,64},{3,1},{4,70},{5,7},{6,68},{7,5},{8,74},{9,11},... | collective-permute-start | bytes 3145736 | tf_op jit(solution)/shard_map/ppermute | solution.py:41
  94.0 19.0 %collective-permute-start.16 = (bf16[256,2560]{1,0:T(8,128)(2,1)}, bf16[256,2560]{1,0:T(8,128)(2,1)S(1)}, u32[]{:S(2)}, u32[]{:S(2)}) collective-permute-start(bf16[256,2560]{1,0:T(8,128)(2,1)} %get-tuple-element.29), channel_id=1, source_target_pairs={{0,12},{1,49},{2,14},{3,51},{4,8},{5,53},{6,10},{7,55},{8,4},{9,57... | collective-permute-start | bytes 3932168 | tf_op jit(solution)/shard_map/ppermute | solution.py:41
  95.9 18.5 %collective-permute-start.18 = (bf16[256,2560]{1,0:T(8,128)(2,1)}, bf16[256,2560]{1,0:T(8,128)(2,1)S(1)}, u32[]{:S(2)}, u32[]{:S(2)}) collective-permute-start(bf16[256,2560]{1,0:T(8,128)(2,1)} %get-tuple-element.31), channel_id=1, source_target_pairs={{0,4},{1,17},{2,6},{3,19},{4,0},{5,21},{6,2},{7,23},{8,12},{9,25},... | collective-permute-start | bytes 3932168 | tf_op jit(solution)/shard_map/ppermute | solution.py:41
  111.1 9.3 %collective-permute-start.21 = (bf16[128,2048]{1,0:T(8,128)(2,1)S(1)}, bf16[128,2048]{1,0:T(8,128)(2,1)S(1)}, u32[]{:S(2)}, u32[]{:S(2)}) collective-permute-start(bf16[128,2048]{1,0:T(8,128)(2,1)S(1)} %slice.206), channel_id=1, source_target_pairs={{0,2},{1,67},{2,0},{3,65},{4,6},{5,71},{6,4},{7,69},{8,10},{9,75},... | collective-permute-start | bytes 1572872 | tf_op jit(solution)/shard_map/ppermute | solution.py:41
  113.5 13.8 %collective-permute-start.17 = (bf16[128,2560]{1,0:T(8,128)(2,1)S(1)}, bf16[128,2560]{1,0:T(8,128)(2,1)S(1)}, u32[]{:S(2)}, u32[]{:S(2)}) collective-permute-start(bf16[128,2560]{1,0:T(8,128)(2,1)S(1)} %slice.205), channel_id=1, source_target_pairs={{0,4},{1,17},{2,6},{3,19},{4,0},{5,21},{6,2},{7,23},{8,12},{9,25},... | collective-permute-start | bytes 1966088 | tf_op jit(solution)/shard_map/ppermute | solution.py:41
  114.9 21.3 %collective-permute-start.19 = (bf16[128,2560]{1,0:T(8,128)(2,1)S(1)}, bf16[128,2560]{1,0:T(8,128)(2,1)S(1)}, u32[]{:S(2)}, u32[]{:S(2)}) collective-permute-start(bf16[128,2560]{1,0:T(8,128)(2,1)S(1)} %slice.204), channel_id=1, source_target_pairs={{0,12},{1,49},{2,14},{3,51},{4,8},{5,53},{6,10},{7,55},{8,4},{9,57... | collective-permute-start | bytes 1966088 | tf_op jit(solution)/shard_map/ppermute | solution.py:41
  136.5 8.9 %collective-permute-start.22 = (bf16[4,8,7168]{2,1,0:T(8,128)(2,1)S(1)}, bf16[4,8,7168]{2,1,0:T(8,128)(2,1)S(1)}, u32[]{:S(2)}, u32[]{:S(2)}) collective-permute-start(bf16[4,8,7168]{2,1,0:T(8,128)(2,1)S(1)} %get-tuple-element.40), channel_id=1, source_target_pairs={{0,16},{1,5},{2,18},{3,7},{4,20},{5,1},{6,22},{7,3},{8,24},{9,13},... | collective-permute-start | bytes 1376264 | tf_op jit(solution)/shard_map/ppermute | solution.py:41
  136.6 15.4 %collective-permute-start.23 = (bf16[4,8,7168]{2,1,0:T(8,128)(2,1)S(1)}, bf16[4,8,7168]{2,1,0:T(8,128)(2,1)S(1)}, u32[]{:S(2)}, u32[]{:S(2)}) collective-permute-start(bf16[4,8,7168]{2,1,0:T(8,128)(2,1)S(1)} %get-tuple-element.42), channel_id=1, source_target_pairs={{0,48},{1,13},{2,50},{3,15},{4,52},{5,9},{6,54},{7,11},{8,56},{9,5... | collective-permute-start | bytes 1376264 | tf_op jit(solution)/shard_map/ppermute | solution.py:41
  141.1 11.7 %collective-permute-start.24 = (bf16[4,8,7168]{2,1,0:T(8,128)(2,1)S(1)}, bf16[4,8,7168]{2,1,0:T(8,128)(2,1)S(1)}, u32[]{:S(2)}, u32[]{:S(2)}) collective-permute-start(bf16[4,8,7168]{2,1,0:T(8,128)(2,1)S(1)} %get-tuple-element.41), channel_id=1, source_target_pairs={{0,32},{1,9},{2,34},{3,11},{4,36},{5,13},{6,38},{7,15},{8,40},{9,1... | collective-permute-start | bytes 1376264 | tf_op jit(solution)/shard_map/ppermute | solution.py:41
  153.1 8.3 %collective-permute-start.28 = (bf16[8,2048]{1,0:T(8,128)(2,1)S(1)}, bf16[8,2048]{1,0:T(8,128)(2,1)S(1)}, u32[]{:S(2)}, u32[]{:S(2)}) collective-permute-start(bf16[8,2048]{1,0:T(8,128)(2,1)S(1)} %get-tuple-element.46), channel_id=1, source_target_pairs={{0,4},{1,17},{2,6},{3,19},{4,0},{5,21},{6,2},{7,23},{8,12},{9,25},... | collective-permute-start | bytes 98312 | tf_op jit(solution)/shard_map/ppermute | solution.py:41
  153.2 8.3 %collective-permute-start.29 = (bf16[8,2048]{1,0:T(8,128)(2,1)S(1)}, bf16[8,2048]{1,0:T(8,128)(2,1)S(1)}, u32[]{:S(2)}, u32[]{:S(2)}) collective-permute-start(bf16[8,2048]{1,0:T(8,128)(2,1)S(1)} %get-tuple-element.48), channel_id=1, source_target_pairs={{0,12},{1,49},{2,14},{3,51},{4,8},{5,53},{6,10},{7,55},{8,4},{9,57... | collective-permute-start | bytes 98312 | tf_op jit(solution)/shard_map/ppermute | solution.py:41
  153.8 7.6 %collective-permute-start.30 = (bf16[8,2048]{1,0:T(8,128)(2,1)S(1)}, bf16[8,2048]{1,0:T(8,128)(2,1)S(1)}, u32[]{:S(2)}, u32[]{:S(2)}) collective-permute-start(bf16[8,2048]{1,0:T(8,128)(2,1)S(1)} %get-tuple-element.47), channel_id=1, source_target_pairs={{0,8},{1,33},{2,10},{3,35},{4,12},{5,37},{6,14},{7,39},{8,0},{9,41... | collective-permute-start | bytes 98312 | tf_op jit(solution)/shard_map/ppermute | solution.py:41
  157.3 4.5 %collective-permute-start.25 = (bf16[8,5120]{1,0:T(8,128)(2,1)S(1)}, bf16[8,5120]{1,0:T(8,128)(2,1)S(1)}, u32[]{:S(2)}, u32[]{:S(2)}) collective-permute-start(bf16[8,5120]{1,0:T(8,128)(2,1)S(1)} %get-tuple-element.43), channel_id=1, source_target_pairs={{0,2},{1,67},{2,0},{3,65},{4,6},{5,71},{6,4},{7,69},{8,10},{9,75},... | collective-permute-start | bytes 245768 | tf_op jit(solution)/shard_map/ppermute | solution.py:41
  158.8 5.7 %collective-permute-start.26 = (bf16[8,5120]{1,0:T(8,128)(2,1)S(1)}, bf16[8,5120]{1,0:T(8,128)(2,1)S(1)}, u32[]{:S(2)}, u32[]{:S(2)}) collective-permute-start(bf16[8,5120]{1,0:T(8,128)(2,1)S(1)} %get-tuple-element.45), channel_id=1, source_target_pairs={{0,66},{1,3},{2,64},{3,1},{4,70},{5,7},{6,68},{7,5},{8,74},{9,11},... | collective-permute-start | bytes 245768 | tf_op jit(solution)/shard_map/ppermute | solution.py:41
  161.4 5.9 %collective-permute-start.27 = (bf16[8,5120]{1,0:T(8,128)(2,1)S(1)}, bf16[8,5120]{1,0:T(8,128)(2,1)S(1)}, u32[]{:S(2)}, u32[]{:S(2)}) collective-permute-start(bf16[8,5120]{1,0:T(8,128)(2,1)S(1)} %get-tuple-element.44), channel_id=1, source_target_pairs={{0,64},{1,65},{2,66},{3,67},{4,68},{5,69},{6,70},{7,71},{8,72},{9,... | collective-permute-start | bytes 245768 | tf_op jit(solution)/shard_map/ppermute | solution.py:41
  (13 other events, 141.2 us)

commit v4 on v3

--- a/solution.py
+++ b/solution.py
@@ -68,6 +68,11 @@
     total = keep.astype(f) + flip(send, axis, order[1]).astype(f)
     half = keep.shape[0] // 2
     return total[:half] + flip(total[half:].astype(keep.dtype), axis, order[0]).astype(f)
+
+
+def together(values):
+    mark = swap_cores(values[:8, :LANES])
+    return values + mark[0, 0] * 0
 
 
 def normalize(values):
@@ -143,84 +148,53 @@
 HIDDEN = 256
 
 
-def copy_in(pairs, sems):
-    copies = [pltpu.make_async_copy(src, dst, sems.at[i]) for i, (src, dst) in enumerate(pairs)]
-    for copy in copies:
-        copy.start()
-    return copies
-
-
 def spans(widths):
     starts = [sum(widths[:i]) for i in range(len(widths))]
     return list(zip(starts, widths))
 
 
-def slab_pairs(slabs, held, widths):
-    return [
-        (slab.at[0, pl.ds(start, width)], held.at[i, pl.ds(start, width)])
-        for start, width in spans(widths)
-        for i, slab in enumerate(slabs)
-    ]
-
-
-def multiply(copies, held, rows, widths, store):
+def multiply(slabs, rows, widths, outs):
     for part, (start, width) in enumerate(spans(widths)):
-        for i in range(4):
-            copies[part * 4 + i].wait()
-            store(
-                part,
-                i,
-                jnp.dot(
-                    rows[part][:, :width],
-                    held[i, pl.ds(start, width)],
-                    preferred_element_type=jnp.float32,
-                ),
+        for i, slab in enumerate(slabs):
+            outs[part][:, pl.ds(i * HIDDEN, HIDDEN)] = jnp.dot(
+                rows[part][:, :width],
+                slab[0, pl.ds(start, width)],
+                preferred_element_type=jnp.float32,
             )
 
 
-def early_kernel(widths, x1, x2, x3, s1, s2, s3, s4, h1, h2, h3, held, sems):
-    copies = copy_in(slab_pairs((s1, s2, s3, s4), held, widths), sems)
-    outs = (h1, h2, h3)
-
-    def store(part, i, product):
-        outs[part][:, pl.ds(i * HIDDEN, HIDDEN)] = product
-
-    multiply(copies, held, (x1, x2, x3), widths, store)
+def call(kernel, args, out_shape, scratch_shapes=(), limit=16):
+    vmem = pl.BlockSpec(memory_space=pltpu.VMEM)
+    return pl.pallas_call(
+        kernel,
+        in_specs=[vmem] * len(args),
+        out_specs=[vmem] * len(out_shape),
+        out_shape=out_shape,
+        scratch_shapes=scratch_shapes,
+        compiler_params=pltpu.CompilerParams(vmem_limit_bytes=limit << 20),
+    )(*args)
+
+
+def early_kernel(widths, x1, x2, x3, s1, s2, s3, s4, h1, h2, h3):
+    multiply((s1, s2, s3, s4), (x1, x2, x3), widths, (h1, h2, h3))
 
 
 def early(rows, slabs, widths):
     count = rows[0].shape[0]
-    vmem, any_ = pl.BlockSpec(memory_space=pltpu.VMEM), pl.BlockSpec(memory_space=pl.ANY)
-    return pl.pallas_call(
-        functools.partial(early_kernel, widths),
-        in_specs=[vmem] * 3 + [any_] * 4,
-        out_specs=[vmem] * 3,
-        out_shape=[jax.ShapeDtypeStruct((count, 4 * HIDDEN), jnp.float32)] * 3,
-        scratch_shapes=[
-            pltpu.VMEM((4, sum(widths), HIDDEN), jnp.bfloat16),
-            pltpu.SemaphoreType.DMA((12,)),
-        ],
-        compiler_params=pltpu.CompilerParams(vmem_limit_bytes=34 << 20),
-    )(*rows, *slabs)
-
-
-def late_kernel(widths, x1, x2, x3, h1, h2, h3, before, picks, s1, s2, s3, s4, own, other, o1, o2, o3, straight, turned, g1, g2, g3, held, low, out1, out2, out3, sems, low_sems, out_sems):
+    out_shape = [jax.ShapeDtypeStruct((count, 4 * HIDDEN), jnp.float32)] * 3
+    return call(functools.partial(early_kernel, widths), (*rows, *slabs), out_shape)
+
+
+def lower(rows, own, other, start, width):
+    cols = pl.ds(start, width)
+    product = jnp.dot(rows[:, :HIDDEN], own[0, :, cols], preferred_element_type=jnp.float32)
+    product += jnp.dot(rows[:, HIDDEN:], other[0, :, cols], preferred_element_type=jnp.float32)
+    return product.astype(jnp.bfloat16)
+
+
+def late_kernel(widths, x1, x2, x3, h1, h2, h3, before, picks, s1, s2, s3, s4, own, other, o1, o2, o3, straight, turned, g1, g2, g3):
     f32, bf = jnp.float32, jnp.bfloat16
-    copies = copy_in(slab_pairs((s1, s2, s3, s4), held, widths), sems)
-    low_copies = copy_in(
-        [
-            (slab.at[0, :, pl.ds(start, width)], low.at[pl.ds(i * HIDDEN, HIDDEN), pl.ds(start, width)])
-            for start, width in spans(widths)
-            for i, slab in enumerate((own, other))
-        ],
-        low_sems,
-    )
-    fresh = (g1, g2, g3)
-
-    def store(part, i, product):
-        fresh[part][:, pl.ds(i * HIDDEN, HIDDEN)] = product
-
-    multiply(copies, held, (x1, x2, x3), widths, store)
+    multiply((s1, s2, s3, s4), (x1, x2, x3), widths, (g1, g2, g3))
     half = x1.shape[0]
     count, block = 2 * half, half // 2
 
@@ -251,53 +225,23 @@
         jnp.concatenate([straight[block:half, :], straight[half + block :, :]], axis=0),
         turned[half:, :],
     )
-    out_copies = []
     for part, (start, width) in enumerate(spans(widths)):
-        low_copies[2 * part].wait()
-        low_copies[2 * part + 1].wait()
-        buffer, out = (out1, out2, out3)[part], (o1, o2, o3)[part]
-        buffer[...] = jnp.dot(leaving[part], low[:, pl.ds(start, width)], preferred_element_type=f32).astype(bf)
-        copy = pltpu.make_async_copy(buffer, out, out_sems.at[part])
-        copy.start()
-        out_copies.append(copy)
-    for copy in out_copies:
-        copy.wait()
+        (o1, o2, o3)[part][...] = lower(leaving[part], own, other, start, width)
 
 
 def late(rows, partial, before, picks, slabs, lows, widths):
     bf, f32 = jnp.bfloat16, jnp.float32
     count = rows[0].shape[0]
-    vmem, any_ = pl.BlockSpec(memory_space=pltpu.VMEM), pl.BlockSpec(memory_space=pl.ANY)
-    return pl.pallas_call(
+    return call(
         functools.partial(late_kernel, widths),
-        in_specs=[vmem] * 8 + [any_] * 6,
-        out_specs=[any_] * 3 + [vmem] * 2,
-        out_shape=[jax.ShapeDtypeStruct((count, width), bf) for width in widths]
+        (*rows, *partial, before, picks, *slabs, *lows),
+        [jax.ShapeDtypeStruct((count, width), bf) for width in widths]
         + [jax.ShapeDtypeStruct((2 * count, 2 * HIDDEN), bf)] * 2,
-        scratch_shapes=[pltpu.VMEM((count, 4 * HIDDEN), f32)] * 3
-        + [
-            pltpu.VMEM((4, sum(widths), HIDDEN), bf),
-            pltpu.VMEM((2 * HIDDEN, sum(widths)), bf),
-        ]
-        + [pltpu.VMEM((count, width), bf) for width in widths]
-        + [
-            pltpu.SemaphoreType.DMA((12,)),
-            pltpu.SemaphoreType.DMA((6,)),
-            pltpu.SemaphoreType.DMA((3,)),
-        ],
-        compiler_params=pltpu.CompilerParams(vmem_limit_bytes=52 << 20),
-    )(*rows, *partial, before, picks, *slabs, *lows)
-
-
-def stay_kernel(widths, straight, turned, own, other, o1, o2, o3, low, sems):
-    copies = copy_in(
-        [
-            (slab.at[0, :, pl.ds(start, width)], low.at[pl.ds(i * HIDDEN, HIDDEN), pl.ds(start, width)])
-            for start, width in spans(widths)
-            for i, slab in enumerate((own, other))
-        ],
-        sems,
-    )
+        [pltpu.VMEM((count, 4 * HIDDEN), f32)] * 3,
+    )
+
+
+def stay_kernel(widths, straight, turned, own, other, o1, o2, o3):
     half = straight.shape[0] // 2
     block = half // 2
     staying = (
@@ -306,33 +250,20 @@
         turned[:half, :],
     )
     for part, (start, width) in enumerate(spans(widths)):
-        copies[2 * part].wait()
-        copies[2 * part + 1].wait()
-        product = jnp.dot(staying[part], low[:, pl.ds(start, width)], preferred_element_type=jnp.float32)
-        (o1, o2, o3)[part][...] = product.astype(jnp.bfloat16)
+        (o1, o2, o3)[part][...] = lower(staying[part], own, other, start, width)
 
 
 def stay(straight, turned, lows, widths):
-    vmem, any_ = pl.BlockSpec(memory_space=pltpu.VMEM), pl.BlockSpec(memory_space=pl.ANY)
     count = straight.shape[0] // 2
-    return pl.pallas_call(
-        functools.partial(stay_kernel, widths),
-        in_specs=[vmem] * 2 + [any_] * 2,
-        out_specs=[vmem] * 3,
-        out_shape=[jax.ShapeDtypeStruct((count, width), jnp.bfloat16) for width in widths],
-        scratch_shapes=[
-            pltpu.VMEM((2 * HIDDEN, sum(widths)), jnp.bfloat16),
-            pltpu.SemaphoreType.DMA((6,)),
-        ],
-        compiler_params=pltpu.CompilerParams(vmem_limit_bytes=20 << 20),
-    )(straight, turned, *lows)
+    out_shape = [jax.ShapeDtypeStruct((count, width), jnp.bfloat16) for width in widths]
+    return call(functools.partial(stay_kernel, widths), (straight, turned, *lows), out_shape)
 
 
 def body(hidden, router, routes, w_gate, w_up, w_down, w_latent, lengths, latent_cache, queries):
     bf, f32 = jnp.bfloat16, jnp.float32
     rows, width = hidden.shape
     experts = router.shape[1]
-    third = 2560
+    third = 19 * LANES
     cut = 2 * third
     widths = (third, third, width - cut)
     mine = lax.rem(lax.axis_index("dev"), experts)
@@ -367,7 +298,7 @@
     y1 = reduce_pairs(staying[0], leaving[0], "a", SAME).astype(bf)
     y2 = reduce_pairs(staying[1], leaving[1], "a", TURNED).astype(bf)
     y3 = reduce_pairs(staying[2], leaving[2], "y", SPLIT).astype(bf)
-    both = jnp.concatenate([y1, y2, y3], axis=1).reshape(4, 4, rows, width)
+    both = together(jnp.concatenate([y1, y2, y3], axis=1)).reshape(4, 4, rows, width)
     both = reduce([both[i] for i in range(4)], "b", SAME).astype(bf)
     first, second = both[..., :cut], both[..., cut:]
     first = reduce([first[i] for i in range(4)], "y", SPLIT)

time: 173 us -> 153 us (0.88)
  waiting for transfers between devices: 74.1 us -> 59.1 us
  Pallas kernels: 32.9 us -> 24.1 us
  starting transfers between devices: 39.4 us -> 46.5 us
  local copies, waits for them, and re-layouts: 8.44 us -> 5.22 us
    ppermute x28, waiting for transfers between devices: 74.1 us -> 59 us  [flip(): return lax.ppermute(values, AXES, partners(AXIS[axis], flips))]
    pallas_call x3, Pallas kernels: 32.9 us -> 24.1 us  [call(): pl.pallas_call(kernel, in_specs=[vmem] * len(args), out_specs=[vmem] * le...]
    ppermute x28, starting transfers between devices: 37.6 us -> 44.6 us  [flip(): return lax.ppermute(values, AXES, partners(AXIS[axis], flips))]
    unnamed x28, local copies, waits for them, and re-layouts: 7.86 us -> 4.13 us
  transfers between devices with their start and end apart: 31 -> 32, of which waited for: 18 -> 19; matrix products, arithmetic and copies ran while one was open for 7% -> 7% of each run, Pallas kernels for 9% -> 8%
where the time goes in v4:
time: 153 us
  waiting for transfers between devices  59.1 us (39%)
  starting transfers between devices  46.5 us (30%)
  Pallas kernels  24.1 us (16%)
  other arithmetic  8.8 us (6%)
  matrix products  7.22 us (5%)
  local copies, waits for them, and re-layouts  5.22 us (3%)
  between operations  2.01 us (1%)
    ppermute x28, waiting for transfers between devices, flip(): return lax.ppermute(values, AXES, partners(AXIS[axis], flips))  59 us
    ppermute x28, starting transfers between devices, flip(): return lax.ppermute(values, AXES, partners(AXIS[axis], flips))  44.6 us
    pallas_call x3, Pallas kernels, call(): pl.pallas_call(kernel, in_specs=[vmem] * len(args), out_specs=[vmem] * le...  24.1 us
    unnamed x28, local copies, waits for them, and re-layouts  4.13 us
  transfers between devices with their start and end apart: 32, of which 19 were waited for; matrix products, arithmetic and copies ran while one was open for 7% of the time, Pallas kernels for 8%

profile of v4, /device:TPU:0, one launch (start us, length us, event | category | flops | bytes accessed | tf_op | source)
XLA Modules:
  0.0 152.9 jit_solution(5321524624845627304)
XLA Ops:
  12.7 2.8 %collective-permute-start.3 = (bf16[2,8,2432]{2,1,0:T(8,128)(2,1)S(1)}, bf16[2,8,2432]{2,1,0:T(8,128)(2,1)S(1)}, u32[]{:S(2)}, u32[]{:S(2)}) collective-permute-start(bf16[2,8,2432]{2,1,0:T(8,128)(2,1)S(1)} %pad_maximum_fusion.5), channel_id=1, source_target_pairs={{0,12},{1,49},{2,14},{3,51},{4,8},{5,53},{6,10},{7,55},{8,4},{9,57... | collective-permute-start | bytes 233480 | tf_op jit(solution)/shard_map/ppermute | solution.py:41
  15.5 2.8 %collective-permute-done.3 = bf16[2,8,2432]{2,1,0:T(8,128)(2,1)S(1)} collective-permute-done((bf16[2,8,2432]{2,1,0:T(8,128)(2,1)S(1)}, bf16[2,8,2432]{2,1,0:T(8,128)(2,1)S(1)}, u32[]{:S(2)}, u32[]{:S(2)}) %collective-permute-start.3) | collective-permute-done | bytes 77856 | tf_op jit(solution)/shard_map/ppermute | solution.py:41
  18.4 2.0 %collective-permute-start.6 = (bf16[4,8,7296]{2,1,0:T(8,128)(2,1)S(1)}, bf16[4,8,7296]{2,1,0:T(8,128)(2,1)S(1)}, u32[]{:S(2)}, u32[]{:S(2)}) collective-permute-start(bf16[4,8,7296]{2,1,0:T(8,128)(2,1)S(1)} %maximum_maximum_fusion), channel_id=1, source_target_pairs={{0,16},{1,5},{2,18},{3,7},{4,20},{5,1},{6,22},{7,3},{8,24},{9,13},... | collective-permute-start | bytes 1400840 | tf_op jit(solution)/shard_map/ppermute | solution.py:41
  20.4 2.5 %collective-permute-start.7 = (bf16[4,8,7296]{2,1,0:T(8,128)(2,1)S(1)}, bf16[4,8,7296]{2,1,0:T(8,128)(2,1)S(1)}, u32[]{:S(2)}, u32[]{:S(2)}) collective-permute-start(bf16[4,8,7296]{2,1,0:T(8,128)(2,1)S(1)} %maximum_maximum_fusion), channel_id=1, source_target_pairs={{0,48},{1,13},{2,50},{3,15},{4,52},{5,9},{6,54},{7,11},{8,56},{9,5... | collective-permute-start | bytes 1400840 | tf_op jit(solution)/shard_map/ppermute | solution.py:41
  24.0 3.1 %collective-permute-done.6 = bf16[4,8,7296]{2,1,0:T(8,128)(2,1)S(1)} collective-permute-done((bf16[4,8,7296]{2,1,0:T(8,128)(2,1)S(1)}, bf16[4,8,7296]{2,1,0:T(8,128)(2,1)S(1)}, u32[]{:S(2)}, u32[]{:S(2)}) %collective-permute-start.6) | collective-permute-done | bytes 466976 | tf_op jit(solution)/shard_map/ppermute | solution.py:41
  27.1 7.0 %collective-permute-done.7 = bf16[4,8,7296]{2,1,0:T(8,128)(2,1)S(1)} collective-permute-done((bf16[4,8,7296]{2,1,0:T(8,128)(2,1)S(1)}, bf16[4,8,7296]{2,1,0:T(8,128)(2,1)S(1)}, u32[]{:S(2)}, u32[]{:S(2)}) %collective-permute-start.7) | collective-permute-done | bytes 466976 | tf_op jit(solution)/shard_map/ppermute | solution.py:41
  36.2 2.8 %collective-permute-start.12 = (bf16[128,2432]{1,0:T(8,128)(2,1)S(1)}, bf16[128,2432]{1,0:T(8,128)(2,1)S(1)}, u32[]{:S(2)}, u32[]{:S(2)}) collective-permute-start(bf16[128,2432]{1,0:T(8,128)(2,1)S(1)} %bitcast.61), channel_id=1, source_target_pairs={{0,12},{1,49},{2,14},{3,51},{4,8},{5,53},{6,10},{7,55},{8,4},{9,57... | collective-permute-start | bytes 1867784 | tf_op jit(solution)/shard_map/ppermute | solution.py:41
  39.0 7.3 %collective-permute-done.14 = bf16[128,2432]{1,0:T(8,128)(2,1)S(1)} collective-permute-done((bf16[128,2432]{1,0:T(8,128)(2,1)S(1)}, bf16[128,2432]{1,0:T(8,128)(2,1)S(1)}, u32[]{:S(2)}, u32[]{:S(2)}) %collective-permute-start.14) | collective-permute-done | bytes 622624 | tf_op jit(solution)/shard_map/ppermute | solution.py:41
  50.3 2.4 %collective-permute-start.11 = (bf16[256,2432]{1,0:T(8,128)(2,1)}, bf16[256,2432]{1,0:T(8,128)(2,1)}, u32[]{:S(2)}, u32[]{:S(2)}) collective-permute-start(bf16[256,2432]{1,0:T(8,128)(2,1)} %pad_maximum_fusion.2.x1), channel_id=1, source_target_pairs={{0,12},{1,49},{2,14},{3,51},{4,8},{5,53},{6,10},{7,55},{8,4},{9,57... | collective-permute-start | bytes 3735560 | tf_op jit(solution)/shard_map/ppermute | solution.py:41
  52.8 2.0 %copy-done.2 = bf16[1,7168,256]{2,1,0:T(8,128)(2,1)S(1)} copy-done((bf16[1,7168,256]{2,1,0:T(8,128)(2,1)S(1)}, bf16[1,7168,256]{2,1,0:T(8,128)(2,1)}, u32[]{:S(2)}) %copy-start.2) | copy-done | bytes 3670040
  54.8 2.0 %copy-done.4 = bf16[1,7168,256]{2,1,0:T(8,128)(2,1)S(1)} copy-done((bf16[1,7168,256]{2,1,0:T(8,128)(2,1)S(1)}, bf16[1,7168,256]{2,1,0:T(8,128)(2,1)}, u32[]{:S(2)}) %copy-start.4) | copy-done | bytes 3670040
  56.8 8.1 %shard_map.113 = (f32[256,1024]{1,0:T(8,128)S(1)}, f32[256,1024]{1,0:T(8,128)S(1)}, f32[256,1024]{1,0:T(8,128)S(1)}) custom-call(bf16[256,2432]{1,0:T(8,128)(2,1)} %pad_maximum_fusion.2.x1, bf16[256,2432]{1,0:T(8,128)(2,1)} %pad_maximum_fusion.3.x2, bf16[256,2432]{1,0:T(8,128)(2,1)S(1)} %pad_maximum_fusion.1.x3, bf16[1,7168,256]{2,1,0:T(8,128)(2,1)S(1)} %copy-done.2, ...), custom_call_target="tpu_custom_call" | custom-call | tf_op jit(solution)/shard_map/pallas_call | solution.py:168
  66.0 2.7 %collective-permute-done.11.x1 = bf16[256,2432]{1,0:T(8,128)(2,1)} collective-permute-done((bf16[256,2432]{1,0:T(8,128)(2,1)}, bf16[256,2432]{1,0:T(8,128)(2,1)}, u32[]{:S(2)}, u32[]{:S(2)}) %collective-permute-start.11) | collective-permute-done | bytes 1245216 | tf_op jit(solution)/shard_map/ppermute | solution.py:41
  68.8 11.7 %shard_map.114 = (bf16[256,2432]{1,0:T(8,128)(2,1)S(1)}, bf16[256,2432]{1,0:T(8,128)(2,1)S(1)}, bf16[256,2304]{1,0:T(8,128)(2,1)S(1)}, bf16[512,512]{1,0:T(8,128)(2,1)S(1)}, bf16[512,512]{1,0:T(8,128)(2,1)S(1)}) custom-call(bf16[256,2432]{1,0:T(8,128)(2,1)} %collective-permute-done.11.x1, bf16[256,2432]{1,0:T(8,128)(2,1)} %collective-permute-done.13.x2, ...), custom_call_target="tpu_custom_call" | custom-call | tf_op jit(solution)/shard_map/pallas_call | solution.py:168
  80.5 2.6 %collective-permute-start.20 = (bf16[256,2304]{1,0:T(8,128)(2,1)S(1)}, bf16[256,2304]{1,0:T(8,128)(2,1)S(1)}, u32[]{:S(2)}, u32[]{:S(2)}) collective-permute-start(bf16[256,2304]{1,0:T(8,128)(2,1)S(1)} %get-tuple-element.33), channel_id=1, source_target_pairs={{0,66},{1,3},{2,64},{3,1},{4,70},{5,7},{6,68},{7,5},{8,74},{9,11},... | collective-permute-start | bytes 3538952 | tf_op jit(solution)/shard_map/ppermute | solution.py:41
  83.1 2.6 %collective-permute-start.16 = (bf16[256,2432]{1,0:T(8,128)(2,1)S(1)}, bf16[256,2432]{1,0:T(8,128)(2,1)S(1)}, u32[]{:S(2)}, u32[]{:S(2)}) collective-permute-start(bf16[256,2432]{1,0:T(8,128)(2,1)S(1)} %get-tuple-element.29), channel_id=1, source_target_pairs={{0,12},{1,49},{2,14},{3,51},{4,8},{5,53},{6,10},{7,55},{8,4},{9,57... | collective-permute-start | bytes 3735560 | tf_op jit(solution)/shard_map/ppermute | solution.py:41
  86.0 4.3 %shard_map.115 = (bf16[256,2432]{1,0:T(8,128)(2,1)S(1)}, bf16[256,2432]{1,0:T(8,128)(2,1)S(1)}, bf16[256,2304]{1,0:T(8,128)(2,1)S(1)}) custom-call(bf16[512,512]{1,0:T(8,128)(2,1)S(1)} %get-tuple-element.26.straight, bf16[512,512]{1,0:T(8,128)(2,1)S(1)} %get-tuple-element.27.turned, bf16[1,256,7168]{2,1,0:T(8,128)(2,1)S(1)} %copy-done.1, ...), custom_call_target="tpu_custom_call" | custom-call | tf_op jit(solution)/shard_map/pallas_call | solution.py:168
  90.2 9.4 %collective-permute-done.20 = bf16[256,2304]{1,0:T(8,128)(2,1)S(1)} collective-permute-done((bf16[256,2304]{1,0:T(8,128)(2,1)S(1)}, bf16[256,2304]{1,0:T(8,128)(2,1)S(1)}, u32[]{:S(2)}, u32[]{:S(2)}) %collective-permute-start.20) | collective-permute-done | bytes 1179680 | tf_op jit(solution)/shard_map/ppermute | solution.py:41
  100.0 2.0 %collective-permute-start.21 = (bf16[128,2304]{1,0:T(8,128)(2,1)S(1)}, bf16[128,2304]{1,0:T(8,128)(2,1)S(1)}, u32[]{:S(2)}, u32[]{:S(2)}) collective-permute-start(bf16[128,2304]{1,0:T(8,128)(2,1)S(1)} %slice.215), channel_id=1, source_target_pairs={{0,2},{1,67},{2,0},{3,65},{4,6},{5,71},{6,4},{7,69},{8,10},{9,75},... | collective-permute-start | bytes 1769480 | tf_op jit(solution)/shard_map/ppermute | solution.py:41
  104.6 3.2 %collective-permute-start.19 = (bf16[128,2432]{1,0:T(8,128)(2,1)S(1)}, bf16[128,2432]{1,0:T(8,128)(2,1)S(1)}, u32[]{:S(2)}, u32[]{:S(2)}) collective-permute-start(bf16[128,2432]{1,0:T(8,128)(2,1)S(1)} %slice.213), channel_id=1, source_target_pairs={{0,12},{1,49},{2,14},{3,51},{4,8},{5,53},{6,10},{7,55},{8,4},{9,57... | collective-permute-start | bytes 1867784 | tf_op jit(solution)/shard_map/ppermute | solution.py:41
  107.8 2.1 %collective-permute-done.21 = bf16[128,2304]{1,0:T(8,128)(2,1)S(1)} collective-permute-done((bf16[128,2304]{1,0:T(8,128)(2,1)S(1)}, bf16[128,2304]{1,0:T(8,128)(2,1)S(1)}, u32[]{:S(2)}, u32[]{:S(2)}) %collective-permute-start.21) | collective-permute-done | bytes 589856 | tf_op jit(solution)/shard_map/ppermute | solution.py:41
  110.0 2.9 %collective-permute-done.17 = bf16[128,2432]{1,0:T(8,128)(2,1)S(1)} collective-permute-done((bf16[128,2432]{1,0:T(8,128)(2,1)S(1)}, bf16[128,2432]{1,0:T(8,128)(2,1)S(1)}, u32[]{:S(2)}, u32[]{:S(2)}) %collective-permute-start.17) | collective-permute-done | bytes 622624 | tf_op jit(solution)/shard_map/ppermute | solution.py:41
  113.1 3.0 %collective-permute-done.19 = bf16[128,2432]{1,0:T(8,128)(2,1)S(1)} collective-permute-done((bf16[128,2432]{1,0:T(8,128)(2,1)S(1)}, bf16[128,2432]{1,0:T(8,128)(2,1)S(1)}, u32[]{:S(2)}, u32[]{:S(2)}) %collective-permute-start.19) | collective-permute-done | bytes 622624 | tf_op jit(solution)/shard_map/ppermute | solution.py:41
  118.3 3.4 %collective-permute-start.24 = (bf16[4,8,7168]{2,1,0:T(8,128)(2,1)S(1)}, bf16[4,8,7168]{2,1,0:T(8,128)(2,1)S(1)}, u32[]{:S(2)}, u32[]{:S(2)}) collective-permute-start(bf16[4,8,7168]{2,1,0:T(8,128)(2,1)S(1)} %get-tuple-element.43), channel_id=1, source_target_pairs={{0,48},{1,13},{2,50},{3,15},{4,52},{5,9},{6,54},{7,11},{8,56},{9,5... | collective-permute-start | bytes 1376264 | tf_op jit(solution)/shard_map/ppermute | solution.py:41
  124.1 2.6 %collective-permute-done.23 = bf16[4,8,7168]{2,1,0:T(8,128)(2,1)S(1)} collective-permute-done((bf16[4,8,7168]{2,1,0:T(8,128)(2,1)S(1)}, bf16[4,8,7168]{2,1,0:T(8,128)(2,1)S(1)}, u32[]{:S(2)}, u32[]{:S(2)}) %collective-permute-start.23) | collective-permute-done | bytes 458784 | tf_op jit(solution)/shard_map/ppermute | solution.py:41
  126.8 6.3 %collective-permute-done.24 = bf16[4,8,7168]{2,1,0:T(8,128)(2,1)S(1)} collective-permute-done((bf16[4,8,7168]{2,1,0:T(8,128)(2,1)S(1)}, bf16[4,8,7168]{2,1,0:T(8,128)(2,1)S(1)}, u32[]{:S(2)}, u32[]{:S(2)}) %collective-permute-start.24) | collective-permute-done | bytes 458784 | tf_op jit(solution)/shard_map/ppermute | solution.py:41
  133.4 3.3 %collective-permute-start.30 = (bf16[8,2304]{1,0:T(8,128)(2,1)S(1)}, bf16[8,2304]{1,0:T(8,128)(2,1)S(1)}, u32[]{:S(2)}, u32[]{:S(2)}) collective-permute-start(bf16[8,2304]{1,0:T(8,128)(2,1)S(1)} %get-tuple-element.49), channel_id=1, source_target_pairs={{0,12},{1,49},{2,14},{3,51},{4,8},{5,53},{6,10},{7,55},{8,4},{9,57... | collective-permute-start | bytes 110600 | tf_op jit(solution)/shard_map/ppermute | solution.py:41
  138.5 3.1 %collective-permute-start.27 = (bf16[8,4864]{1,0:T(8,128)(2,1)S(1)}, bf16[8,4864]{1,0:T(8,128)(2,1)S(1)}, u32[]{:S(2)}, u32[]{:S(2)}) collective-permute-start(bf16[8,4864]{1,0:T(8,128)(2,1)S(1)} %get-tuple-element.46), channel_id=1, source_target_pairs={{0,66},{1,3},{2,64},{3,1},{4,70},{5,7},{6,68},{7,5},{8,74},{9,11},... | collective-permute-start | bytes 233480 | tf_op jit(solution)/shard_map/ppermute | solution.py:41
  142.6 1.8 %collective-permute-done.27 = bf16[8,4864]{1,0:T(8,128)(2,1)S(1)} collective-permute-done((bf16[8,4864]{1,0:T(8,128)(2,1)S(1)}, bf16[8,4864]{1,0:T(8,128)(2,1)S(1)}, u32[]{:S(2)}, u32[]{:S(2)}) %collective-permute-start.27) | collective-permute-done | bytes 77856 | tf_op jit(solution)/shard_map/ppermute | solution.py:41
  144.4 3.1 %collective-permute-done.28 = bf16[8,4864]{1,0:T(8,128)(2,1)S(1)} collective-permute-done((bf16[8,4864]{1,0:T(8,128)(2,1)S(1)}, bf16[8,4864]{1,0:T(8,128)(2,1)S(1)}, u32[]{:S(2)}, u32[]{:S(2)}) %collective-permute-start.28) | collective-permute-done | bytes 77856 | tf_op jit(solution)/shard_map/ppermute | solution.py:41
  147.8 2.2 %fusion.21 = f32[8,576]{1,0:T(8,128)S(1)} fusion(bf16[7168,576]{0,1:T(8,128)(2,1)S(1)} %bitcast.55, bf16[8,7168]{1,0:T(8,128)(2,1)S(1)} %get-tuple-element.37, f32[8]{0:T(128)S(1)} %add_rsqrt_fusion.1), kind=kOutput, calls=%fused_computation.54 | convolution fusion | flops 66232320 | bytes 8390688 | tf_op jit(solution)/shard_map/dot_general | solution.py:131
  150.7 2.2 %add_convert_fusion = bf16[8,128,512]{2,1,0:T(8,128)(2,1)} fusion(bf16[8,384,576]{1,2,0:T(8,128)(2,1)S(1)} %copy-done.6, f32[8,512]{1,0:T(8,128)S(1)} %get-tuple-element.34, f32[8,128]{1,0:T(8,128)S(1)} %get-tuple-element.53, f32[8,128]{1,0:T(8,128)S(1)} %get-tuple-element.52, f32[8,128,384]{2,1,0:T(8,128)S(1)} %get-tuple-element.59, ...), kind=kOutput, calls=%fused_computation.5 | convolution fusion | flops 405929984 | bytes 5798912 | tf_op jit(solution)/shard_map/rhj,rjc->rhc/dot_general | solution.py:123
  (120 shorter events, 31.5 us)
Async XLA Ops:
  0.6 17.8 %collective-permute-start.4 = (bf16[1,7168,256]{2,1,0:T(8,128)(2,1)}, bf16[1,7168,256]{2,1,0:T(8,128)(2,1)}, u32[]{:S(2)}, u32[]{:S(2)}) collective-permute-start(bf16[1,7168,256]{2,1,0:T(8,128)(2,1)} %s1_.3), channel_id=1, source_target_pairs={{0,1},{1,0},{2,3},{3,2},{4,5},{5,4},{6,7},{7,6},{8,9},{9,8},{10,11... | collective-permute-start | bytes 11010056 | tf_op jit(solution)/shard_map/ppermute | solution.py:45
  0.7 17.7 %collective-permute-start.5 = (bf16[1,7168,256]{2,1,0:T(8,128)(2,1)}, bf16[1,7168,256]{2,1,0:T(8,128)(2,1)}, u32[]{:S(2)}, u32[]{:S(2)}) collective-permute-start(bf16[1,7168,256]{2,1,0:T(8,128)(2,1)} %s2_.3), channel_id=1, source_target_pairs={{0,1},{1,0},{2,3},{3,2},{4,5},{5,4},{6,7},{7,6},{8,9},{9,8},{10,11... | collective-permute-start | bytes 11010056 | tf_op jit(solution)/shard_map/ppermute | solution.py:45
  3.3 6.8 %collective-permute-start = (bf16[1,8,4864]{2,1,0:T(8,128)(2,1)S(1)}, bf16[1,8,4864]{2,1,0:T(8,128)(2,1)S(1)}, u32[]{:S(2)}, u32[]{:S(2)}) collective-permute-start(bf16[1,8,4864]{2,1,0:T(8,128)(2,1)S(1)} %slice_bitcast_fusion.8), channel_id=1, source_target_pairs={{0,2},{1,67},{2,0},{3,65},{4,6},{5,71},{6,4},{7,69},{8,10},{9,75},... | collective-permute-start | bytes 233480 | tf_op jit(solution)/shard_map/ppermute | solution.py:41
  5.1 30.8 %collective-permute-start.9 = (bf16[1,256,7168]{2,1,0:T(8,128)(2,1)}, bf16[1,256,7168]{2,1,0:T(8,128)(2,1)}, u32[]{:S(2)}, u32[]{:S(2)}) collective-permute-start(bf16[1,256,7168]{2,1,0:T(8,128)(2,1)} %own.3), channel_id=1, source_target_pairs={{0,1},{1,0},{2,3},{3,2},{4,5},{5,4},{6,7},{7,6},{8,9},{9,8},{10,11... | collective-permute-start | bytes 11010056 | tf_op jit(solution)/shard_map/ppermute | solution.py:45
  8.7 4.0 %collective-permute-start.2 = (bf16[1,8,2432]{2,1,0:T(8,128)(2,1)S(1)}, bf16[1,8,2432]{2,1,0:T(8,128)(2,1)S(1)}, u32[]{:S(2)}, u32[]{:S(2)}) collective-permute-start(bf16[1,8,2432]{2,1,0:T(8,128)(2,1)S(1)} %bitcast.67), channel_id=1, source_target_pairs={{0,4},{1,17},{2,6},{3,19},{4,0},{5,21},{6,2},{7,23},{8,12},{9,25},... | collective-permute-start | bytes 116744 | tf_op jit(solution)/shard_map/ppermute | solution.py:41
  10.2 8.2 %collective-permute-start.1 = (bf16[2,8,4864]{2,1,0:T(8,128)(2,1)S(1)}, bf16[2,8,4864]{2,1,0:T(8,128)(2,1)S(1)}, u32[]{:S(2)}, u32[]{:S(2)}) collective-permute-start(bf16[2,8,4864]{2,1,0:T(8,128)(2,1)S(1)} %pad_maximum_fusion.4), channel_id=1, source_target_pairs={{0,66},{1,3},{2,64},{3,1},{4,70},{5,7},{6,68},{7,5},{8,74},{9,11},... | collective-permute-start | bytes 466952 | tf_op jit(solution)/shard_map/ppermute | solution.py:41
  12.7 5.7 %collective-permute-start.3 = (bf16[2,8,2432]{2,1,0:T(8,128)(2,1)S(1)}, bf16[2,8,2432]{2,1,0:T(8,128)(2,1)S(1)}, u32[]{:S(2)}, u32[]{:S(2)}) collective-permute-start(bf16[2,8,2432]{2,1,0:T(8,128)(2,1)S(1)} %pad_maximum_fusion.5), channel_id=1, source_target_pairs={{0,12},{1,49},{2,14},{3,51},{4,8},{5,53},{6,10},{7,55},{8,4},{9,57... | collective-permute-start | bytes 233480 | tf_op jit(solution)/shard_map/ppermute | solution.py:41
  18.4 8.6 %collective-permute-start.6 = (bf16[4,8,7296]{2,1,0:T(8,128)(2,1)S(1)}, bf16[4,8,7296]{2,1,0:T(8,128)(2,1)S(1)}, u32[]{:S(2)}, u32[]{:S(2)}) collective-permute-start(bf16[4,8,7296]{2,1,0:T(8,128)(2,1)S(1)} %maximum_maximum_fusion), channel_id=1, source_target_pairs={{0,16},{1,5},{2,18},{3,7},{4,20},{5,1},{6,22},{7,3},{8,24},{9,13},... | collective-permute-start | bytes 1400840 | tf_op jit(solution)/shard_map/ppermute | solution.py:41
  20.4 13.6 %collective-permute-start.7 = (bf16[4,8,7296]{2,1,0:T(8,128)(2,1)S(1)}, bf16[4,8,7296]{2,1,0:T(8,128)(2,1)S(1)}, u32[]{:S(2)}, u32[]{:S(2)}) collective-permute-start(bf16[4,8,7296]{2,1,0:T(8,128)(2,1)S(1)} %maximum_maximum_fusion), channel_id=1, source_target_pairs={{0,48},{1,13},{2,50},{3,15},{4,52},{5,9},{6,54},{7,11},{8,56},{9,5... | collective-permute-start | bytes 1400840 | tf_op jit(solution)/shard_map/ppermute | solution.py:41
  22.9 12.6 %collective-permute-start.8 = (bf16[4,8,7296]{2,1,0:T(8,128)(2,1)S(1)}, bf16[4,8,7296]{2,1,0:T(8,128)(2,1)S(1)}, u32[]{:S(2)}, u32[]{:S(2)}) collective-permute-start(bf16[4,8,7296]{2,1,0:T(8,128)(2,1)S(1)} %maximum_maximum_fusion), channel_id=1, source_target_pairs={{0,32},{1,9},{2,34},{3,11},{4,36},{5,13},{6,38},{7,15},{8,40},{9,1... | collective-permute-start | bytes 1400840 | tf_op jit(solution)/shard_map/ppermute | solution.py:41
  36.0 10.3 %collective-permute-start.14 = (bf16[128,2432]{1,0:T(8,128)(2,1)S(1)}, bf16[128,2432]{1,0:T(8,128)(2,1)S(1)}, u32[]{:S(2)}, u32[]{:S(2)}) collective-permute-start(bf16[128,2432]{1,0:T(8,128)(2,1)S(1)} %bitcast.56), channel_id=1, source_target_pairs={{0,2},{1,67},{2,0},{3,65},{4,6},{5,71},{6,4},{7,69},{8,10},{9,75},... | collective-permute-start | bytes 1867784 | tf_op jit(solution)/shard_map/ppermute | solution.py:41
  36.2 11.4 %collective-permute-start.12 = (bf16[128,2432]{1,0:T(8,128)(2,1)S(1)}, bf16[128,2432]{1,0:T(8,128)(2,1)S(1)}, u32[]{:S(2)}, u32[]{:S(2)}) collective-permute-start(bf16[128,2432]{1,0:T(8,128)(2,1)S(1)} %bitcast.61), channel_id=1, source_target_pairs={{0,12},{1,49},{2,14},{3,51},{4,8},{5,53},{6,10},{7,55},{8,4},{9,57... | collective-permute-start | bytes 1867784 | tf_op jit(solution)/shard_map/ppermute | solution.py:41
  39.0 10.2 %collective-permute-start.10 = (bf16[128,2432]{1,0:T(8,128)(2,1)S(1)}, bf16[128,2432]{1,0:T(8,128)(2,1)S(1)}, u32[]{:S(2)}, u32[]{:S(2)}) collective-permute-start(bf16[128,2432]{1,0:T(8,128)(2,1)S(1)} %bitcast.59), channel_id=1, source_target_pairs={{0,4},{1,17},{2,6},{3,19},{4,0},{5,21},{6,2},{7,23},{8,12},{9,25},... | collective-permute-start | bytes 1867784 | tf_op jit(solution)/shard_map/ppermute | solution.py:41
  46.4 18.6 %collective-permute-start.15 = (bf16[256,2432]{1,0:T(8,128)(2,1)S(1)}, bf16[256,2432]{1,0:T(8,128)(2,1)}, u32[]{:S(2)}, u32[]{:S(2)}) collective-permute-start(bf16[256,2432]{1,0:T(8,128)(2,1)S(1)} %pad_maximum_fusion.1.x3), channel_id=1, source_target_pairs={{0,66},{1,3},{2,64},{3,1},{4,70},{5,7},{6,68},{7,5},{8,74},{9,11},... | collective-permute-start | bytes 3735560 | tf_op jit(solution)/shard_map/ppermute | solution.py:41
  48.8 17.2 %collective-permute-start.13 = (bf16[256,2432]{1,0:T(8,128)(2,1)}, bf16[256,2432]{1,0:T(8,128)(2,1)}, u32[]{:S(2)}, u32[]{:S(2)}) collective-permute-start(bf16[256,2432]{1,0:T(8,128)(2,1)} %pad_maximum_fusion.3.x2), channel_id=1, source_target_pairs={{0,4},{1,17},{2,6},{3,19},{4,0},{5,21},{6,2},{7,23},{8,12},{9,25},... | collective-permute-start | bytes 3735560 | tf_op jit(solution)/shard_map/ppermute | solution.py:41
  50.3 18.4 %collective-permute-start.11 = (bf16[256,2432]{1,0:T(8,128)(2,1)}, bf16[256,2432]{1,0:T(8,128)(2,1)}, u32[]{:S(2)}, u32[]{:S(2)}) collective-permute-start(bf16[256,2432]{1,0:T(8,128)(2,1)} %pad_maximum_fusion.2.x1), channel_id=1, source_target_pairs={{0,12},{1,49},{2,14},{3,51},{4,8},{5,53},{6,10},{7,55},{8,4},{9,57... | collective-permute-start | bytes 3735560 | tf_op jit(solution)/shard_map/ppermute | solution.py:41
  80.5 19.1 %collective-permute-start.20 = (bf16[256,2304]{1,0:T(8,128)(2,1)S(1)}, bf16[256,2304]{1,0:T(8,128)(2,1)S(1)}, u32[]{:S(2)}, u32[]{:S(2)}) collective-permute-start(bf16[256,2304]{1,0:T(8,128)(2,1)S(1)} %get-tuple-element.33), channel_id=1, source_target_pairs={{0,66},{1,3},{2,64},{3,1},{4,70},{5,7},{6,68},{7,5},{8,74},{9,11},... | collective-permute-start | bytes 3538952 | tf_op jit(solution)/shard_map/ppermute | solution.py:41
  83.1 18.9 %collective-permute-start.16 = (bf16[256,2432]{1,0:T(8,128)(2,1)S(1)}, bf16[256,2432]{1,0:T(8,128)(2,1)S(1)}, u32[]{:S(2)}, u32[]{:S(2)}) collective-permute-start(bf16[256,2432]{1,0:T(8,128)(2,1)S(1)} %get-tuple-element.29), channel_id=1, source_target_pairs={{0,12},{1,49},{2,14},{3,51},{4,8},{5,53},{6,10},{7,55},{8,4},{9,57... | collective-permute-start | bytes 3735560 | tf_op jit(solution)/shard_map/ppermute | solution.py:41
  85.7 18.4 %collective-permute-start.18 = (bf16[256,2432]{1,0:T(8,128)(2,1)S(1)}, bf16[256,2432]{1,0:T(8,128)(2,1)S(1)}, u32[]{:S(2)}, u32[]{:S(2)}) collective-permute-start(bf16[256,2432]{1,0:T(8,128)(2,1)S(1)} %get-tuple-element.31), channel_id=1, source_target_pairs={{0,4},{1,17},{2,6},{3,19},{4,0},{5,21},{6,2},{7,23},{8,12},{9,25},... | collective-permute-start | bytes 3735560 | tf_op jit(solution)/shard_map/ppermute | solution.py:41
  100.0 10.0 %collective-permute-start.21 = (bf16[128,2304]{1,0:T(8,128)(2,1)S(1)}, bf16[128,2304]{1,0:T(8,128)(2,1)S(1)}, u32[]{:S(2)}, u32[]{:S(2)}) collective-permute-start(bf16[128,2304]{1,0:T(8,128)(2,1)S(1)} %slice.215), channel_id=1, source_target_pairs={{0,2},{1,67},{2,0},{3,65},{4,6},{5,71},{6,4},{7,69},{8,10},{9,75},... | collective-permute-start | bytes 1769480 | tf_op jit(solution)/shard_map/ppermute | solution.py:41
  102.4 10.5 %collective-permute-start.17 = (bf16[128,2432]{1,0:T(8,128)(2,1)S(1)}, bf16[128,2432]{1,0:T(8,128)(2,1)S(1)}, u32[]{:S(2)}, u32[]{:S(2)}) collective-permute-start(bf16[128,2432]{1,0:T(8,128)(2,1)S(1)} %slice.214), channel_id=1, source_target_pairs={{0,4},{1,17},{2,6},{3,19},{4,0},{5,21},{6,2},{7,23},{8,12},{9,25},... | collective-permute-start | bytes 1867784 | tf_op jit(solution)/shard_map/ppermute | solution.py:41
  104.6 11.5 %collective-permute-start.19 = (bf16[128,2432]{1,0:T(8,128)(2,1)S(1)}, bf16[128,2432]{1,0:T(8,128)(2,1)S(1)}, u32[]{:S(2)}, u32[]{:S(2)}) collective-permute-start(bf16[128,2432]{1,0:T(8,128)(2,1)S(1)} %slice.213), channel_id=1, source_target_pairs={{0,12},{1,49},{2,14},{3,51},{4,8},{5,53},{6,10},{7,55},{8,4},{9,57... | collective-permute-start | bytes 1867784 | tf_op jit(solution)/shard_map/ppermute | solution.py:41
  113.0 3.2 %collective-permute-start.22 = (bf16[8,128]{1,0:T(8,128)(2,1)S(1)}, bf16[8,128]{1,0:T(8,128)(2,1)S(1)}, u32[]{:S(2)}, u32[]{:S(2)}) collective-permute-start(bf16[8,128]{1,0:T(8,128)(2,1)S(1)} %slice.150), channel_id=1, source_target_pairs={{0,1},{1,0},{2,3},{3,2},{4,5},{5,4},{6,7},{7,6},{8,9},{9,8},{10,11... | collective-permute-start | bytes 6152 | tf_op jit(solution)/shard_map/ppermute | solution.py:45
  118.2 8.6 %collective-permute-start.23 = (bf16[4,8,7168]{2,1,0:T(8,128)(2,1)S(1)}, bf16[4,8,7168]{2,1,0:T(8,128)(2,1)S(1)}, u32[]{:S(2)}, u32[]{:S(2)}) collective-permute-start(bf16[4,8,7168]{2,1,0:T(8,128)(2,1)S(1)} %get-tuple-element.41), channel_id=1, source_target_pairs={{0,16},{1,5},{2,18},{3,7},{4,20},{5,1},{6,22},{7,3},{8,24},{9,13},... | collective-permute-start | bytes 1376264 | tf_op jit(solution)/shard_map/ppermute | solution.py:41
  118.3 14.8 %collective-permute-start.24 = (bf16[4,8,7168]{2,1,0:T(8,128)(2,1)S(1)}, bf16[4,8,7168]{2,1,0:T(8,128)(2,1)S(1)}, u32[]{:S(2)}, u32[]{:S(2)}) collective-permute-start(bf16[4,8,7168]{2,1,0:T(8,128)(2,1)S(1)} %get-tuple-element.43), channel_id=1, source_target_pairs={{0,48},{1,13},{2,50},{3,15},{4,52},{5,9},{6,54},{7,11},{8,56},{9,5... | collective-permute-start | bytes 1376264 | tf_op jit(solution)/shard_map/ppermute | solution.py:41
  121.7 11.4 %collective-permute-start.25 = (bf16[4,8,7168]{2,1,0:T(8,128)(2,1)S(1)}, bf16[4,8,7168]{2,1,0:T(8,128)(2,1)S(1)}, u32[]{:S(2)}, u32[]{:S(2)}) collective-permute-start(bf16[4,8,7168]{2,1,0:T(8,128)(2,1)S(1)} %get-tuple-element.42), channel_id=1, source_target_pairs={{0,32},{1,9},{2,34},{3,11},{4,36},{5,13},{6,38},{7,15},{8,40},{9,1... | collective-permute-start | bytes 1376264 | tf_op jit(solution)/shard_map/ppermute | solution.py:41
  133.3 8.3 %collective-permute-start.29 = (bf16[8,2304]{1,0:T(8,128)(2,1)S(1)}, bf16[8,2304]{1,0:T(8,128)(2,1)S(1)}, u32[]{:S(2)}, u32[]{:S(2)}) collective-permute-start(bf16[8,2304]{1,0:T(8,128)(2,1)S(1)} %get-tuple-element.47), channel_id=1, source_target_pairs={{0,4},{1,17},{2,6},{3,19},{4,0},{5,21},{6,2},{7,23},{8,12},{9,25},... | collective-permute-start | bytes 110600 | tf_op jit(solution)/shard_map/ppermute | solution.py:41
  133.4 8.9 %collective-permute-start.30 = (bf16[8,2304]{1,0:T(8,128)(2,1)S(1)}, bf16[8,2304]{1,0:T(8,128)(2,1)S(1)}, u32[]{:S(2)}, u32[]{:S(2)}) collective-permute-start(bf16[8,2304]{1,0:T(8,128)(2,1)S(1)} %get-tuple-element.49), channel_id=1, source_target_pairs={{0,12},{1,49},{2,14},{3,51},{4,8},{5,53},{6,10},{7,55},{8,4},{9,57... | collective-permute-start | bytes 110600 | tf_op jit(solution)/shard_map/ppermute | solution.py:41
  136.7 5.6 %collective-permute-start.31 = (bf16[8,2304]{1,0:T(8,128)(2,1)S(1)}, bf16[8,2304]{1,0:T(8,128)(2,1)S(1)}, u32[]{:S(2)}, u32[]{:S(2)}) collective-permute-start(bf16[8,2304]{1,0:T(8,128)(2,1)S(1)} %get-tuple-element.48), channel_id=1, source_target_pairs={{0,8},{1,33},{2,10},{3,35},{4,12},{5,37},{6,14},{7,39},{8,0},{9,41... | collective-permute-start | bytes 110600 | tf_op jit(solution)/shard_map/ppermute | solution.py:41
  138.1 4.5 %collective-permute-start.26 = (bf16[8,4864]{1,0:T(8,128)(2,1)S(1)}, bf16[8,4864]{1,0:T(8,128)(2,1)S(1)}, u32[]{:S(2)}, u32[]{:S(2)}) collective-permute-start(bf16[8,4864]{1,0:T(8,128)(2,1)S(1)} %get-tuple-element.44), channel_id=1, source_target_pairs={{0,2},{1,67},{2,0},{3,65},{4,6},{5,71},{6,4},{7,69},{8,10},{9,75},... | collective-permute-start | bytes 233480 | tf_op jit(solution)/shard_map/ppermute | solution.py:41
  138.5 5.9 %collective-permute-start.27 = (bf16[8,4864]{1,0:T(8,128)(2,1)S(1)}, bf16[8,4864]{1,0:T(8,128)(2,1)S(1)}, u32[]{:S(2)}, u32[]{:S(2)}) collective-permute-start(bf16[8,4864]{1,0:T(8,128)(2,1)S(1)} %get-tuple-element.46), channel_id=1, source_target_pairs={{0,66},{1,3},{2,64},{3,1},{4,70},{5,7},{6,68},{7,5},{8,74},{9,11},... | collective-permute-start | bytes 233480 | tf_op jit(solution)/shard_map/ppermute | solution.py:41
  141.6 5.9 %collective-permute-start.28 = (bf16[8,4864]{1,0:T(8,128)(2,1)S(1)}, bf16[8,4864]{1,0:T(8,128)(2,1)S(1)}, u32[]{:S(2)}, u32[]{:S(2)}) collective-permute-start(bf16[8,4864]{1,0:T(8,128)(2,1)S(1)} %get-tuple-element.45), channel_id=1, source_target_pairs={{0,64},{1,65},{2,66},{3,67},{4,68},{5,69},{6,70},{7,71},{8,72},{9,... | collective-permute-start | bytes 233480 | tf_op jit(solution)/shard_map/ppermute | solution.py:41
  (14 other events, 277.2 us)

commit v5 on v4

--- a/solution.py
+++ b/solution.py
@@ -77,20 +77,6 @@
 
 def normalize(values):
     return values * lax.rsqrt(jnp.mean(values * values, axis=-1, keepdims=True) + 1e-06)
-
-
-def prepare(router, routes, hidden):
-    experts = router.shape[1]
-    normed = normalize(hidden.astype(jnp.float32)).astype(jnp.bfloat16)
-    logits = jnp.dot(normed, router, preferred_element_type=jnp.float32)
-    labels = jnp.arange(experts, dtype=jnp.int32)
-    chosen = jnp.any(routes[:, :, None] == labels[None, None, :], axis=1)
-    affinity = jnp.where(chosen, jax.nn.sigmoid(logits), 0.0)
-    weights = 2.5 * affinity / jnp.sum(affinity, axis=1, keepdims=True)
-    high = weights.astype(jnp.bfloat16)
-    low = (weights - high.astype(jnp.float32)).astype(jnp.bfloat16)
-    pad = jnp.zeros((hidden.shape[0], LANES - 2 * experts), jnp.bfloat16)
-    return normed, jnp.concatenate([high, low, pad], axis=1)
 
 
 def rotate(values, positions):
@@ -153,21 +139,11 @@
     return list(zip(starts, widths))
 
 
-def multiply(slabs, rows, widths, outs):
-    for part, (start, width) in enumerate(spans(widths)):
-        for i, slab in enumerate(slabs):
-            outs[part][:, pl.ds(i * HIDDEN, HIDDEN)] = jnp.dot(
-                rows[part][:, :width],
-                slab[0, pl.ds(start, width)],
-                preferred_element_type=jnp.float32,
-            )
-
-
-def call(kernel, args, out_shape, scratch_shapes=(), limit=16):
-    vmem = pl.BlockSpec(memory_space=pltpu.VMEM)
+def call(kernel, args, in_hbm, out_shape, scratch_shapes=(), limit=16):
+    vmem, hbm = pl.BlockSpec(memory_space=pltpu.VMEM), pl.BlockSpec(memory_space=pltpu.HBM)
     return pl.pallas_call(
         kernel,
-        in_specs=[vmem] * len(args),
+        in_specs=[vmem] * (len(args) - in_hbm) + [hbm] * in_hbm,
         out_specs=[vmem] * len(out_shape),
         out_shape=out_shape,
         scratch_shapes=scratch_shapes,
@@ -175,28 +151,97 @@
     )(*args)
 
 
-def early_kernel(widths, x1, x2, x3, s1, s2, s3, s4, h1, h2, h3):
-    multiply((s1, s2, s3, s4), (x1, x2, x3), widths, (h1, h2, h3))
+def prepare_kernel(cut, hidden, router, routes, first, second):
+    f32, bf = jnp.float32, jnp.bfloat16
+    rows, experts = hidden.shape[0], router.shape[1]
+    values = hidden[...].astype(f32)
+    normed = normalize(values).astype(bf)
+    first[...] = normed[:, :cut]
+    rest = hidden.shape[1] - cut
+    second[:, :rest] = normed[:, cut:]
+    logits = jnp.dot(normed, router[...], preferred_element_type=f32)
+    labels = lax.broadcasted_iota(jnp.int32, (rows, experts), 1)
+    chosen = labels == routes[:, 0:1]
+    for k in range(1, routes.shape[1]):
+        chosen = chosen | (labels == routes[:, k : k + 1])
+    affinity = jnp.where(chosen, 1.0 / (1.0 + jnp.exp(-logits)), 0.0)
+    weights = 2.5 * affinity / jnp.sum(affinity, axis=1, keepdims=True)
+    high = weights.astype(bf)
+    low = (weights - high.astype(f32)).astype(bf)
+    source = lax.broadcasted_iota(jnp.int32, (experts, LANES), 0)
+    target = lax.broadcasted_iota(jnp.int32, (experts, LANES), 1)
+    spread = jnp.dot(high, (source == target).astype(bf), preferred_element_type=f32)
+    spread += jnp.dot(low, (source + experts == target).astype(bf), preferred_element_type=f32)
+    second[:, rest:] = spread.astype(bf)
+
+
+def prepare(router, routes, hidden, cut):
+    rows, width = hidden.shape
+    widths = (cut, width - cut + LANES)
+    out_shape = [jax.ShapeDtypeStruct((rows, w), jnp.bfloat16) for w in widths]
+    return call(functools.partial(prepare_kernel, cut), (hidden, router, routes), 0, out_shape)
+
+
+def fetch(sources, targets, sems):
+    copies = [pltpu.make_async_copy(s.at[0], t, sems.at[i]) for i, (s, t) in enumerate(zip(sources, targets))]
+    for copy in copies:
+        copy.start()
+    return copies
+
+
+def multiply(slab, i, rows, outs, widths):
+    for (start, width), values, out in zip(spans(widths), rows, outs):
+        out[:, pl.ds(i * HIDDEN, HIDDEN)] = jnp.dot(
+            values, slab[pl.ds(start, width)], preferred_element_type=jnp.float32
+        )
+
+
+def lift(slabs, ring, sems, rows, outs, widths, meanwhile):
+    copies = [pltpu.make_async_copy(s.at[0], ring.at[i % 2], sems.at[i]) for i, s in enumerate(slabs)]
+    copies[0].start()
+    copies[1].start()
+    for i, copy in enumerate(copies):
+        copy.wait()
+        multiply(ring.at[i % 2], i, rows, outs, widths)
+        if i + 2 < len(copies):
+            copies[i + 2].start()
+        if i == 1:
+            meanwhile()
+
+
+def early_kernel(widths, x1, x2, x3, s1, s2, s3, s4, h1, h2, h3, ring, sems):
+    rows = [x[:, :w] for x, w in zip((x1, x2, x3), widths)]
+    lift((s1, s2, s3, s4), ring, sems, rows, (h1, h2, h3), widths, lambda: None)
 
 
 def early(rows, slabs, widths):
     count = rows[0].shape[0]
-    out_shape = [jax.ShapeDtypeStruct((count, 4 * HIDDEN), jnp.float32)] * 3
-    return call(functools.partial(early_kernel, widths), (*rows, *slabs), out_shape)
-
-
-def lower(rows, own, other, start, width):
-    cols = pl.ds(start, width)
-    product = jnp.dot(rows[:, :HIDDEN], own[0, :, cols], preferred_element_type=jnp.float32)
-    product += jnp.dot(rows[:, HIDDEN:], other[0, :, cols], preferred_element_type=jnp.float32)
-    return product.astype(jnp.bfloat16)
-
-
-def late_kernel(widths, x1, x2, x3, h1, h2, h3, before, picks, s1, s2, s3, s4, own, other, o1, o2, o3, straight, turned, g1, g2, g3):
+    return call(
+        functools.partial(early_kernel, widths),
+        (*rows, *slabs),
+        4,
+        [jax.ShapeDtypeStruct((count, 4 * HIDDEN), jnp.float32)] * 3,
+        [pltpu.VMEM((2, *slabs[0].shape[1:]), jnp.bfloat16), pltpu.SemaphoreType.DMA((4,))],
+        14,
+    )
+
+
+def late_kernel(widths, x1, x2, x3, h1, h2, h3, before, picks, s1, s2, s3, s4, own_low, low, o1, o2, o3, straight, turned, g1, g2, g3, ring, lows, sems):
     f32, bf = jnp.float32, jnp.bfloat16
-    multiply((s1, s2, s3, s4), (x1, x2, x3), widths, (g1, g2, g3))
     half = x1.shape[0]
     count, block = 2 * half, half // 2
+    low_targets = [lows.at[pl.ds(i * HIDDEN, HIDDEN)] for i in range(2)]
+    low_copies = [
+        pltpu.make_async_copy(s.at[0], t, sems.at[4 + i])
+        for i, (s, t) in enumerate(zip((own_low, low), low_targets))
+    ]
+
+    def fetch_lows():
+        for copy in low_copies:
+            copy.start()
+
+    rows = [x[:, :w] for x, w in zip((x1, x2, x3), widths)]
+    lift((s1, s2, s3, s4), ring, sems, rows, (g1, g2, g3), widths, fetch_lows)
 
     def turn(values):
         cells = values.reshape(4, 4, 4, count // 64, values.shape[-1])
@@ -211,7 +256,8 @@
         third = jnp.concatenate([h3[:, cols], g3[:, cols]], axis=0)
         return first + second + turn(third)
 
-    cells = jnp.concatenate([before[...], x3[:, pl.ds(widths[2], LANES)]], axis=0).astype(f32)
+    tile = pl.ds(widths[2], LANES)
+    cells = jnp.concatenate([before[...], x3[:, tile]], axis=0).astype(f32)
     for i in range(2):
         weight = turn(cells * picks[pl.ds(i, 1), :])
         weight = jnp.sum(weight, axis=1, keepdims=True)
@@ -225,38 +271,57 @@
         jnp.concatenate([straight[block:half, :], straight[half + block :, :]], axis=0),
         turned[half:, :],
     )
-    for part, (start, width) in enumerate(spans(widths)):
-        (o1, o2, o3)[part][...] = lower(leaving[part], own, other, start, width)
-
-
-def late(rows, partial, before, picks, slabs, lows, widths):
+    for copy in low_copies:
+        copy.wait()
+    for (start, width), values, out in zip(spans(widths), leaving, (o1, o2, o3)):
+        out[...] = jnp.dot(values, lows[:, pl.ds(start, width)], preferred_element_type=f32).astype(bf)
+
+
+def late(rows, partial, cells, picks, slabs, lows, widths):
     bf, f32 = jnp.bfloat16, jnp.float32
-    count = rows[0].shape[0]
+    half = rows[0].shape[0]
+    depth = slabs[0].shape[1]
     return call(
         functools.partial(late_kernel, widths),
-        (*rows, *partial, before, picks, *slabs, *lows),
-        [jax.ShapeDtypeStruct((count, width), bf) for width in widths]
-        + [jax.ShapeDtypeStruct((2 * count, 2 * HIDDEN), bf)] * 2,
-        [pltpu.VMEM((count, 4 * HIDDEN), f32)] * 3,
-    )
-
-
-def stay_kernel(widths, straight, turned, own, other, o1, o2, o3):
-    half = straight.shape[0] // 2
-    block = half // 2
+        (*rows, *partial, cells, picks, *slabs, *lows),
+        6,
+        [jax.ShapeDtypeStruct((half, width), bf) for width in widths]
+        + [jax.ShapeDtypeStruct((2 * half, 2 * HIDDEN), bf)] * 2,
+        [pltpu.VMEM((half, 4 * HIDDEN), f32)] * 3
+        + [
+            pltpu.VMEM((2, depth, HIDDEN), bf),
+            pltpu.VMEM((2 * HIDDEN, depth), bf),
+            pltpu.SemaphoreType.DMA((6,)),
+        ],
+        34,
+    )
+
+
+def stay_kernel(widths, straight, turned, own_low, low, o1, o2, o3, lows, sems):
+    copies = fetch((own_low, low), [lows.at[pl.ds(i * HIDDEN, HIDDEN)] for i in range(2)], sems)
+    block = straight.shape[0] // 4
     staying = (
-        straight[:half, :],
-        jnp.concatenate([straight[:block, :], straight[half : half + block, :]], axis=0),
-        turned[:half, :],
-    )
-    for part, (start, width) in enumerate(spans(widths)):
-        (o1, o2, o3)[part][...] = lower(staying[part], own, other, start, width)
+        straight[: 2 * block, :],
+        jnp.concatenate([straight[:block, :], straight[2 * block : 3 * block, :]], axis=0),
+        turned[: 2 * block, :],
+    )
+    for copy in copies:
+        copy.wait()
+    for (start, width), values, out in zip(spans(widths), staying, (o1, o2, o3)):
+        product = jnp.dot(values, lows[:, pl.ds(start, width)], preferred_element_type=jnp.float32)
+        out[...] = product.astype(jnp.bfloat16)
 
 
 def stay(straight, turned, lows, widths):
     count = straight.shape[0] // 2
-    out_shape = [jax.ShapeDtypeStruct((count, width), jnp.bfloat16) for width in widths]
-    return call(functools.partial(stay_kernel, widths), (straight, turned, *lows), out_shape)
+    return call(
+        functools.partial(stay_kernel, widths),
+        (straight, turned, *lows),
+        2,
+        [jax.ShapeDtypeStruct((count, width), jnp.bfloat16) for width in widths],
+        [pltpu.VMEM((2 * HIDDEN, lows[0].shape[2]), jnp.bfloat16), pltpu.SemaphoreType.DMA((2,))],
+        14,
+    )
 
 
 def body(hidden, router, routes, w_gate, w_up, w_down, w_latent, lengths, latent_cache, queries):
@@ -270,11 +335,11 @@
     other = mine + 1 - 2 * lax.rem(mine, 2)
 
     other_gate, other_up = swap_cores(w_gate), swap_cores(w_up)
-    normed, gates = prepare(router, routes, hidden)
-
-    first = gather_pairs(normed[None, :, :cut], "y", SPLIT)
-    second = gather_pairs(jnp.concatenate([normed[:, cut:], gates], axis=1)[None], "a", SAME)
-    both = jnp.concatenate([jnp.concatenate(first), jnp.concatenate(second)], axis=2)
+    first, second = prepare(router, routes, hidden, cut)
+
+    first = jnp.concatenate(gather_pairs(first[None], "y", SPLIT))
+    second = jnp.concatenate(gather_pairs(second[None], "a", SAME))
+    both = jnp.concatenate([first, second], axis=2)
     both, other_gate, other_up = lax.optimization_barrier((both, other_gate, other_up))
     other_down = swap_cores(w_down)
     both = jnp.stack(gather(both, "b", SAME))
@@ -288,22 +353,19 @@
     marks = jnp.stack([(spots == e) | (spots == e + experts) for e in (mine, other)]).astype(f32)
     picks = jnp.concatenate([marks, jnp.zeros((6, LANES), f32)])
     slabs, lows = (w_gate, w_up, other_gate, other_up), (w_down, other_down)
-    partial = early((x1[0], x2[0], x3[0]), slabs, widths)
-    before = x3[0][:, widths[2] :]
-    *leaving, straight, turned = late(
-        (x1[1], x2[1], x3[1]), partial, before, picks, slabs, lows, widths
-    )
+    partial = early([part[0] for part in (x1, x2, x3)], slabs, widths)
+    cells = x3[0][:, widths[2] :]
+    last_rows = [part[1] for part in (x1, x2, x3)]
+    *leaving, straight, turned = late(last_rows, partial, cells, picks, slabs, lows, widths)
     staying = stay(straight, turned, lows, widths)
 
-    y1 = reduce_pairs(staying[0], leaving[0], "a", SAME).astype(bf)
-    y2 = reduce_pairs(staying[1], leaving[1], "a", TURNED).astype(bf)
-    y3 = reduce_pairs(staying[2], leaving[2], "y", SPLIT).astype(bf)
-    both = together(jnp.concatenate([y1, y2, y3], axis=1)).reshape(4, 4, rows, width)
+    ways = (("a", SAME), ("a", TURNED), ("y", SPLIT))
+    sums = [reduce_pairs(staying[i], leaving[i], *way).astype(bf) for i, way in enumerate(ways)]
+    both = together(jnp.concatenate(sums, axis=1)).reshape(4, 4, rows, width)
     both = reduce([both[i] for i in range(4)], "b", SAME).astype(bf)
-    first, second = both[..., :cut], both[..., cut:]
-    first = reduce([first[i] for i in range(4)], "y", SPLIT)
-    second = reduce([second[i] for i in range(4)], "a", SAME)
-    mixture = jnp.concatenate([first, second], axis=1)
+    first = reduce_pairs(both[:2, :, :cut], both[2:, :, :cut], "y", SPLIT)
+    second = reduce_pairs(both[:2, :, cut:], both[2:, :, cut:], "a", SAME)
+    mixture = jnp.concatenate([first[0], second[0]], axis=1)
     layer_out = (hidden.astype(f32) + mixture).astype(bf)
 
     highest, total, summed = attend_cache(lengths, latent_cache, queries)

time: 153 us -> 152 us (level)
  starting transfers between devices: 46.5 us -> 42.4 us
  waiting for transfers between devices: 59.1 us -> 62.6 us
  other arithmetic: 8.8 us -> 5.75 us
  Pallas kernels: 24.1 us -> 26.2 us
  local copies, waits for them, and re-layouts: 5.22 us -> 7.03 us
    ppermute x28 -> x26, waiting for transfers between devices: 59 us -> 62.6 us  [flip(): return lax.ppermute(values, AXES, partners(AXIS[axis], flips))]
    ppermute x28 -> x26, starting transfers between devices: 44.6 us -> 41.6 us  [flip(): return lax.ppermute(values, AXES, partners(AXIS[axis], flips))]
    pallas_call x3 -> x4, Pallas kernels: 24.1 us -> 26.2 us  [call(): pl.pallas_call(kernel, in_specs=[vmem] * (len(args) - in_hbm) + [hbm] * i...]
    unnamed x28 -> x35, local copies, waits for them, and re-layouts: 4.13 us -> 6.02 us
  transfers between devices with their start and end apart: 32 -> 30, of which waited for: 19 -> 18; matrix products, arithmetic and copies ran while one was open for 7% -> 5% of each run, Pallas kernels for 8% -> 9%
where the time goes in v5:
time: 152 us
  waiting for transfers between devices  62.6 us (41%)
  starting transfers between devices  42.4 us (28%)
  Pallas kernels  26.2 us (17%)
  local copies, waits for them, and re-layouts  7.03 us (5%)
  matrix products  5.85 us (4%)
  other arithmetic  5.75 us (4%)
  between operations  1.78 us (1%)
    ppermute x26, waiting for transfers between devices, flip(): return lax.ppermute(values, AXES, partners(AXIS[axis], flips))  62.6 us
    ppermute x26, starting transfers between devices, flip(): return lax.ppermute(values, AXES, partners(AXIS[axis], flips))  41.6 us
    pallas_call x4, Pallas kernels, call(): pl.pallas_call(kernel, in_specs=[vmem] * (len(args) - in_hbm) + [hbm] * i...  26.2 us
    unnamed x35, local copies, waits for them, and re-layouts  6.02 us
  transfers between devices with their start and end apart: 30, of which 18 were waited for; matrix products, arithmetic and copies ran while one was open for 5% of the time, Pallas kernels for 9%

profile of v5, /device:TPU:0, one launch (start us, length us, event | category | flops | bytes accessed | tf_op | source)
XLA Modules:
  0.0 151.6 jit_solution(8273034900211114989)
XLA Ops:
  1.4 1.9 %copy.12.router = bf16[7168,32]{1,0:T(8,128)(2,1)S(1)} copy(bf16[7168,32]{0,1:T(8,128)(2,1)} %param.11) | data formatting | bytes 917504 | tf_op args[1]
  8.4 3.2 %collective-permute-start.1 = (bf16[2,8,4864]{2,1,0:T(8,128)(2,1)S(1)}, bf16[2,8,4864]{2,1,0:T(8,128)(2,1)S(1)}, u32[]{:S(2)}, u32[]{:S(2)}) collective-permute-start(bf16[2,8,4864]{2,1,0:T(8,128)(2,1)S(1)} %pad_maximum_fusion.4), channel_id=1, source_target_pairs={{0,66},{1,3},{2,64},{3,1},{4,70},{5,7},{6,68},{7,5},{8,74},{9,11},... | collective-permute-start | bytes 466952 | tf_op jit(solution)/shard_map/ppermute | solution.py:41
  11.6 2.8 %collective-permute-start.3 = (bf16[2,8,2432]{2,1,0:T(8,128)(2,1)S(1)}, bf16[2,8,2432]{2,1,0:T(8,128)(2,1)S(1)}, u32[]{:S(2)}, u32[]{:S(2)}) collective-permute-start(bf16[2,8,2432]{2,1,0:T(8,128)(2,1)S(1)} %pad_maximum_fusion.5), channel_id=1, source_target_pairs={{0,12},{1,49},{2,14},{3,51},{4,8},{5,53},{6,10},{7,55},{8,4},{9,57... | collective-permute-start | bytes 233480 | tf_op jit(solution)/shard_map/ppermute | solution.py:41
  14.4 2.8 %collective-permute-done.3 = bf16[2,8,2432]{2,1,0:T(8,128)(2,1)S(1)} collective-permute-done((bf16[2,8,2432]{2,1,0:T(8,128)(2,1)S(1)}, bf16[2,8,2432]{2,1,0:T(8,128)(2,1)S(1)}, u32[]{:S(2)}, u32[]{:S(2)}) %collective-permute-start.3) | collective-permute-done | bytes 77856 | tf_op jit(solution)/shard_map/ppermute | solution.py:41
  17.3 2.0 %collective-permute-start.6 = (bf16[4,8,7296]{2,1,0:T(8,128)(2,1)S(1)}, bf16[4,8,7296]{2,1,0:T(8,128)(2,1)S(1)}, u32[]{:S(2)}, u32[]{:S(2)}) collective-permute-start(bf16[4,8,7296]{2,1,0:T(8,128)(2,1)S(1)} %maximum_maximum_fusion), channel_id=1, source_target_pairs={{0,16},{1,5},{2,18},{3,7},{4,20},{5,1},{6,22},{7,3},{8,24},{9,13},... | collective-permute-start | bytes 1400840 | tf_op jit(solution)/shard_map/ppermute | solution.py:41
  19.3 2.5 %collective-permute-start.7 = (bf16[4,8,7296]{2,1,0:T(8,128)(2,1)S(1)}, bf16[4,8,7296]{2,1,0:T(8,128)(2,1)S(1)}, u32[]{:S(2)}, u32[]{:S(2)}) collective-permute-start(bf16[4,8,7296]{2,1,0:T(8,128)(2,1)S(1)} %maximum_maximum_fusion), channel_id=1, source_target_pairs={{0,48},{1,13},{2,50},{3,15},{4,52},{5,9},{6,54},{7,11},{8,56},{9,5... | collective-permute-start | bytes 1400840 | tf_op jit(solution)/shard_map/ppermute | solution.py:41
  22.9 3.1 %collective-permute-done.6 = bf16[4,8,7296]{2,1,0:T(8,128)(2,1)S(1)} collective-permute-done((bf16[4,8,7296]{2,1,0:T(8,128)(2,1)S(1)}, bf16[4,8,7296]{2,1,0:T(8,128)(2,1)S(1)}, u32[]{:S(2)}, u32[]{:S(2)}) %collective-permute-start.6) | collective-permute-done | bytes 466976 | tf_op jit(solution)/shard_map/ppermute | solution.py:41
  26.0 7.0 %collective-permute-done.7 = bf16[4,8,7296]{2,1,0:T(8,128)(2,1)S(1)} collective-permute-done((bf16[4,8,7296]{2,1,0:T(8,128)(2,1)S(1)}, bf16[4,8,7296]{2,1,0:T(8,128)(2,1)S(1)}, u32[]{:S(2)}, u32[]{:S(2)}) %collective-permute-start.7) | collective-permute-done | bytes 466976 | tf_op jit(solution)/shard_map/ppermute | solution.py:41
  35.2 2.8 %collective-permute-start.12 = (bf16[128,2432]{1,0:T(8,128)(2,1)S(1)}, bf16[128,2432]{1,0:T(8,128)(2,1)S(1)}, u32[]{:S(2)}, u32[]{:S(2)}) collective-permute-start(bf16[128,2432]{1,0:T(8,128)(2,1)S(1)} %bitcast.46), channel_id=1, source_target_pairs={{0,12},{1,49},{2,14},{3,51},{4,8},{5,53},{6,10},{7,55},{8,4},{9,57... | collective-permute-start | bytes 1867784 | tf_op jit(solution)/shard_map/ppermute | solution.py:41
  37.9 7.6 %collective-permute-done.14 = bf16[128,2432]{1,0:T(8,128)(2,1)S(1)} collective-permute-done((bf16[128,2432]{1,0:T(8,128)(2,1)S(1)}, bf16[128,2432]{1,0:T(8,128)(2,1)S(1)}, u32[]{:S(2)}, u32[]{:S(2)}) %collective-permute-start.14) | collective-permute-done | bytes 622624 | tf_op jit(solution)/shard_map/ppermute | solution.py:41
  50.4 2.1 %collective-permute-start.11 = (bf16[256,2432]{1,0:T(8,128)(2,1)}, bf16[256,2432]{1,0:T(8,128)(2,1)}, u32[]{:S(2)}, u32[]{:S(2)}) collective-permute-start(bf16[256,2432]{1,0:T(8,128)(2,1)} %pad_maximum_fusion.2.x1), channel_id=1, source_target_pairs={{0,12},{1,49},{2,14},{3,51},{4,8},{5,53},{6,10},{7,55},{8,4},{9,57... | collective-permute-start | bytes 3735560 | tf_op jit(solution)/shard_map/ppermute | solution.py:41
  52.6 2.0 %copy-done.2 = bf16[1,7168,256]{2,1,0:T(8,128)(2,1)S(1)} copy-done((bf16[1,7168,256]{2,1,0:T(8,128)(2,1)S(1)}, bf16[1,7168,256]{2,1,0:T(8,128)(2,1)}, u32[]{:S(2)}) %copy-start.2) | copy-done | bytes 3670040
  54.6 2.0 %copy-done.4 = bf16[1,7168,256]{2,1,0:T(8,128)(2,1)S(1)} copy-done((bf16[1,7168,256]{2,1,0:T(8,128)(2,1)S(1)}, bf16[1,7168,256]{2,1,0:T(8,128)(2,1)}, u32[]{:S(2)}) %copy-start.4) | copy-done | bytes 3670040
  56.7 8.9 %shard_map.114 = (f32[256,1024]{1,0:T(8,128)S(1)}, f32[256,1024]{1,0:T(8,128)S(1)}, f32[256,1024]{1,0:T(8,128)S(1)}) custom-call(bf16[256,2432]{1,0:T(8,128)(2,1)} %pad_maximum_fusion.2.x1, bf16[256,2432]{1,0:T(8,128)(2,1)} %pad_maximum_fusion.3.x2, bf16[256,2432]{1,0:T(8,128)(2,1)S(1)} %pad_maximum_fusion.1.x3, bf16[1,7168,256]{2,1,0:T(8,128)(2,1)S(1)} %copy-done.2, ...), custom_call_target="tpu_custom_call" | custom-call | tf_op jit(solution)/shard_map/pallas_call | solution.py:144
  65.6 3.2 %collective-permute-done.11.x1 = bf16[256,2432]{1,0:T(8,128)(2,1)} collective-permute-done((bf16[256,2432]{1,0:T(8,128)(2,1)}, bf16[256,2432]{1,0:T(8,128)(2,1)}, u32[]{:S(2)}, u32[]{:S(2)}) %collective-permute-start.11) | collective-permute-done | bytes 1245216 | tf_op jit(solution)/shard_map/ppermute | solution.py:41
  68.9 12.2 %shard_map.115 = (bf16[256,2432]{1,0:T(8,128)(2,1)S(1)}, bf16[256,2432]{1,0:T(8,128)(2,1)S(1)}, bf16[256,2304]{1,0:T(8,128)(2,1)S(1)}, bf16[512,512]{1,0:T(8,128)(2,1)S(1)}, bf16[512,512]{1,0:T(8,128)(2,1)S(1)}) custom-call(bf16[256,2432]{1,0:T(8,128)(2,1)} %collective-permute-done.11.x1, bf16[256,2432]{1,0:T(8,128)(2,1)} %collective-permute-done.13.x2, ...), custom_call_target="tpu_custom_call" | custom-call | tf_op jit(solution)/shard_map/pallas_call | solution.py:144
  81.1 1.8 %collective-permute-start.20 = (bf16[256,2304]{1,0:T(8,128)(2,1)S(1)}, bf16[256,2304]{1,0:T(8,128)(2,1)S(1)}, u32[]{:S(2)}, u32[]{:S(2)}) collective-permute-start(bf16[256,2304]{1,0:T(8,128)(2,1)S(1)} %get-tuple-element.37), channel_id=1, source_target_pairs={{0,66},{1,3},{2,64},{3,1},{4,70},{5,7},{6,68},{7,5},{8,74},{9,11},... | collective-permute-start | bytes 3538952 | tf_op jit(solution)/shard_map/ppermute | solution.py:41
  82.8 2.6 %collective-permute-start.16 = (bf16[256,2432]{1,0:T(8,128)(2,1)S(1)}, bf16[256,2432]{1,0:T(8,128)(2,1)S(1)}, u32[]{:S(2)}, u32[]{:S(2)}) collective-permute-start(bf16[256,2432]{1,0:T(8,128)(2,1)S(1)} %get-tuple-element.33), channel_id=1, source_target_pairs={{0,12},{1,49},{2,14},{3,51},{4,8},{5,53},{6,10},{7,55},{8,4},{9,57... | collective-permute-start | bytes 3735560 | tf_op jit(solution)/shard_map/ppermute | solution.py:41
  85.9 4.4 %shard_map.116 = (bf16[256,2432]{1,0:T(8,128)(2,1)S(1)}, bf16[256,2432]{1,0:T(8,128)(2,1)S(1)}, bf16[256,2304]{1,0:T(8,128)(2,1)S(1)}) custom-call(bf16[512,512]{1,0:T(8,128)(2,1)S(1)} %get-tuple-element.30.straight, bf16[512,512]{1,0:T(8,128)(2,1)S(1)} %get-tuple-element.31.turned, bf16[1,256,7168]{2,1,0:T(8,128)(2,1)S(1)} %copy-done.1, ...), custom_call_target="tpu_custom_call" | custom-call | tf_op jit(solution)/shard_map/pallas_call | solution.py:144
  90.4 10.5 %collective-permute-done.20 = bf16[256,2304]{1,0:T(8,128)(2,1)S(1)} collective-permute-done((bf16[256,2304]{1,0:T(8,128)(2,1)S(1)}, bf16[256,2304]{1,0:T(8,128)(2,1)S(1)}, u32[]{:S(2)}, u32[]{:S(2)}) %collective-permute-start.20) | collective-permute-done | bytes 1179680 | tf_op jit(solution)/shard_map/ppermute | solution.py:41
  102.9 2.9 %collective-permute-start.19 = (bf16[128,2432]{1,0:T(8,128)(2,1)S(1)}, bf16[128,2432]{1,0:T(8,128)(2,1)S(1)}, u32[]{:S(2)}, u32[]{:S(2)}) collective-permute-start(bf16[128,2432]{1,0:T(8,128)(2,1)S(1)} %slice.192), channel_id=1, source_target_pairs={{0,12},{1,49},{2,14},{3,51},{4,8},{5,53},{6,10},{7,55},{8,4},{9,57... | collective-permute-start | bytes 1867784 | tf_op jit(solution)/shard_map/ppermute | solution.py:41
  105.8 5.4 %collective-permute-done.21 = bf16[128,2304]{1,0:T(8,128)(2,1)S(1)} collective-permute-done((bf16[128,2304]{1,0:T(8,128)(2,1)S(1)}, bf16[128,2304]{1,0:T(8,128)(2,1)S(1)}, u32[]{:S(2)}, u32[]{:S(2)}) %collective-permute-start.21) | collective-permute-done | bytes 589856 | tf_op jit(solution)/shard_map/ppermute | solution.py:41
  112.2 2.3 %collective-permute-done.19 = bf16[128,2432]{1,0:T(8,128)(2,1)S(1)} collective-permute-done((bf16[128,2432]{1,0:T(8,128)(2,1)S(1)}, bf16[128,2432]{1,0:T(8,128)(2,1)S(1)}, u32[]{:S(2)}, u32[]{:S(2)}) %collective-permute-start.19) | collective-permute-done | bytes 622624 | tf_op jit(solution)/shard_map/ppermute | solution.py:41
  116.3 2.9 %collective-permute-start.24 = (bf16[4,8,7168]{2,1,0:T(8,128)(2,1)S(1)}, bf16[4,8,7168]{2,1,0:T(8,128)(2,1)S(1)}, u32[]{:S(2)}, u32[]{:S(2)}) collective-permute-start(bf16[4,8,7168]{2,1,0:T(8,128)(2,1)S(1)} %get-tuple-element.47), channel_id=1, source_target_pairs={{0,48},{1,13},{2,50},{3,15},{4,52},{5,9},{6,54},{7,11},{8,56},{9,5... | collective-permute-start | bytes 1376264 | tf_op jit(solution)/shard_map/ppermute | solution.py:41
  122.2 2.7 %collective-permute-done.23 = bf16[4,8,7168]{2,1,0:T(8,128)(2,1)S(1)} collective-permute-done((bf16[4,8,7168]{2,1,0:T(8,128)(2,1)S(1)}, bf16[4,8,7168]{2,1,0:T(8,128)(2,1)S(1)}, u32[]{:S(2)}, u32[]{:S(2)}) %collective-permute-start.23) | collective-permute-done | bytes 458784 | tf_op jit(solution)/shard_map/ppermute | solution.py:41
  124.8 5.3 %collective-permute-done.24 = bf16[4,8,7168]{2,1,0:T(8,128)(2,1)S(1)} collective-permute-done((bf16[4,8,7168]{2,1,0:T(8,128)(2,1)S(1)}, bf16[4,8,7168]{2,1,0:T(8,128)(2,1)S(1)}, u32[]{:S(2)}, u32[]{:S(2)}) %collective-permute-start.24) | collective-permute-done | bytes 458784 | tf_op jit(solution)/shard_map/ppermute | solution.py:41
  131.3 3.0 %collective-permute-start.28 = (bf16[2,8,2304]{2,1,0:T(8,128)(2,1)S(1)}, bf16[2,8,2304]{2,1,0:T(8,128)(2,1)S(1)}, u32[]{:S(2)}, u32[]{:S(2)}) collective-permute-start(bf16[2,8,2304]{2,1,0:T(8,128)(2,1)S(1)} %slice.142), channel_id=1, source_target_pairs={{0,12},{1,49},{2,14},{3,51},{4,8},{5,53},{6,10},{7,55},{8,4},{9,57... | collective-permute-start | bytes 221192 | tf_op jit(solution)/shard_map/ppermute | solution.py:41
  134.3 3.1 %collective-permute-start.26 = (bf16[2,8,4864]{2,1,0:T(8,128)(2,1)S(1)}, bf16[2,8,4864]{2,1,0:T(8,128)(2,1)S(1)}, u32[]{:S(2)}, u32[]{:S(2)}) collective-permute-start(bf16[2,8,4864]{2,1,0:T(8,128)(2,1)S(1)} %slice.138), channel_id=1, source_target_pairs={{0,66},{1,3},{2,64},{3,1},{4,70},{5,7},{6,68},{7,5},{8,74},{9,11},... | collective-permute-start | bytes 466952 | tf_op jit(solution)/shard_map/ppermute | solution.py:41
  137.6 4.1 %collective-permute-done.26 = bf16[2,8,4864]{2,1,0:T(8,128)(2,1)S(1)} collective-permute-done((bf16[2,8,4864]{2,1,0:T(8,128)(2,1)S(1)}, bf16[2,8,4864]{2,1,0:T(8,128)(2,1)S(1)}, u32[]{:S(2)}, u32[]{:S(2)}) %collective-permute-start.26) | collective-permute-done | bytes 155680 | tf_op jit(solution)/shard_map/ppermute | solution.py:41
  142.5 3.7 %collective-permute-done.27 = bf16[1,8,4864]{2,1,0:T(8,128)(2,1)S(1)} collective-permute-done((bf16[1,8,4864]{2,1,0:T(8,128)(2,1)S(1)}, bf16[1,8,4864]{2,1,0:T(8,128)(2,1)S(1)}, u32[]{:S(2)}, u32[]{:S(2)}) %collective-permute-start.27) | collective-permute-done | bytes 77856 | tf_op jit(solution)/shard_map/ppermute | solution.py:41
  146.5 2.2 %fusion.14 = f32[8,576]{1,0:T(8,128)S(1)} fusion(bf16[7168,576]{0,1:T(8,128)(2,1)S(1)} %bitcast.40, bf16[8,7168]{1,0:T(8,128)(2,1)S(1)} %get-tuple-element.41, f32[8]{0:T(128)S(1)} %add_rsqrt_fusion.1), kind=kOutput, calls=%fused_computation.47 | convolution fusion | flops 66232320 | bytes 8390688 | tf_op jit(solution)/shard_map/dot_general | solution.py:117
  149.4 2.2 %add_convert_fusion = bf16[8,128,512]{2,1,0:T(8,128)(2,1)} fusion(bf16[8,384,576]{1,2,0:T(8,128)(2,1)S(1)} %copy-done.10, f32[8,512]{1,0:T(8,128)S(1)} %get-tuple-element.38, f32[8,128]{1,0:T(8,128)S(1)} %get-tuple-element.51, f32[8,128]{1,0:T(8,128)S(1)} %get-tuple-element.50, f32[8,128,384]{2,1,0:T(8,128)S(1)} %get-tuple-element.53, ...), kind=kOutput, calls=%fused_computation.5 | convolution fusion | flops 405929984 | bytes 5798912 | tf_op jit(solution)/shard_map/rhj,rjc->rhc/dot_general | solution.py:109
  (118 shorter events, 24.7 us)
Async XLA Ops:
  0.6 119.8 %copy-start = (bf16[8,128,576]{1,2,0:T(8,128)(2,1)S(1)}, bf16[8,128,576]{1,2,0:T(8,128)(2,1)}, u32[]{:S(2)}) copy-start(bf16[8,128,576]{1,2,0:T(8,128)(2,1)} %param.19) | copy-start | bytes 3538948
  0.7 16.6 %collective-permute-start.4 = (bf16[1,7168,256]{2,1,0:T(8,128)(2,1)}, bf16[1,7168,256]{2,1,0:T(8,128)(2,1)}, u32[]{:S(2)}, u32[]{:S(2)}) collective-permute-start(bf16[1,7168,256]{2,1,0:T(8,128)(2,1)} %s1_.3), channel_id=1, source_target_pairs={{0,1},{1,0},{2,3},{3,2},{4,5},{5,4},{6,7},{7,6},{8,9},{9,8},{10,11... | collective-permute-start | bytes 11010056 | tf_op jit(solution)/shard_map/ppermute | solution.py:45
  0.8 16.6 %collective-permute-start.5 = (bf16[1,7168,256]{2,1,0:T(8,128)(2,1)}, bf16[1,7168,256]{2,1,0:T(8,128)(2,1)}, u32[]{:S(2)}, u32[]{:S(2)}) collective-permute-start(bf16[1,7168,256]{2,1,0:T(8,128)(2,1)} %s2_.3), channel_id=1, source_target_pairs={{0,1},{1,0},{2,3},{3,2},{4,5},{5,4},{6,7},{7,6},{8,9},{9,8},{10,11... | collective-permute-start | bytes 11010056 | tf_op jit(solution)/shard_map/ppermute | solution.py:45
  1.3 33.5 %collective-permute-start.9 = (bf16[1,256,7168]{2,1,0:T(8,128)(2,1)}, bf16[1,256,7168]{2,1,0:T(8,128)(2,1)}, u32[]{:S(2)}, u32[]{:S(2)}) collective-permute-start(bf16[1,256,7168]{2,1,0:T(8,128)(2,1)} %own_low.3), channel_id=1, source_target_pairs={{0,1},{1,0},{2,3},{3,2},{4,5},{5,4},{6,7},{7,6},{8,9},{9,8},{10,11... | collective-permute-start | bytes 11010056 | tf_op jit(solution)/shard_map/ppermute | solution.py:45
  3.9 4.4 %collective-permute-start = (bf16[1,8,4864]{2,1,0:T(8,128)(2,1)S(1)}, bf16[1,8,4864]{2,1,0:T(8,128)(2,1)S(1)}, u32[]{:S(2)}, u32[]{:S(2)}) collective-permute-start(bf16[1,8,4864]{2,1,0:T(8,128)(2,1)S(1)} %bitcast.33), channel_id=1, source_target_pairs={{0,2},{1,67},{2,0},{3,65},{4,6},{5,71},{6,4},{7,69},{8,10},{9,75},... | collective-permute-start | bytes 233480 | tf_op jit(solution)/shard_map/ppermute | solution.py:41
  5.6 5.9 %collective-permute-start.2 = (bf16[1,8,2432]{2,1,0:T(8,128)(2,1)S(1)}, bf16[1,8,2432]{2,1,0:T(8,128)(2,1)S(1)}, u32[]{:S(2)}, u32[]{:S(2)}) collective-permute-start(bf16[1,8,2432]{2,1,0:T(8,128)(2,1)S(1)} %bitcast.36), channel_id=1, source_target_pairs={{0,4},{1,17},{2,6},{3,19},{4,0},{5,21},{6,2},{7,23},{8,12},{9,25},... | collective-permute-start | bytes 116744 | tf_op jit(solution)/shard_map/ppermute | solution.py:41
  8.4 8.9 %collective-permute-start.1 = (bf16[2,8,4864]{2,1,0:T(8,128)(2,1)S(1)}, bf16[2,8,4864]{2,1,0:T(8,128)(2,1)S(1)}, u32[]{:S(2)}, u32[]{:S(2)}) collective-permute-start(bf16[2,8,4864]{2,1,0:T(8,128)(2,1)S(1)} %pad_maximum_fusion.4), channel_id=1, source_target_pairs={{0,66},{1,3},{2,64},{3,1},{4,70},{5,7},{6,68},{7,5},{8,74},{9,11},... | collective-permute-start | bytes 466952 | tf_op jit(solution)/shard_map/ppermute | solution.py:41
  11.6 5.7 %collective-permute-start.3 = (bf16[2,8,2432]{2,1,0:T(8,128)(2,1)S(1)}, bf16[2,8,2432]{2,1,0:T(8,128)(2,1)S(1)}, u32[]{:S(2)}, u32[]{:S(2)}) collective-permute-start(bf16[2,8,2432]{2,1,0:T(8,128)(2,1)S(1)} %pad_maximum_fusion.5), channel_id=1, source_target_pairs={{0,12},{1,49},{2,14},{3,51},{4,8},{5,53},{6,10},{7,55},{8,4},{9,57... | collective-permute-start | bytes 233480 | tf_op jit(solution)/shard_map/ppermute | solution.py:41
  17.3 8.6 %collective-permute-start.6 = (bf16[4,8,7296]{2,1,0:T(8,128)(2,1)S(1)}, bf16[4,8,7296]{2,1,0:T(8,128)(2,1)S(1)}, u32[]{:S(2)}, u32[]{:S(2)}) collective-permute-start(bf16[4,8,7296]{2,1,0:T(8,128)(2,1)S(1)} %maximum_maximum_fusion), channel_id=1, source_target_pairs={{0,16},{1,5},{2,18},{3,7},{4,20},{5,1},{6,22},{7,3},{8,24},{9,13},... | collective-permute-start | bytes 1400840 | tf_op jit(solution)/shard_map/ppermute | solution.py:41
  19.3 13.6 %collective-permute-start.7 = (bf16[4,8,7296]{2,1,0:T(8,128)(2,1)S(1)}, bf16[4,8,7296]{2,1,0:T(8,128)(2,1)S(1)}, u32[]{:S(2)}, u32[]{:S(2)}) collective-permute-start(bf16[4,8,7296]{2,1,0:T(8,128)(2,1)S(1)} %maximum_maximum_fusion), channel_id=1, source_target_pairs={{0,48},{1,13},{2,50},{3,15},{4,52},{5,9},{6,54},{7,11},{8,56},{9,5... | collective-permute-start | bytes 1400840 | tf_op jit(solution)/shard_map/ppermute | solution.py:41
  21.9 12.6 %collective-permute-start.8 = (bf16[4,8,7296]{2,1,0:T(8,128)(2,1)S(1)}, bf16[4,8,7296]{2,1,0:T(8,128)(2,1)S(1)}, u32[]{:S(2)}, u32[]{:S(2)}) collective-permute-start(bf16[4,8,7296]{2,1,0:T(8,128)(2,1)S(1)} %maximum_maximum_fusion), channel_id=1, source_target_pairs={{0,32},{1,9},{2,34},{3,11},{4,36},{5,13},{6,38},{7,15},{8,40},{9,1... | collective-permute-start | bytes 1400840 | tf_op jit(solution)/shard_map/ppermute | solution.py:41
  34.9 10.6 %collective-permute-start.14 = (bf16[128,2432]{1,0:T(8,128)(2,1)S(1)}, bf16[128,2432]{1,0:T(8,128)(2,1)S(1)}, u32[]{:S(2)}, u32[]{:S(2)}) collective-permute-start(bf16[128,2432]{1,0:T(8,128)(2,1)S(1)} %bitcast.41), channel_id=1, source_target_pairs={{0,2},{1,67},{2,0},{3,65},{4,6},{5,71},{6,4},{7,69},{8,10},{9,75},... | collective-permute-start | bytes 1867784 | tf_op jit(solution)/shard_map/ppermute | solution.py:41
  35.2 11.4 %collective-permute-start.12 = (bf16[128,2432]{1,0:T(8,128)(2,1)S(1)}, bf16[128,2432]{1,0:T(8,128)(2,1)S(1)}, u32[]{:S(2)}, u32[]{:S(2)}) collective-permute-start(bf16[128,2432]{1,0:T(8,128)(2,1)S(1)} %bitcast.46), channel_id=1, source_target_pairs={{0,12},{1,49},{2,14},{3,51},{4,8},{5,53},{6,10},{7,55},{8,4},{9,57... | collective-permute-start | bytes 1867784 | tf_op jit(solution)/shard_map/ppermute | solution.py:41
  37.9 11.4 %collective-permute-start.10 = (bf16[128,2432]{1,0:T(8,128)(2,1)S(1)}, bf16[128,2432]{1,0:T(8,128)(2,1)S(1)}, u32[]{:S(2)}, u32[]{:S(2)}) collective-permute-start(bf16[128,2432]{1,0:T(8,128)(2,1)S(1)} %bitcast.44), channel_id=1, source_target_pairs={{0,4},{1,17},{2,6},{3,19},{4,0},{5,21},{6,2},{7,23},{8,12},{9,25},... | collective-permute-start | bytes 1867784 | tf_op jit(solution)/shard_map/ppermute | solution.py:41
  45.6 19.9 %collective-permute-start.15 = (bf16[256,2432]{1,0:T(8,128)(2,1)S(1)}, bf16[256,2432]{1,0:T(8,128)(2,1)}, u32[]{:S(2)}, u32[]{:S(2)}) collective-permute-start(bf16[256,2432]{1,0:T(8,128)(2,1)S(1)} %pad_maximum_fusion.1.x3), channel_id=1, source_target_pairs={{0,66},{1,3},{2,64},{3,1},{4,70},{5,7},{6,68},{7,5},{8,74},{9,11},... | collective-permute-start | bytes 3735560 | tf_op jit(solution)/shard_map/ppermute | solution.py:41
  47.8 17.9 %collective-permute-start.13 = (bf16[256,2432]{1,0:T(8,128)(2,1)}, bf16[256,2432]{1,0:T(8,128)(2,1)}, u32[]{:S(2)}, u32[]{:S(2)}) collective-permute-start(bf16[256,2432]{1,0:T(8,128)(2,1)} %pad_maximum_fusion.3.x2), channel_id=1, source_target_pairs={{0,4},{1,17},{2,6},{3,19},{4,0},{5,21},{6,2},{7,23},{8,12},{9,25},... | collective-permute-start | bytes 3735560 | tf_op jit(solution)/shard_map/ppermute | solution.py:41
  50.4 18.4 %collective-permute-start.11 = (bf16[256,2432]{1,0:T(8,128)(2,1)}, bf16[256,2432]{1,0:T(8,128)(2,1)}, u32[]{:S(2)}, u32[]{:S(2)}) collective-permute-start(bf16[256,2432]{1,0:T(8,128)(2,1)} %pad_maximum_fusion.2.x1), channel_id=1, source_target_pairs={{0,12},{1,49},{2,14},{3,51},{4,8},{5,53},{6,10},{7,55},{8,4},{9,57... | collective-permute-start | bytes 3735560 | tf_op jit(solution)/shard_map/ppermute | solution.py:41
  81.1 19.8 %collective-permute-start.20 = (bf16[256,2304]{1,0:T(8,128)(2,1)S(1)}, bf16[256,2304]{1,0:T(8,128)(2,1)S(1)}, u32[]{:S(2)}, u32[]{:S(2)}) collective-permute-start(bf16[256,2304]{1,0:T(8,128)(2,1)S(1)} %get-tuple-element.37), channel_id=1, source_target_pairs={{0,66},{1,3},{2,64},{3,1},{4,70},{5,7},{6,68},{7,5},{8,74},{9,11},... | collective-permute-start | bytes 3538952 | tf_op jit(solution)/shard_map/ppermute | solution.py:41
  82.8 18.5 %collective-permute-start.16 = (bf16[256,2432]{1,0:T(8,128)(2,1)S(1)}, bf16[256,2432]{1,0:T(8,128)(2,1)S(1)}, u32[]{:S(2)}, u32[]{:S(2)}) collective-permute-start(bf16[256,2432]{1,0:T(8,128)(2,1)S(1)} %get-tuple-element.33), channel_id=1, source_target_pairs={{0,12},{1,49},{2,14},{3,51},{4,8},{5,53},{6,10},{7,55},{8,4},{9,57... | collective-permute-start | bytes 3735560 | tf_op jit(solution)/shard_map/ppermute | solution.py:41
  85.5 17.1 %collective-permute-start.18 = (bf16[256,2432]{1,0:T(8,128)(2,1)S(1)}, bf16[256,2432]{1,0:T(8,128)(2,1)S(1)}, u32[]{:S(2)}, u32[]{:S(2)}) collective-permute-start(bf16[256,2432]{1,0:T(8,128)(2,1)S(1)} %get-tuple-element.35), channel_id=1, source_target_pairs={{0,4},{1,17},{2,6},{3,19},{4,0},{5,21},{6,2},{7,23},{8,12},{9,25},... | collective-permute-start | bytes 3735560 | tf_op jit(solution)/shard_map/ppermute | solution.py:41
  101.2 10.0 %collective-permute-start.21 = (bf16[128,2304]{1,0:T(8,128)(2,1)S(1)}, bf16[128,2304]{1,0:T(8,128)(2,1)S(1)}, u32[]{:S(2)}, u32[]{:S(2)}) collective-permute-start(bf16[128,2304]{1,0:T(8,128)(2,1)S(1)} %slice.194), channel_id=1, source_target_pairs={{0,2},{1,67},{2,0},{3,65},{4,6},{5,71},{6,4},{7,69},{8,10},{9,75},... | collective-permute-start | bytes 1769480 | tf_op jit(solution)/shard_map/ppermute | solution.py:41
  101.6 10.3 %collective-permute-start.17 = (bf16[128,2432]{1,0:T(8,128)(2,1)S(1)}, bf16[128,2432]{1,0:T(8,128)(2,1)S(1)}, u32[]{:S(2)}, u32[]{:S(2)}) collective-permute-start(bf16[128,2432]{1,0:T(8,128)(2,1)S(1)} %slice.193), channel_id=1, source_target_pairs={{0,4},{1,17},{2,6},{3,19},{4,0},{5,21},{6,2},{7,23},{8,12},{9,25},... | collective-permute-start | bytes 1867784 | tf_op jit(solution)/shard_map/ppermute | solution.py:41
  102.9 11.5 %collective-permute-start.19 = (bf16[128,2432]{1,0:T(8,128)(2,1)S(1)}, bf16[128,2432]{1,0:T(8,128)(2,1)S(1)}, u32[]{:S(2)}, u32[]{:S(2)}) collective-permute-start(bf16[128,2432]{1,0:T(8,128)(2,1)S(1)} %slice.192), channel_id=1, source_target_pairs={{0,12},{1,49},{2,14},{3,51},{4,8},{5,53},{6,10},{7,55},{8,4},{9,57... | collective-permute-start | bytes 1867784 | tf_op jit(solution)/shard_map/ppermute | solution.py:41
  112.1 2.5 %collective-permute-start.22 = (bf16[8,128]{1,0:T(8,128)(2,1)S(1)}, bf16[8,128]{1,0:T(8,128)(2,1)S(1)}, u32[]{:S(2)}, u32[]{:S(2)}) collective-permute-start(bf16[8,128]{1,0:T(8,128)(2,1)S(1)} %slice.132), channel_id=1, source_target_pairs={{0,1},{1,0},{2,3},{3,2},{4,5},{5,4},{6,7},{7,6},{8,9},{9,8},{10,11... | collective-permute-start | bytes 6152 | tf_op jit(solution)/shard_map/ppermute | solution.py:45
  116.1 30.3 %slice-start = ((s8[8257536]{0:T(1024)(128)(4,1)}), s8[4194304]{0:T(1024)(128)(4,1)S(1)}, s32[]{:S(2)}) async-start(s8[8257536]{0:T(1024)(128)(4,1)} %bitcast.39), calls=%async_computation | async-start | bytes 8388608
  116.3 8.6 %collective-permute-start.23 = (bf16[4,8,7168]{2,1,0:T(8,128)(2,1)S(1)}, bf16[4,8,7168]{2,1,0:T(8,128)(2,1)S(1)}, u32[]{:S(2)}, u32[]{:S(2)}) collective-permute-start(bf16[4,8,7168]{2,1,0:T(8,128)(2,1)S(1)} %get-tuple-element.45), channel_id=1, source_target_pairs={{0,16},{1,5},{2,18},{3,7},{4,20},{5,1},{6,22},{7,3},{8,24},{9,13},... | collective-permute-start | bytes 1376264 | tf_op jit(solution)/shard_map/ppermute | solution.py:41
  116.3 13.8 %collective-permute-start.24 = (bf16[4,8,7168]{2,1,0:T(8,128)(2,1)S(1)}, bf16[4,8,7168]{2,1,0:T(8,128)(2,1)S(1)}, u32[]{:S(2)}, u32[]{:S(2)}) collective-permute-start(bf16[4,8,7168]{2,1,0:T(8,128)(2,1)S(1)} %get-tuple-element.47), channel_id=1, source_target_pairs={{0,48},{1,13},{2,50},{3,15},{4,52},{5,9},{6,54},{7,11},{8,56},{9,5... | collective-permute-start | bytes 1376264 | tf_op jit(solution)/shard_map/ppermute | solution.py:41
  119.2 11.8 %collective-permute-start.25 = (bf16[4,8,7168]{2,1,0:T(8,128)(2,1)S(1)}, bf16[4,8,7168]{2,1,0:T(8,128)(2,1)S(1)}, u32[]{:S(2)}, u32[]{:S(2)}) collective-permute-start(bf16[4,8,7168]{2,1,0:T(8,128)(2,1)S(1)} %get-tuple-element.46), channel_id=1, source_target_pairs={{0,32},{1,9},{2,34},{3,11},{4,36},{5,13},{6,38},{7,15},{8,40},{9,1... | collective-permute-start | bytes 1376264 | tf_op jit(solution)/shard_map/ppermute | solution.py:41
  131.3 6.1 %collective-permute-start.28 = (bf16[2,8,2304]{2,1,0:T(8,128)(2,1)S(1)}, bf16[2,8,2304]{2,1,0:T(8,128)(2,1)S(1)}, u32[]{:S(2)}, u32[]{:S(2)}) collective-permute-start(bf16[2,8,2304]{2,1,0:T(8,128)(2,1)S(1)} %slice.142), channel_id=1, source_target_pairs={{0,12},{1,49},{2,14},{3,51},{4,8},{5,53},{6,10},{7,55},{8,4},{9,57... | collective-permute-start | bytes 221192 | tf_op jit(solution)/shard_map/ppermute | solution.py:41
  134.3 7.4 %collective-permute-start.26 = (bf16[2,8,4864]{2,1,0:T(8,128)(2,1)S(1)}, bf16[2,8,4864]{2,1,0:T(8,128)(2,1)S(1)}, u32[]{:S(2)}, u32[]{:S(2)}) collective-permute-start(bf16[2,8,4864]{2,1,0:T(8,128)(2,1)S(1)} %slice.138), channel_id=1, source_target_pairs={{0,66},{1,3},{2,64},{3,1},{4,70},{5,7},{6,68},{7,5},{8,74},{9,11},... | collective-permute-start | bytes 466952 | tf_op jit(solution)/shard_map/ppermute | solution.py:41
  137.5 5.0 %collective-permute-start.29 = (bf16[1,8,2304]{2,1,0:T(8,128)(2,1)S(1)}, bf16[1,8,2304]{2,1,0:T(8,128)(2,1)S(1)}, u32[]{:S(2)}, u32[]{:S(2)}) collective-permute-start(bf16[1,8,2304]{2,1,0:T(8,128)(2,1)S(1)} %slice.196), channel_id=1, source_target_pairs={{0,4},{1,17},{2,6},{3,19},{4,0},{5,21},{6,2},{7,23},{8,12},{9,25},... | collective-permute-start | bytes 110600 | tf_op jit(solution)/shard_map/ppermute | solution.py:41
  141.7 4.5 %collective-permute-start.27 = (bf16[1,8,4864]{2,1,0:T(8,128)(2,1)S(1)}, bf16[1,8,4864]{2,1,0:T(8,128)(2,1)S(1)}, u32[]{:S(2)}, u32[]{:S(2)}) collective-permute-start(bf16[1,8,4864]{2,1,0:T(8,128)(2,1)S(1)} %slice.195), channel_id=1, source_target_pairs={{0,2},{1,67},{2,0},{3,65},{4,6},{5,71},{6,4},{7,69},{8,10},{9,75},... | collective-permute-start | bytes 233480 | tf_op jit(solution)/shard_map/ppermute | solution.py:41
  (15 other events, 134.3 us)

commit v6 on v5

--- a/solution.py
+++ b/solution.py
@@ -51,7 +51,10 @@
 
 
 def gather_pairs(values, axis, order):
-    own = jnp.concatenate([values, flip(values, axis, order[0])], axis=0)
+    count = values.shape[0]
+    room = jnp.pad(values, [(0, count)] + [(0, 0)] * (values.ndim - 1))
+    room = lax.optimization_barrier(room)
+    own = lax.dynamic_update_slice_in_dim(room, flip(values, axis, order[0]), count, 0)
     return own, flip(own, axis, order[1])
 
 
@@ -368,7 +371,9 @@
     mixture = jnp.concatenate([first[0], second[0]], axis=1)
     layer_out = (hidden.astype(f32) + mixture).astype(bf)
 
-    highest, total, summed = attend_cache(lengths, latent_cache, queries)
+    highest, total, summed = lax.optimization_barrier(
+        attend_cache(lengths, latent_cache, queries)
+    )
     attention = attend_own(layer_out, w_latent, lengths, queries, highest, total, summed)
     return (layer_out, attention)
 

time: 152 us -> 151 us (level)
  starting transfers between devices: 42.4 us -> 36.2 us
  local copies, waits for them, and re-layouts: 7.03 us -> 11.7 us
  waiting for transfers between devices: 62.6 us -> 64.5 us
    ppermute x26, starting transfers between devices: 41.6 us -> 35.4 us  [flip(): return lax.ppermute(values, AXES, partners(AXIS[axis], flips))]
    pad x0 -> x5, local copies, waits for them, and re-layouts: none -> 2.4 us  [gather_pairs(): room = jnp.pad(values, [(0, count)] + [(0, 0)] * (values.ndim - 1))]
    concatenate x6 -> x0, other arithmetic: 2.4 us -> none  [gather_pairs(): own = jnp.concatenate([values, flip(values, axis, order[0])], axis=0)]
    ppermute x26, waiting for transfers between devices: 62.6 us -> 64.5 us  [flip(): return lax.ppermute(values, AXES, partners(AXIS[axis], flips))]
    dynamic_update_slice x0 -> x5, local copies, waits for them, and re-layouts: none -> 1.84 us  [gather_pairs(): lax.dynamic_update_slice_in_dim(room, flip(values, axis, order[0]), count...]
    unnamed x35 -> x27, local copies, waits for them, and re-layouts: 6.02 us -> 6.41 us
  transfers between devices with their start and end apart: 30 -> 30, of which waited for: 18 -> 20; matrix products, arithmetic and copies ran while one was open for 5% -> 7% of each run, Pallas kernels for 9% -> 9%
where the time goes in v6:
time: 151 us; the launch traced here: 150 us
  waiting for transfers between devices  64.5 us (43%)
  starting transfers between devices  36.2 us (24%)
  Pallas kernels  26.2 us (17%)
  local copies, waits for them, and re-layouts  11.7 us (8%)
  other arithmetic  4.82 us (3%)
  matrix products  4.78 us (3%)
  between operations  1.77 us (1%)
    ppermute x26, waiting for transfers between devices, flip(): return lax.ppermute(values, AXES, partners(AXIS[axis], flips))  64.5 us
    ppermute x26, starting transfers between devices, flip(): return lax.ppermute(values, AXES, partners(AXIS[axis], flips))  35.4 us
    pallas_call x4, Pallas kernels, call(): pl.pallas_call(kernel, in_specs=[vmem] * (len(args) - in_hbm) + [hbm] * i...  26.2 us
    unnamed x27, local copies, waits for them, and re-layouts  6.41 us
  transfers between devices with their start and end apart: 30, of which 20 were waited for; matrix products, arithmetic and copies ran while one was open for 7% of the time, Pallas kernels for 9%

profile of v6, /device:TPU:0, one launch (start us, length us, event | category | flops | bytes accessed | tf_op | source)
XLA Modules:
  0.0 149.9 jit_solution(14682843983074432527)
XLA Ops:
  1.4 1.9 %copy.12.router = bf16[7168,32]{1,0:T(8,128)(2,1)S(1)} copy(bf16[7168,32]{0,1:T(8,128)(2,1)} %param.11) | data formatting | bytes 917504 | tf_op args[1]
  3.9 1.7 %collective-permute-start = (bf16[1,8,4864]{2,1,0:T(8,128)(2,1)S(1)}, bf16[1,8,4864]{2,1,0:T(8,128)(2,1)S(1)}, u32[]{:S(2)}, u32[]{:S(2)}) collective-permute-start(bf16[1,8,4864]{2,1,0:T(8,128)(2,1)S(1)} %bitcast.33), channel_id=1, source_target_pairs={{0,2},{1,67},{2,0},{3,65},{4,6},{5,71},{6,4},{7,69},{8,10},{9,75},... | collective-permute-start | bytes 233480 | tf_op jit(solution)/shard_map/ppermute | solution.py:41
  5.6 1.5 collective-permute-start.2
  8.4 3.1 %collective-permute-start.1 = (bf16[2,8,4864]{2,1,0:T(8,128)(2,1)S(1)}, bf16[2,8,4864]{2,1,0:T(8,128)(2,1)S(1)}, u32[]{:S(2)}, u32[]{:S(2)}) collective-permute-start(bf16[2,8,4864]{2,1,0:T(8,128)(2,1)S(1)} %constant_dynamic-update-slice_fusion.4), channel_id=1, source_target_pairs={{0,66},{1,3},{2,64},{3,1},{4,70},{5,7},{6,68},{7,5},{8,74},{9,11},... | collective-permute-start | bytes 466952 | tf_op jit(solution)/shard_map/ppermute | solution.py:41
  11.5 2.8 %collective-permute-start.3 = (bf16[2,8,2432]{2,1,0:T(8,128)(2,1)S(1)}, bf16[2,8,2432]{2,1,0:T(8,128)(2,1)S(1)}, u32[]{:S(2)}, u32[]{:S(2)}) collective-permute-start(bf16[2,8,2432]{2,1,0:T(8,128)(2,1)S(1)} %constant_dynamic-update-slice_fusion.3), channel_id=1, source_target_pairs={{0,12},{1,49},{2,14},{3,51},{4,8},{5,53},{6,10},{7,55},{8,4},{9,57... | collective-permute-start | bytes 233480 | tf_op jit(solution)/shard_map/ppermute | solution.py:41
  14.3 2.8 %collective-permute-done.3 = bf16[2,8,2432]{2,1,0:T(8,128)(2,1)S(1)} collective-permute-done((bf16[2,8,2432]{2,1,0:T(8,128)(2,1)S(1)}, bf16[2,8,2432]{2,1,0:T(8,128)(2,1)S(1)}, u32[]{:S(2)}, u32[]{:S(2)}) %collective-permute-start.3) | collective-permute-done | bytes 77856 | tf_op jit(solution)/shard_map/ppermute | solution.py:41
  17.2 2.0 %collective-permute-start.6 = (bf16[4,8,7296]{2,1,0:T(8,128)(2,1)S(1)}, bf16[4,8,7296]{2,1,0:T(8,128)(2,1)S(1)}, u32[]{:S(2)}, u32[]{:S(2)}) collective-permute-start(bf16[4,8,7296]{2,1,0:T(8,128)(2,1)S(1)} %maximum_maximum_fusion), channel_id=1, source_target_pairs={{0,16},{1,5},{2,18},{3,7},{4,20},{5,1},{6,22},{7,3},{8,24},{9,13},... | collective-permute-start | bytes 1400840 | tf_op jit(solution)/shard_map/ppermute | solution.py:41
  19.2 2.5 %collective-permute-start.7 = (bf16[4,8,7296]{2,1,0:T(8,128)(2,1)S(1)}, bf16[4,8,7296]{2,1,0:T(8,128)(2,1)S(1)}, u32[]{:S(2)}, u32[]{:S(2)}) collective-permute-start(bf16[4,8,7296]{2,1,0:T(8,128)(2,1)S(1)} %maximum_maximum_fusion), channel_id=1, source_target_pairs={{0,48},{1,13},{2,50},{3,15},{4,52},{5,9},{6,54},{7,11},{8,56},{9,5... | collective-permute-start | bytes 1400840 | tf_op jit(solution)/shard_map/ppermute | solution.py:41
  22.8 3.1 %collective-permute-done.6 = bf16[4,8,7296]{2,1,0:T(8,128)(2,1)S(1)} collective-permute-done((bf16[4,8,7296]{2,1,0:T(8,128)(2,1)S(1)}, bf16[4,8,7296]{2,1,0:T(8,128)(2,1)S(1)}, u32[]{:S(2)}, u32[]{:S(2)}) %collective-permute-start.6) | collective-permute-done | bytes 466976 | tf_op jit(solution)/shard_map/ppermute | solution.py:41
  25.9 7.0 %collective-permute-done.7 = bf16[4,8,7296]{2,1,0:T(8,128)(2,1)S(1)} collective-permute-done((bf16[4,8,7296]{2,1,0:T(8,128)(2,1)S(1)}, bf16[4,8,7296]{2,1,0:T(8,128)(2,1)S(1)}, u32[]{:S(2)}, u32[]{:S(2)}) %collective-permute-start.7) | collective-permute-done | bytes 466976 | tf_op jit(solution)/shard_map/ppermute | solution.py:41
  32.8 1.5 %collective-permute-done.8 = bf16[4,8,7296]{2,1,0:T(8,128)(2,1)S(1)} collective-permute-done((bf16[4,8,7296]{2,1,0:T(8,128)(2,1)S(1)}, bf16[4,8,7296]{2,1,0:T(8,128)(2,1)S(1)}, u32[]{:S(2)}, u32[]{:S(2)}) %collective-permute-start.8) | collective-permute-done | bytes 466976 | tf_op jit(solution)/shard_map/ppermute | solution.py:41
  35.0 2.8 %collective-permute-start.12 = (bf16[128,2432]{1,0:T(8,128)(2,1)S(1)}, bf16[128,2432]{1,0:T(8,128)(2,1)S(1)}, u32[]{:S(2)}, u32[]{:S(2)}) collective-permute-start(bf16[128,2432]{1,0:T(8,128)(2,1)S(1)} %bitcast.41), channel_id=1, source_target_pairs={{0,12},{1,49},{2,14},{3,51},{4,8},{5,53},{6,10},{7,55},{8,4},{9,57... | collective-permute-start | bytes 1867784 | tf_op jit(solution)/shard_map/ppermute | solution.py:41
  40.2 5.3 %collective-permute-done.14 = bf16[128,2432]{1,0:T(8,128)(2,1)S(1)} collective-permute-done((bf16[128,2432]{1,0:T(8,128)(2,1)S(1)}, bf16[128,2432]{1,0:T(8,128)(2,1)S(1)}, u32[]{:S(2)}, u32[]{:S(2)}) %collective-permute-start.14) | collective-permute-done | bytes 622624 | tf_op jit(solution)/shard_map/ppermute | solution.py:41
  47.3 1.6 %collective-permute-start.13 = (bf16[256,2432]{1,0:T(8,128)(2,1)}, bf16[256,2432]{1,0:T(8,128)(2,1)}, u32[]{:S(2)}, u32[]{:S(2)}) collective-permute-start(bf16[256,2432]{1,0:T(8,128)(2,1)} %constant_dynamic-update-slice_fusion.1.x2), channel_id=1, source_target_pairs={{0,4},{1,17},{2,6},{3,19},{4,0},{5,21},{6,2},{7,23},{8,12},{9,25},... | collective-permute-start | bytes 3735560 | tf_op jit(solution)/shard_map/ppermute | solution.py:41
  48.9 1.5 %collective-permute-done.10 = bf16[128,2432]{1,0:T(8,128)(2,1)S(1)} collective-permute-done((bf16[128,2432]{1,0:T(8,128)(2,1)S(1)}, bf16[128,2432]{1,0:T(8,128)(2,1)S(1)}, u32[]{:S(2)}, u32[]{:S(2)}) %collective-permute-start.10) | collective-permute-done | bytes 622624 | tf_op jit(solution)/shard_map/ppermute | solution.py:41
  52.0 2.0 %copy-done.2 = bf16[1,7168,256]{2,1,0:T(8,128)(2,1)S(1)} copy-done((bf16[1,7168,256]{2,1,0:T(8,128)(2,1)S(1)}, bf16[1,7168,256]{2,1,0:T(8,128)(2,1)}, u32[]{:S(2)}) %copy-start.2) | copy-done | bytes 3670040
  54.0 2.0 %copy-done.4 = bf16[1,7168,256]{2,1,0:T(8,128)(2,1)S(1)} copy-done((bf16[1,7168,256]{2,1,0:T(8,128)(2,1)S(1)}, bf16[1,7168,256]{2,1,0:T(8,128)(2,1)}, u32[]{:S(2)}) %copy-start.4) | copy-done | bytes 3670040
  56.1 8.9 %shard_map.114 = (f32[256,1024]{1,0:T(8,128)S(1)}, f32[256,1024]{1,0:T(8,128)S(1)}, f32[256,1024]{1,0:T(8,128)S(1)}) custom-call(bf16[256,2432]{1,0:T(8,128)(2,1)} %constant_dynamic-update-slice_fusion.2.x1, bf16[256,2432]{1,0:T(8,128)(2,1)} %constant_dynamic-update-slice_fusion.1.x2, bf16[256,2432]{1,0:T(8,128)(2,1)S(1)} %constant_dynamic-update-slice_fusion.x3, ...), custom_call_target="tpu_custom_call" | custom-call | tf_op jit(solution)/shard_map/pallas_call | solution.py:147
  65.0 4.8 %collective-permute-done.11.x1 = bf16[256,2432]{1,0:T(8,128)(2,1)} collective-permute-done((bf16[256,2432]{1,0:T(8,128)(2,1)}, bf16[256,2432]{1,0:T(8,128)(2,1)}, u32[]{:S(2)}, u32[]{:S(2)}) %collective-permute-start.11) | collective-permute-done | bytes 1245216 | tf_op jit(solution)/shard_map/ppermute | solution.py:41
  69.8 12.2 %shard_map.115 = (bf16[256,2432]{1,0:T(8,128)(2,1)S(1)}, bf16[256,2432]{1,0:T(8,128)(2,1)S(1)}, bf16[256,2304]{1,0:T(8,128)(2,1)S(1)}, bf16[512,512]{1,0:T(8,128)(2,1)S(1)}, bf16[512,512]{1,0:T(8,128)(2,1)S(1)}) custom-call(bf16[256,2432]{1,0:T(8,128)(2,1)} %collective-permute-done.11.x1, bf16[256,2432]{1,0:T(8,128)(2,1)} %collective-permute-done.13.x2, ...), custom_call_target="tpu_custom_call" | custom-call | tf_op jit(solution)/shard_map/pallas_call | solution.py:147
  86.9 4.4 %shard_map.116 = (bf16[256,2432]{1,0:T(8,128)(2,1)S(1)}, bf16[256,2432]{1,0:T(8,128)(2,1)S(1)}, bf16[256,2304]{1,0:T(8,128)(2,1)S(1)}) custom-call(bf16[512,512]{1,0:T(8,128)(2,1)S(1)} %get-tuple-element.33.straight, bf16[512,512]{1,0:T(8,128)(2,1)S(1)} %get-tuple-element.34.turned, bf16[1,256,7168]{2,1,0:T(8,128)(2,1)S(1)} %copy-done.1, ...), custom_call_target="tpu_custom_call" | custom-call | tf_op jit(solution)/shard_map/pallas_call | solution.py:147
  91.3 9.3 %collective-permute-done.20 = bf16[256,2304]{1,0:T(8,128)(2,1)S(1)} collective-permute-done((bf16[256,2304]{1,0:T(8,128)(2,1)S(1)}, bf16[256,2304]{1,0:T(8,128)(2,1)S(1)}, u32[]{:S(2)}, u32[]{:S(2)}) %collective-permute-start.20) | collective-permute-done | bytes 1179680 | tf_op jit(solution)/shard_map/ppermute | solution.py:41
  100.9 2.1 %collective-permute-start.21 = (bf16[128,2304]{1,0:T(8,128)(2,1)S(1)}, bf16[128,2304]{1,0:T(8,128)(2,1)S(1)}, u32[]{:S(2)}, u32[]{:S(2)}) collective-permute-start(bf16[128,2304]{1,0:T(8,128)(2,1)S(1)} %slice.185), channel_id=1, source_target_pairs={{0,2},{1,67},{2,0},{3,65},{4,6},{5,71},{6,4},{7,69},{8,10},{9,75},... | collective-permute-start | bytes 1769480 | tf_op jit(solution)/shard_map/ppermute | solution.py:41
  103.9 1.6 %collective-permute-start.19 = (bf16[128,2432]{1,0:T(8,128)(2,1)S(1)}, bf16[128,2432]{1,0:T(8,128)(2,1)S(1)}, u32[]{:S(2)}, u32[]{:S(2)}) collective-permute-start(bf16[128,2432]{1,0:T(8,128)(2,1)S(1)} %slice.183), channel_id=1, source_target_pairs={{0,12},{1,49},{2,14},{3,51},{4,8},{5,53},{6,10},{7,55},{8,4},{9,57... | collective-permute-start | bytes 1867784 | tf_op jit(solution)/shard_map/ppermute | solution.py:41
  105.5 5.3 %collective-permute-done.21 = bf16[128,2304]{1,0:T(8,128)(2,1)S(1)} collective-permute-done((bf16[128,2304]{1,0:T(8,128)(2,1)S(1)}, bf16[128,2304]{1,0:T(8,128)(2,1)S(1)}, u32[]{:S(2)}, u32[]{:S(2)}) %collective-permute-start.21) | collective-permute-done | bytes 589856 | tf_op jit(solution)/shard_map/ppermute | solution.py:41
  111.0 2.7 %collective-permute-done.17 = bf16[128,2432]{1,0:T(8,128)(2,1)S(1)} collective-permute-done((bf16[128,2432]{1,0:T(8,128)(2,1)S(1)}, bf16[128,2432]{1,0:T(8,128)(2,1)S(1)}, u32[]{:S(2)}, u32[]{:S(2)}) %collective-permute-start.17) | collective-permute-done | bytes 622624 | tf_op jit(solution)/shard_map/ppermute | solution.py:41
  118.2 3.8 %collective-permute-start.24 = (bf16[4,8,7168]{2,1,0:T(8,128)(2,1)S(1)}, bf16[4,8,7168]{2,1,0:T(8,128)(2,1)S(1)}, u32[]{:S(2)}, u32[]{:S(2)}) collective-permute-start(bf16[4,8,7168]{2,1,0:T(8,128)(2,1)S(1)} %get-tuple-element.53), channel_id=1, source_target_pairs={{0,48},{1,13},{2,50},{3,15},{4,52},{5,9},{6,54},{7,11},{8,56},{9,5... | collective-permute-start | bytes 1376264 | tf_op jit(solution)/shard_map/ppermute | solution.py:41
  125.8 7.1 %collective-permute-done.24 = bf16[4,8,7168]{2,1,0:T(8,128)(2,1)S(1)} collective-permute-done((bf16[4,8,7168]{2,1,0:T(8,128)(2,1)S(1)}, bf16[4,8,7168]{2,1,0:T(8,128)(2,1)S(1)}, u32[]{:S(2)}, u32[]{:S(2)}) %collective-permute-start.24) | collective-permute-done | bytes 458784 | tf_op jit(solution)/shard_map/ppermute | solution.py:41
  134.3 2.1 %collective-permute-start.26 = (bf16[2,8,4864]{2,1,0:T(8,128)(2,1)S(1)}, bf16[2,8,4864]{2,1,0:T(8,128)(2,1)S(1)}, u32[]{:S(2)}, u32[]{:S(2)}) collective-permute-start(bf16[2,8,4864]{2,1,0:T(8,128)(2,1)S(1)} %slice.137), channel_id=1, source_target_pairs={{0,66},{1,3},{2,64},{3,1},{4,70},{5,7},{6,68},{7,5},{8,74},{9,11},... | collective-permute-start | bytes 466952 | tf_op jit(solution)/shard_map/ppermute | solution.py:41
  136.5 3.4 %collective-permute-done.28 = bf16[2,8,2304]{2,1,0:T(8,128)(2,1)S(1)} collective-permute-done((bf16[2,8,2304]{2,1,0:T(8,128)(2,1)S(1)}, bf16[2,8,2304]{2,1,0:T(8,128)(2,1)S(1)}, u32[]{:S(2)}, u32[]{:S(2)}) %collective-permute-start.28) | collective-permute-done | bytes 73760 | tf_op jit(solution)/shard_map/ppermute | solution.py:41
  141.2 2.7 %collective-permute-done.29 = bf16[1,8,2304]{2,1,0:T(8,128)(2,1)S(1)} collective-permute-done((bf16[1,8,2304]{2,1,0:T(8,128)(2,1)S(1)}, bf16[1,8,2304]{2,1,0:T(8,128)(2,1)S(1)}, u32[]{:S(2)}, u32[]{:S(2)}) %collective-permute-start.29) | collective-permute-done | bytes 36896 | tf_op jit(solution)/shard_map/ppermute | solution.py:41
  145.6 2.2 %fusion.12 = f32[8,576]{1,0:T(8,128)S(1)} fusion(bf16[7168,576]{0,1:T(8,128)(2,1)S(1)} %bitcast.38, bf16[8,7168]{1,0:T(8,128)(2,1)S(1)} %get-tuple-element.47, f32[8]{0:T(128)S(1)} %add_rsqrt_fusion.1), kind=kOutput, calls=%fused_computation.41 | convolution fusion | flops 66232320 | bytes 8390688 | tf_op jit(solution)/shard_map/dot_general | solution.py:120
  (116 shorter events, 30.4 us)
Async XLA Ops:
  0.6 84.2 %copy-start = (bf16[8,128,576]{1,2,0:T(8,128)(2,1)S(1)}, bf16[8,128,576]{1,2,0:T(8,128)(2,1)}, u32[]{:S(2)}) copy-start(bf16[8,128,576]{1,2,0:T(8,128)(2,1)} %param.19) | copy-start | bytes 3538948
  0.7 16.5 %collective-permute-start.4 = (bf16[1,7168,256]{2,1,0:T(8,128)(2,1)}, bf16[1,7168,256]{2,1,0:T(8,128)(2,1)}, u32[]{:S(2)}, u32[]{:S(2)}) collective-permute-start(bf16[1,7168,256]{2,1,0:T(8,128)(2,1)} %s1_.3), channel_id=1, source_target_pairs={{0,1},{1,0},{2,3},{3,2},{4,5},{5,4},{6,7},{7,6},{8,9},{9,8},{10,11... | collective-permute-start | bytes 11010056 | tf_op jit(solution)/shard_map/ppermute | solution.py:45
  0.8 16.5 %collective-permute-start.5 = (bf16[1,7168,256]{2,1,0:T(8,128)(2,1)}, bf16[1,7168,256]{2,1,0:T(8,128)(2,1)}, u32[]{:S(2)}, u32[]{:S(2)}) collective-permute-start(bf16[1,7168,256]{2,1,0:T(8,128)(2,1)} %s2_.3), channel_id=1, source_target_pairs={{0,1},{1,0},{2,3},{3,2},{4,5},{5,4},{6,7},{7,6},{8,9},{9,8},{10,11... | collective-permute-start | bytes 11010056 | tf_op jit(solution)/shard_map/ppermute | solution.py:45
  1.3 33.4 %collective-permute-start.9 = (bf16[1,256,7168]{2,1,0:T(8,128)(2,1)}, bf16[1,256,7168]{2,1,0:T(8,128)(2,1)}, u32[]{:S(2)}, u32[]{:S(2)}) collective-permute-start(bf16[1,256,7168]{2,1,0:T(8,128)(2,1)} %own_low.3), channel_id=1, source_target_pairs={{0,1},{1,0},{2,3},{3,2},{4,5},{5,4},{6,7},{7,6},{8,9},{9,8},{10,11... | collective-permute-start | bytes 11010056 | tf_op jit(solution)/shard_map/ppermute | solution.py:45
  3.9 4.4 %collective-permute-start = (bf16[1,8,4864]{2,1,0:T(8,128)(2,1)S(1)}, bf16[1,8,4864]{2,1,0:T(8,128)(2,1)S(1)}, u32[]{:S(2)}, u32[]{:S(2)}) collective-permute-start(bf16[1,8,4864]{2,1,0:T(8,128)(2,1)S(1)} %bitcast.33), channel_id=1, source_target_pairs={{0,2},{1,67},{2,0},{3,65},{4,6},{5,71},{6,4},{7,69},{8,10},{9,75},... | collective-permute-start | bytes 233480 | tf_op jit(solution)/shard_map/ppermute | solution.py:41
  5.6 5.8 %collective-permute-start.2 = (bf16[1,8,2432]{2,1,0:T(8,128)(2,1)S(1)}, bf16[1,8,2432]{2,1,0:T(8,128)(2,1)S(1)}, u32[]{:S(2)}, u32[]{:S(2)}) collective-permute-start(bf16[1,8,2432]{2,1,0:T(8,128)(2,1)S(1)} %bitcast.35), channel_id=1, source_target_pairs={{0,4},{1,17},{2,6},{3,19},{4,0},{5,21},{6,2},{7,23},{8,12},{9,25},... | collective-permute-start | bytes 116744 | tf_op jit(solution)/shard_map/ppermute | solution.py:41
  8.4 8.8 %collective-permute-start.1 = (bf16[2,8,4864]{2,1,0:T(8,128)(2,1)S(1)}, bf16[2,8,4864]{2,1,0:T(8,128)(2,1)S(1)}, u32[]{:S(2)}, u32[]{:S(2)}) collective-permute-start(bf16[2,8,4864]{2,1,0:T(8,128)(2,1)S(1)} %constant_dynamic-update-slice_fusion.4), channel_id=1, source_target_pairs={{0,66},{1,3},{2,64},{3,1},{4,70},{5,7},{6,68},{7,5},{8,74},{9,11},... | collective-permute-start | bytes 466952 | tf_op jit(solution)/shard_map/ppermute | solution.py:41
  11.5 5.7 %collective-permute-start.3 = (bf16[2,8,2432]{2,1,0:T(8,128)(2,1)S(1)}, bf16[2,8,2432]{2,1,0:T(8,128)(2,1)S(1)}, u32[]{:S(2)}, u32[]{:S(2)}) collective-permute-start(bf16[2,8,2432]{2,1,0:T(8,128)(2,1)S(1)} %constant_dynamic-update-slice_fusion.3), channel_id=1, source_target_pairs={{0,12},{1,49},{2,14},{3,51},{4,8},{5,53},{6,10},{7,55},{8,4},{9,57... | collective-permute-start | bytes 233480 | tf_op jit(solution)/shard_map/ppermute | solution.py:41
  17.2 8.6 %collective-permute-start.6 = (bf16[4,8,7296]{2,1,0:T(8,128)(2,1)S(1)}, bf16[4,8,7296]{2,1,0:T(8,128)(2,1)S(1)}, u32[]{:S(2)}, u32[]{:S(2)}) collective-permute-start(bf16[4,8,7296]{2,1,0:T(8,128)(2,1)S(1)} %maximum_maximum_fusion), channel_id=1, source_target_pairs={{0,16},{1,5},{2,18},{3,7},{4,20},{5,1},{6,22},{7,3},{8,24},{9,13},... | collective-permute-start | bytes 1400840 | tf_op jit(solution)/shard_map/ppermute | solution.py:41
  19.2 13.6 %collective-permute-start.7 = (bf16[4,8,7296]{2,1,0:T(8,128)(2,1)S(1)}, bf16[4,8,7296]{2,1,0:T(8,128)(2,1)S(1)}, u32[]{:S(2)}, u32[]{:S(2)}) collective-permute-start(bf16[4,8,7296]{2,1,0:T(8,128)(2,1)S(1)} %maximum_maximum_fusion), channel_id=1, source_target_pairs={{0,48},{1,13},{2,50},{3,15},{4,52},{5,9},{6,54},{7,11},{8,56},{9,5... | collective-permute-start | bytes 1400840 | tf_op jit(solution)/shard_map/ppermute | solution.py:41
  21.8 12.6 %collective-permute-start.8 = (bf16[4,8,7296]{2,1,0:T(8,128)(2,1)S(1)}, bf16[4,8,7296]{2,1,0:T(8,128)(2,1)S(1)}, u32[]{:S(2)}, u32[]{:S(2)}) collective-permute-start(bf16[4,8,7296]{2,1,0:T(8,128)(2,1)S(1)} %maximum_maximum_fusion), channel_id=1, source_target_pairs={{0,32},{1,9},{2,34},{3,11},{4,36},{5,13},{6,38},{7,15},{8,40},{9,1... | collective-permute-start | bytes 1400840 | tf_op jit(solution)/shard_map/ppermute | solution.py:41
  34.8 10.6 %collective-permute-start.14 = (bf16[128,2432]{1,0:T(8,128)(2,1)S(1)}, bf16[128,2432]{1,0:T(8,128)(2,1)S(1)}, u32[]{:S(2)}, u32[]{:S(2)}) collective-permute-start(bf16[128,2432]{1,0:T(8,128)(2,1)S(1)} %bitcast.43), channel_id=1, source_target_pairs={{0,2},{1,67},{2,0},{3,65},{4,6},{5,71},{6,4},{7,69},{8,10},{9,75},... | collective-permute-start | bytes 1867784 | tf_op jit(solution)/shard_map/ppermute | solution.py:41
  35.0 11.4 %collective-permute-start.12 = (bf16[128,2432]{1,0:T(8,128)(2,1)S(1)}, bf16[128,2432]{1,0:T(8,128)(2,1)S(1)}, u32[]{:S(2)}, u32[]{:S(2)}) collective-permute-start(bf16[128,2432]{1,0:T(8,128)(2,1)S(1)} %bitcast.41), channel_id=1, source_target_pairs={{0,12},{1,49},{2,14},{3,51},{4,8},{5,53},{6,10},{7,55},{8,4},{9,57... | collective-permute-start | bytes 1867784 | tf_op jit(solution)/shard_map/ppermute | solution.py:41
  40.2 10.2 %collective-permute-start.10 = (bf16[128,2432]{1,0:T(8,128)(2,1)S(1)}, bf16[128,2432]{1,0:T(8,128)(2,1)S(1)}, u32[]{:S(2)}, u32[]{:S(2)}) collective-permute-start(bf16[128,2432]{1,0:T(8,128)(2,1)S(1)} %bitcast.40), channel_id=1, source_target_pairs={{0,4},{1,17},{2,6},{3,19},{4,0},{5,21},{6,2},{7,23},{8,12},{9,25},... | collective-permute-start | bytes 1867784 | tf_op jit(solution)/shard_map/ppermute | solution.py:41
  45.5 19.4 %collective-permute-start.15 = (bf16[256,2432]{1,0:T(8,128)(2,1)S(1)}, bf16[256,2432]{1,0:T(8,128)(2,1)}, u32[]{:S(2)}, u32[]{:S(2)}) collective-permute-start(bf16[256,2432]{1,0:T(8,128)(2,1)S(1)} %constant_dynamic-update-slice_fusion.x3), channel_id=1, source_target_pairs={{0,66},{1,3},{2,64},{3,1},{4,70},{5,7},{6,68},{7,5},{8,74},{9,11},... | collective-permute-start | bytes 3735560 | tf_op jit(solution)/shard_map/ppermute | solution.py:41
  47.3 17.6 %collective-permute-start.13 = (bf16[256,2432]{1,0:T(8,128)(2,1)}, bf16[256,2432]{1,0:T(8,128)(2,1)}, u32[]{:S(2)}, u32[]{:S(2)}) collective-permute-start(bf16[256,2432]{1,0:T(8,128)(2,1)} %constant_dynamic-update-slice_fusion.1.x2), channel_id=1, source_target_pairs={{0,4},{1,17},{2,6},{3,19},{4,0},{5,21},{6,2},{7,23},{8,12},{9,25},... | collective-permute-start | bytes 3735560 | tf_op jit(solution)/shard_map/ppermute | solution.py:41
  51.3 18.4 %collective-permute-start.11 = (bf16[256,2432]{1,0:T(8,128)(2,1)}, bf16[256,2432]{1,0:T(8,128)(2,1)}, u32[]{:S(2)}, u32[]{:S(2)}) collective-permute-start(bf16[256,2432]{1,0:T(8,128)(2,1)} %constant_dynamic-update-slice_fusion.2.x1), channel_id=1, source_target_pairs={{0,12},{1,49},{2,14},{3,51},{4,8},{5,53},{6,10},{7,55},{8,4},{9,57... | collective-permute-start | bytes 3735560 | tf_op jit(solution)/shard_map/ppermute | solution.py:41
  81.9 18.7 %collective-permute-start.20 = (bf16[256,2304]{1,0:T(8,128)(2,1)S(1)}, bf16[256,2304]{1,0:T(8,128)(2,1)S(1)}, u32[]{:S(2)}, u32[]{:S(2)}) collective-permute-start(bf16[256,2304]{1,0:T(8,128)(2,1)S(1)} %get-tuple-element.40), channel_id=1, source_target_pairs={{0,66},{1,3},{2,64},{3,1},{4,70},{5,7},{6,68},{7,5},{8,74},{9,11},... | collective-permute-start | bytes 3538952 | tf_op jit(solution)/shard_map/ppermute | solution.py:41
  83.4 19.6 %collective-permute-start.16 = (bf16[256,2432]{1,0:T(8,128)(2,1)S(1)}, bf16[256,2432]{1,0:T(8,128)(2,1)S(1)}, u32[]{:S(2)}, u32[]{:S(2)}) collective-permute-start(bf16[256,2432]{1,0:T(8,128)(2,1)S(1)} %get-tuple-element.36), channel_id=1, source_target_pairs={{0,12},{1,49},{2,14},{3,51},{4,8},{5,53},{6,10},{7,55},{8,4},{9,57... | collective-permute-start | bytes 3735560 | tf_op jit(solution)/shard_map/ppermute | solution.py:41
  85.9 17.5 %collective-permute-start.18 = (bf16[256,2432]{1,0:T(8,128)(2,1)S(1)}, bf16[256,2432]{1,0:T(8,128)(2,1)S(1)}, u32[]{:S(2)}, u32[]{:S(2)}) collective-permute-start(bf16[256,2432]{1,0:T(8,128)(2,1)S(1)} %get-tuple-element.38), channel_id=1, source_target_pairs={{0,4},{1,17},{2,6},{3,19},{4,0},{5,21},{6,2},{7,23},{8,12},{9,25},... | collective-permute-start | bytes 3735560 | tf_op jit(solution)/shard_map/ppermute | solution.py:41
  100.9 10.0 %collective-permute-start.21 = (bf16[128,2304]{1,0:T(8,128)(2,1)S(1)}, bf16[128,2304]{1,0:T(8,128)(2,1)S(1)}, u32[]{:S(2)}, u32[]{:S(2)}) collective-permute-start(bf16[128,2304]{1,0:T(8,128)(2,1)S(1)} %slice.185), channel_id=1, source_target_pairs={{0,2},{1,67},{2,0},{3,65},{4,6},{5,71},{6,4},{7,69},{8,10},{9,75},... | collective-permute-start | bytes 1769480 | tf_op jit(solution)/shard_map/ppermute | solution.py:41
  103.4 10.3 %collective-permute-start.17 = (bf16[128,2432]{1,0:T(8,128)(2,1)S(1)}, bf16[128,2432]{1,0:T(8,128)(2,1)S(1)}, u32[]{:S(2)}, u32[]{:S(2)}) collective-permute-start(bf16[128,2432]{1,0:T(8,128)(2,1)S(1)} %slice.184), channel_id=1, source_target_pairs={{0,4},{1,17},{2,6},{3,19},{4,0},{5,21},{6,2},{7,23},{8,12},{9,25},... | collective-permute-start | bytes 1867784 | tf_op jit(solution)/shard_map/ppermute | solution.py:41
  103.9 11.5 %collective-permute-start.19 = (bf16[128,2432]{1,0:T(8,128)(2,1)S(1)}, bf16[128,2432]{1,0:T(8,128)(2,1)S(1)}, u32[]{:S(2)}, u32[]{:S(2)}) collective-permute-start(bf16[128,2432]{1,0:T(8,128)(2,1)S(1)} %slice.183), channel_id=1, source_target_pairs={{0,12},{1,49},{2,14},{3,51},{4,8},{5,53},{6,10},{7,55},{8,4},{9,57... | collective-permute-start | bytes 1867784 | tf_op jit(solution)/shard_map/ppermute | solution.py:41
  113.9 1.7 %collective-permute-start.22 = (bf16[8,128]{1,0:T(8,128)(2,1)S(1)}, bf16[8,128]{1,0:T(8,128)(2,1)S(1)}, u32[]{:S(2)}, u32[]{:S(2)}) collective-permute-start(bf16[8,128]{1,0:T(8,128)(2,1)S(1)} %slice.131), channel_id=1, source_target_pairs={{0,1},{1,0},{2,3},{3,2},{4,5},{5,4},{6,7},{7,6},{8,9},{9,8},{10,11... | collective-permute-start | bytes 6152 | tf_op jit(solution)/shard_map/ppermute | solution.py:45
  117.1 28.5 %slice-start = ((s8[8257536]{0:T(1024)(128)(4,1)}), s8[4194304]{0:T(1024)(128)(4,1)S(1)}, s32[]{:S(2)}) async-start(s8[8257536]{0:T(1024)(128)(4,1)} %bitcast.37), calls=%async_computation | async-start | bytes 8388608
  117.2 8.6 %collective-permute-start.23 = (bf16[4,8,7168]{2,1,0:T(8,128)(2,1)S(1)}, bf16[4,8,7168]{2,1,0:T(8,128)(2,1)S(1)}, u32[]{:S(2)}, u32[]{:S(2)}) collective-permute-start(bf16[4,8,7168]{2,1,0:T(8,128)(2,1)S(1)} %get-tuple-element.51), channel_id=1, source_target_pairs={{0,16},{1,5},{2,18},{3,7},{4,20},{5,1},{6,22},{7,3},{8,24},{9,13},... | collective-permute-start | bytes 1376264 | tf_op jit(solution)/shard_map/ppermute | solution.py:41
  118.2 14.7 %collective-permute-start.24 = (bf16[4,8,7168]{2,1,0:T(8,128)(2,1)S(1)}, bf16[4,8,7168]{2,1,0:T(8,128)(2,1)S(1)}, u32[]{:S(2)}, u32[]{:S(2)}) collective-permute-start(bf16[4,8,7168]{2,1,0:T(8,128)(2,1)S(1)} %get-tuple-element.53), channel_id=1, source_target_pairs={{0,48},{1,13},{2,50},{3,15},{4,52},{5,9},{6,54},{7,11},{8,56},{9,5... | collective-permute-start | bytes 1376264 | tf_op jit(solution)/shard_map/ppermute | solution.py:41
  122.0 12.0 %collective-permute-start.25 = (bf16[4,8,7168]{2,1,0:T(8,128)(2,1)S(1)}, bf16[4,8,7168]{2,1,0:T(8,128)(2,1)S(1)}, u32[]{:S(2)}, u32[]{:S(2)}) collective-permute-start(bf16[4,8,7168]{2,1,0:T(8,128)(2,1)S(1)} %get-tuple-element.52), channel_id=1, source_target_pairs={{0,32},{1,9},{2,34},{3,11},{4,36},{5,13},{6,38},{7,15},{8,40},{9,1... | collective-permute-start | bytes 1376264 | tf_op jit(solution)/shard_map/ppermute | solution.py:41
  134.2 5.6 %collective-permute-start.28 = (bf16[2,8,2304]{2,1,0:T(8,128)(2,1)S(1)}, bf16[2,8,2304]{2,1,0:T(8,128)(2,1)S(1)}, u32[]{:S(2)}, u32[]{:S(2)}) collective-permute-start(bf16[2,8,2304]{2,1,0:T(8,128)(2,1)S(1)} %slice.141), channel_id=1, source_target_pairs={{0,12},{1,49},{2,14},{3,51},{4,8},{5,53},{6,10},{7,55},{8,4},{9,57... | collective-permute-start | bytes 221192 | tf_op jit(solution)/shard_map/ppermute | solution.py:41
  134.3 6.5 %collective-permute-start.26 = (bf16[2,8,4864]{2,1,0:T(8,128)(2,1)S(1)}, bf16[2,8,4864]{2,1,0:T(8,128)(2,1)S(1)}, u32[]{:S(2)}, u32[]{:S(2)}) collective-permute-start(bf16[2,8,4864]{2,1,0:T(8,128)(2,1)S(1)} %slice.137), channel_id=1, source_target_pairs={{0,66},{1,3},{2,64},{3,1},{4,70},{5,7},{6,68},{7,5},{8,74},{9,11},... | collective-permute-start | bytes 466952 | tf_op jit(solution)/shard_map/ppermute | solution.py:41
  139.9 4.0 %collective-permute-start.29 = (bf16[1,8,2304]{2,1,0:T(8,128)(2,1)S(1)}, bf16[1,8,2304]{2,1,0:T(8,128)(2,1)S(1)}, u32[]{:S(2)}, u32[]{:S(2)}) collective-permute-start(bf16[1,8,2304]{2,1,0:T(8,128)(2,1)S(1)} %slice.187), channel_id=1, source_target_pairs={{0,4},{1,17},{2,6},{3,19},{4,0},{5,21},{6,2},{7,23},{8,12},{9,25},... | collective-permute-start | bytes 110600 | tf_op jit(solution)/shard_map/ppermute | solution.py:41
  140.9 4.5 %collective-permute-start.27 = (bf16[1,8,4864]{2,1,0:T(8,128)(2,1)S(1)}, bf16[1,8,4864]{2,1,0:T(8,128)(2,1)S(1)}, u32[]{:S(2)}, u32[]{:S(2)}) collective-permute-start(bf16[1,8,4864]{2,1,0:T(8,128)(2,1)S(1)} %slice.186), channel_id=1, source_target_pairs={{0,2},{1,67},{2,0},{3,65},{4,6},{5,71},{6,4},{7,69},{8,10},{9,75},... | collective-permute-start | bytes 233480 | tf_op jit(solution)/shard_map/ppermute | solution.py:41
  (11 other events, 93.5 us)

commit v7 on v6

--- a/solution.py
+++ b/solution.py
@@ -366,7 +366,7 @@
     sums = [reduce_pairs(staying[i], leaving[i], *way).astype(bf) for i, way in enumerate(ways)]
     both = together(jnp.concatenate(sums, axis=1)).reshape(4, 4, rows, width)
     both = reduce([both[i] for i in range(4)], "b", SAME).astype(bf)
-    first = reduce_pairs(both[:2, :, :cut], both[2:, :, :cut], "y", SPLIT)
+    first = reduce([both[i : i + 1, :, :cut] for i in range(4)], "y", SPLIT)
     second = reduce_pairs(both[:2, :, cut:], both[2:, :, cut:], "a", SAME)
     mixture = jnp.concatenate([first[0], second[0]], axis=1)
     layer_out = (hidden.astype(f32) + mixture).astype(bf)

time: 151 us -> 149 us (0.987)
  waiting for transfers between devices: 64.5 us -> 61.6 us
  starting transfers between devices: 36.2 us -> 38.5 us
    ppermute x26 -> x27, waiting for transfers between devices: 64.5 us -> 61.6 us  [flip(): return lax.ppermute(values, AXES, partners(AXIS[axis], flips))]
    ppermute x26 -> x27, starting transfers between devices: 35.4 us -> 37.8 us  [flip(): return lax.ppermute(values, AXES, partners(AXIS[axis], flips))]
  transfers between devices with their start and end apart: 30 -> 31, of which waited for: 20 -> 20; matrix products, arithmetic and copies ran while one was open for 7% -> 7% of each run, Pallas kernels for 9% -> 9%
where the time goes in v7:
time: 149 us
  waiting for transfers between devices  61.6 us (41%)
  starting transfers between devices  38.5 us (26%)
  Pallas kernels  26.2 us (18%)
  local copies, waits for them, and re-layouts  11.3 us (8%)
  other arithmetic  4.8 us (3%)
  matrix products  4.77 us (3%)
  between operations  1.73 us (1%)
    ppermute x27, waiting for transfers between devices, flip(): return lax.ppermute(values, AXES, partners(AXIS[axis], flips))  61.6 us
    ppermute x27, starting transfers between devices, flip(): return lax.ppermute(values, AXES, partners(AXIS[axis], flips))  37.8 us
    pallas_call x4, Pallas kernels, call(): pl.pallas_call(kernel, in_specs=[vmem] * (len(args) - in_hbm) + [hbm] * i...  26.2 us
    unnamed x27, local copies, waits for them, and re-layouts  6.09 us
  transfers between devices with their start and end apart: 31, of which 20 were waited for; matrix products, arithmetic and copies ran while one was open for 7% of the time, Pallas kernels for 9%

profile of v7, /device:TPU:0, one launch (start us, length us, event | category | flops | bytes accessed | tf_op | source)
XLA Modules:
  0.0 148.9 jit_solution(15659619665229116554)
XLA Ops:
  1.4 1.9 %copy.12.router = bf16[7168,32]{1,0:T(8,128)(2,1)S(1)} copy(bf16[7168,32]{0,1:T(8,128)(2,1)} %param.11) | data formatting | bytes 917504 | tf_op args[1]
  3.9 1.7 %collective-permute-start = (bf16[1,8,4864]{2,1,0:T(8,128)(2,1)S(1)}, bf16[1,8,4864]{2,1,0:T(8,128)(2,1)S(1)}, u32[]{:S(2)}, u32[]{:S(2)}) collective-permute-start(bf16[1,8,4864]{2,1,0:T(8,128)(2,1)S(1)} %bitcast.33), channel_id=1, source_target_pairs={{0,2},{1,67},{2,0},{3,65},{4,6},{5,71},{6,4},{7,69},{8,10},{9,75},... | collective-permute-start | bytes 233480 | tf_op jit(solution)/shard_map/ppermute | solution.py:41
  8.4 3.1 %collective-permute-start.1 = (bf16[2,8,4864]{2,1,0:T(8,128)(2,1)S(1)}, bf16[2,8,4864]{2,1,0:T(8,128)(2,1)S(1)}, u32[]{:S(2)}, u32[]{:S(2)}) collective-permute-start(bf16[2,8,4864]{2,1,0:T(8,128)(2,1)S(1)} %constant_dynamic-update-slice_fusion.4), channel_id=1, source_target_pairs={{0,66},{1,3},{2,64},{3,1},{4,70},{5,7},{6,68},{7,5},{8,74},{9,11},... | collective-permute-start | bytes 466952 | tf_op jit(solution)/shard_map/ppermute | solution.py:41
  11.5 2.8 %collective-permute-start.3 = (bf16[2,8,2432]{2,1,0:T(8,128)(2,1)S(1)}, bf16[2,8,2432]{2,1,0:T(8,128)(2,1)S(1)}, u32[]{:S(2)}, u32[]{:S(2)}) collective-permute-start(bf16[2,8,2432]{2,1,0:T(8,128)(2,1)S(1)} %constant_dynamic-update-slice_fusion.3), channel_id=1, source_target_pairs={{0,12},{1,49},{2,14},{3,51},{4,8},{5,53},{6,10},{7,55},{8,4},{9,57... | collective-permute-start | bytes 233480 | tf_op jit(solution)/shard_map/ppermute | solution.py:41
  14.3 2.8 %collective-permute-done.3 = bf16[2,8,2432]{2,1,0:T(8,128)(2,1)S(1)} collective-permute-done((bf16[2,8,2432]{2,1,0:T(8,128)(2,1)S(1)}, bf16[2,8,2432]{2,1,0:T(8,128)(2,1)S(1)}, u32[]{:S(2)}, u32[]{:S(2)}) %collective-permute-start.3) | collective-permute-done | bytes 77856 | tf_op jit(solution)/shard_map/ppermute | solution.py:41
  17.2 2.0 %collective-permute-start.6 = (bf16[4,8,7296]{2,1,0:T(8,128)(2,1)S(1)}, bf16[4,8,7296]{2,1,0:T(8,128)(2,1)S(1)}, u32[]{:S(2)}, u32[]{:S(2)}) collective-permute-start(bf16[4,8,7296]{2,1,0:T(8,128)(2,1)S(1)} %maximum_maximum_fusion), channel_id=1, source_target_pairs={{0,16},{1,5},{2,18},{3,7},{4,20},{5,1},{6,22},{7,3},{8,24},{9,13},... | collective-permute-start | bytes 1400840 | tf_op jit(solution)/shard_map/ppermute | solution.py:41
  19.2 2.5 %collective-permute-start.7 = (bf16[4,8,7296]{2,1,0:T(8,128)(2,1)S(1)}, bf16[4,8,7296]{2,1,0:T(8,128)(2,1)S(1)}, u32[]{:S(2)}, u32[]{:S(2)}) collective-permute-start(bf16[4,8,7296]{2,1,0:T(8,128)(2,1)S(1)} %maximum_maximum_fusion), channel_id=1, source_target_pairs={{0,48},{1,13},{2,50},{3,15},{4,52},{5,9},{6,54},{7,11},{8,56},{9,5... | collective-permute-start | bytes 1400840 | tf_op jit(solution)/shard_map/ppermute | solution.py:41
  22.8 3.1 %collective-permute-done.6 = bf16[4,8,7296]{2,1,0:T(8,128)(2,1)S(1)} collective-permute-done((bf16[4,8,7296]{2,1,0:T(8,128)(2,1)S(1)}, bf16[4,8,7296]{2,1,0:T(8,128)(2,1)S(1)}, u32[]{:S(2)}, u32[]{:S(2)}) %collective-permute-start.6) | collective-permute-done | bytes 466976 | tf_op jit(solution)/shard_map/ppermute | solution.py:41
  25.9 7.0 %collective-permute-done.7 = bf16[4,8,7296]{2,1,0:T(8,128)(2,1)S(1)} collective-permute-done((bf16[4,8,7296]{2,1,0:T(8,128)(2,1)S(1)}, bf16[4,8,7296]{2,1,0:T(8,128)(2,1)S(1)}, u32[]{:S(2)}, u32[]{:S(2)}) %collective-permute-start.7) | collective-permute-done | bytes 466976 | tf_op jit(solution)/shard_map/ppermute | solution.py:41
  32.8 1.5 %collective-permute-done.8 = bf16[4,8,7296]{2,1,0:T(8,128)(2,1)S(1)} collective-permute-done((bf16[4,8,7296]{2,1,0:T(8,128)(2,1)S(1)}, bf16[4,8,7296]{2,1,0:T(8,128)(2,1)S(1)}, u32[]{:S(2)}, u32[]{:S(2)}) %collective-permute-start.8) | collective-permute-done | bytes 466976 | tf_op jit(solution)/shard_map/ppermute | solution.py:41
  35.0 2.8 %collective-permute-start.12 = (bf16[128,2432]{1,0:T(8,128)(2,1)S(1)}, bf16[128,2432]{1,0:T(8,128)(2,1)S(1)}, u32[]{:S(2)}, u32[]{:S(2)}) collective-permute-start(bf16[128,2432]{1,0:T(8,128)(2,1)S(1)} %bitcast.41), channel_id=1, source_target_pairs={{0,12},{1,49},{2,14},{3,51},{4,8},{5,53},{6,10},{7,55},{8,4},{9,57... | collective-permute-start | bytes 1867784 | tf_op jit(solution)/shard_map/ppermute | solution.py:41
  40.2 5.3 %collective-permute-done.14 = bf16[128,2432]{1,0:T(8,128)(2,1)S(1)} collective-permute-done((bf16[128,2432]{1,0:T(8,128)(2,1)S(1)}, bf16[128,2432]{1,0:T(8,128)(2,1)S(1)}, u32[]{:S(2)}, u32[]{:S(2)}) %collective-permute-start.14) | collective-permute-done | bytes 622624 | tf_op jit(solution)/shard_map/ppermute | solution.py:41
  47.4 1.6 %collective-permute-start.13 = (bf16[256,2432]{1,0:T(8,128)(2,1)}, bf16[256,2432]{1,0:T(8,128)(2,1)}, u32[]{:S(2)}, u32[]{:S(2)}) collective-permute-start(bf16[256,2432]{1,0:T(8,128)(2,1)} %constant_dynamic-update-slice_fusion.1.x2), channel_id=1, source_target_pairs={{0,4},{1,17},{2,6},{3,19},{4,0},{5,21},{6,2},{7,23},{8,12},{9,25},... | collective-permute-start | bytes 3735560 | tf_op jit(solution)/shard_map/ppermute | solution.py:41
  52.0 2.0 %copy-done.2 = bf16[1,7168,256]{2,1,0:T(8,128)(2,1)S(1)} copy-done((bf16[1,7168,256]{2,1,0:T(8,128)(2,1)S(1)}, bf16[1,7168,256]{2,1,0:T(8,128)(2,1)}, u32[]{:S(2)}) %copy-start.2) | copy-done | bytes 3670040
  54.0 2.0 %copy-done.4 = bf16[1,7168,256]{2,1,0:T(8,128)(2,1)S(1)} copy-done((bf16[1,7168,256]{2,1,0:T(8,128)(2,1)S(1)}, bf16[1,7168,256]{2,1,0:T(8,128)(2,1)}, u32[]{:S(2)}) %copy-start.4) | copy-done | bytes 3670040
  56.0 8.9 %shard_map.114 = (f32[256,1024]{1,0:T(8,128)S(1)}, f32[256,1024]{1,0:T(8,128)S(1)}, f32[256,1024]{1,0:T(8,128)S(1)}) custom-call(bf16[256,2432]{1,0:T(8,128)(2,1)} %constant_dynamic-update-slice_fusion.2.x1, bf16[256,2432]{1,0:T(8,128)(2,1)} %constant_dynamic-update-slice_fusion.1.x2, bf16[256,2432]{1,0:T(8,128)(2,1)S(1)} %constant_dynamic-update-slice_fusion.x3, ...), custom_call_target="tpu_custom_call" | custom-call | tf_op jit(solution)/shard_map/pallas_call | solution.py:147
  65.0 4.8 %collective-permute-done.11.x1 = bf16[256,2432]{1,0:T(8,128)(2,1)} collective-permute-done((bf16[256,2432]{1,0:T(8,128)(2,1)}, bf16[256,2432]{1,0:T(8,128)(2,1)}, u32[]{:S(2)}, u32[]{:S(2)}) %collective-permute-start.11) | collective-permute-done | bytes 1245216 | tf_op jit(solution)/shard_map/ppermute | solution.py:41
  69.7 12.2 %shard_map.115 = (bf16[256,2432]{1,0:T(8,128)(2,1)S(1)}, bf16[256,2432]{1,0:T(8,128)(2,1)S(1)}, bf16[256,2304]{1,0:T(8,128)(2,1)S(1)}, bf16[512,512]{1,0:T(8,128)(2,1)S(1)}, bf16[512,512]{1,0:T(8,128)(2,1)S(1)}) custom-call(bf16[256,2432]{1,0:T(8,128)(2,1)} %collective-permute-done.11.x1, bf16[256,2432]{1,0:T(8,128)(2,1)} %collective-permute-done.13.x2, ...), custom_call_target="tpu_custom_call" | custom-call | tf_op jit(solution)/shard_map/pallas_call | solution.py:147
  83.5 1.6 %collective-permute-start.16 = (bf16[256,2432]{1,0:T(8,128)(2,1)S(1)}, bf16[256,2432]{1,0:T(8,128)(2,1)S(1)}, u32[]{:S(2)}, u32[]{:S(2)}) collective-permute-start(bf16[256,2432]{1,0:T(8,128)(2,1)S(1)} %get-tuple-element.36), channel_id=1, source_target_pairs={{0,12},{1,49},{2,14},{3,51},{4,8},{5,53},{6,10},{7,55},{8,4},{9,57... | collective-permute-start | bytes 3735560 | tf_op jit(solution)/shard_map/ppermute | solution.py:41
  87.1 4.5 %shard_map.116 = (bf16[256,2432]{1,0:T(8,128)(2,1)S(1)}, bf16[256,2432]{1,0:T(8,128)(2,1)S(1)}, bf16[256,2304]{1,0:T(8,128)(2,1)S(1)}) custom-call(bf16[512,512]{1,0:T(8,128)(2,1)S(1)} %get-tuple-element.33.straight, bf16[512,512]{1,0:T(8,128)(2,1)S(1)} %get-tuple-element.34.turned, bf16[1,256,7168]{2,1,0:T(8,128)(2,1)S(1)} %copy-done.1, ...), custom_call_target="tpu_custom_call" | custom-call | tf_op jit(solution)/shard_map/pallas_call | solution.py:147
  91.5 9.0 %collective-permute-done.20 = bf16[256,2304]{1,0:T(8,128)(2,1)S(1)} collective-permute-done((bf16[256,2304]{1,0:T(8,128)(2,1)S(1)}, bf16[256,2304]{1,0:T(8,128)(2,1)S(1)}, u32[]{:S(2)}, u32[]{:S(2)}) %collective-permute-start.20) | collective-permute-done | bytes 1179680 | tf_op jit(solution)/shard_map/ppermute | solution.py:41
  100.9 2.1 %collective-permute-start.21 = (bf16[128,2304]{1,0:T(8,128)(2,1)S(1)}, bf16[128,2304]{1,0:T(8,128)(2,1)S(1)}, u32[]{:S(2)}, u32[]{:S(2)}) collective-permute-start(bf16[128,2304]{1,0:T(8,128)(2,1)S(1)} %slice.180), channel_id=1, source_target_pairs={{0,2},{1,67},{2,0},{3,65},{4,6},{5,71},{6,4},{7,69},{8,10},{9,75},... | collective-permute-start | bytes 1769480 | tf_op jit(solution)/shard_map/ppermute | solution.py:41
  104.0 2.0 %collective-permute-start.19 = (bf16[128,2432]{1,0:T(8,128)(2,1)S(1)}, bf16[128,2432]{1,0:T(8,128)(2,1)S(1)}, u32[]{:S(2)}, u32[]{:S(2)}) collective-permute-start(bf16[128,2432]{1,0:T(8,128)(2,1)S(1)} %slice.178), channel_id=1, source_target_pairs={{0,12},{1,49},{2,14},{3,51},{4,8},{5,53},{6,10},{7,55},{8,4},{9,57... | collective-permute-start | bytes 1867784 | tf_op jit(solution)/shard_map/ppermute | solution.py:41
  106.0 4.9 %collective-permute-done.21 = bf16[128,2304]{1,0:T(8,128)(2,1)S(1)} collective-permute-done((bf16[128,2304]{1,0:T(8,128)(2,1)S(1)}, bf16[128,2304]{1,0:T(8,128)(2,1)S(1)}, u32[]{:S(2)}, u32[]{:S(2)}) %collective-permute-start.21) | collective-permute-done | bytes 589856 | tf_op jit(solution)/shard_map/ppermute | solution.py:41
  111.0 2.7 %collective-permute-done.17 = bf16[128,2432]{1,0:T(8,128)(2,1)S(1)} collective-permute-done((bf16[128,2432]{1,0:T(8,128)(2,1)S(1)}, bf16[128,2432]{1,0:T(8,128)(2,1)S(1)}, u32[]{:S(2)}, u32[]{:S(2)}) %collective-permute-start.17) | collective-permute-done | bytes 622624 | tf_op jit(solution)/shard_map/ppermute | solution.py:41
  113.9 1.6 %collective-permute-done.19 = bf16[128,2432]{1,0:T(8,128)(2,1)S(1)} collective-permute-done((bf16[128,2432]{1,0:T(8,128)(2,1)S(1)}, bf16[128,2432]{1,0:T(8,128)(2,1)S(1)}, u32[]{:S(2)}, u32[]{:S(2)}) %collective-permute-start.19) | collective-permute-done | bytes 622624 | tf_op jit(solution)/shard_map/ppermute | solution.py:41
  118.1 3.8 %collective-permute-start.24 = (bf16[4,8,7168]{2,1,0:T(8,128)(2,1)S(1)}, bf16[4,8,7168]{2,1,0:T(8,128)(2,1)S(1)}, u32[]{:S(2)}, u32[]{:S(2)}) collective-permute-start(bf16[4,8,7168]{2,1,0:T(8,128)(2,1)S(1)} %get-tuple-element.53), channel_id=1, source_target_pairs={{0,48},{1,13},{2,50},{3,15},{4,52},{5,9},{6,54},{7,11},{8,56},{9,5... | collective-permute-start | bytes 1376264 | tf_op jit(solution)/shard_map/ppermute | solution.py:41
  123.7 2.2 %collective-permute-done.23 = bf16[4,8,7168]{2,1,0:T(8,128)(2,1)S(1)} collective-permute-done((bf16[4,8,7168]{2,1,0:T(8,128)(2,1)S(1)}, bf16[4,8,7168]{2,1,0:T(8,128)(2,1)S(1)}, u32[]{:S(2)}, u32[]{:S(2)}) %collective-permute-start.23) | collective-permute-done | bytes 458784 | tf_op jit(solution)/shard_map/ppermute | solution.py:41
  125.9 6.9 %collective-permute-done.24 = bf16[4,8,7168]{2,1,0:T(8,128)(2,1)S(1)} collective-permute-done((bf16[4,8,7168]{2,1,0:T(8,128)(2,1)S(1)}, bf16[4,8,7168]{2,1,0:T(8,128)(2,1)S(1)}, u32[]{:S(2)}, u32[]{:S(2)}) %collective-permute-start.24) | collective-permute-done | bytes 458784 | tf_op jit(solution)/shard_map/ppermute | solution.py:41
  135.4 3.0 %collective-permute-start.27 = (bf16[1,8,4864]{2,1,0:T(8,128)(2,1)S(1)}, bf16[1,8,4864]{2,1,0:T(8,128)(2,1)S(1)}, u32[]{:S(2)}, u32[]{:S(2)}) collective-permute-start(bf16[1,8,4864]{2,1,0:T(8,128)(2,1)S(1)} %get-tuple-element.56), channel_id=1, source_target_pairs={{0,66},{1,3},{2,64},{3,1},{4,70},{5,7},{6,68},{7,5},{8,74},{9,11},... | collective-permute-start | bytes 233480 | tf_op jit(solution)/shard_map/ppermute | solution.py:41
  141.2 3.1 %collective-permute-done.28 = bf16[1,8,4864]{2,1,0:T(8,128)(2,1)S(1)} collective-permute-done((bf16[1,8,4864]{2,1,0:T(8,128)(2,1)S(1)}, bf16[1,8,4864]{2,1,0:T(8,128)(2,1)S(1)}, u32[]{:S(2)}, u32[]{:S(2)}) %collective-permute-start.28) | collective-permute-done | bytes 77856 | tf_op jit(solution)/shard_map/ppermute | solution.py:41
  144.6 2.2 %fusion.11 = f32[8,576]{1,0:T(8,128)S(1)} fusion(bf16[7168,576]{0,1:T(8,128)(2,1)S(1)} %bitcast.38, bf16[8,7168]{1,0:T(8,128)(2,1)S(1)} %get-tuple-element.47, f32[8]{0:T(128)S(1)} %add_rsqrt_fusion.1), kind=kOutput, calls=%fused_computation.38 | convolution fusion | flops 66232320 | bytes 8390688 | tf_op jit(solution)/shard_map/dot_general | solution.py:120
  (116 shorter events, 29.8 us)
Async XLA Ops:
  0.6 84.4 %copy-start = (bf16[8,128,576]{1,2,0:T(8,128)(2,1)S(1)}, bf16[8,128,576]{1,2,0:T(8,128)(2,1)}, u32[]{:S(2)}) copy-start(bf16[8,128,576]{1,2,0:T(8,128)(2,1)} %param.19) | copy-start | bytes 3538948
  0.7 16.5 %collective-permute-start.4 = (bf16[1,7168,256]{2,1,0:T(8,128)(2,1)}, bf16[1,7168,256]{2,1,0:T(8,128)(2,1)}, u32[]{:S(2)}, u32[]{:S(2)}) collective-permute-start(bf16[1,7168,256]{2,1,0:T(8,128)(2,1)} %s1_.3), channel_id=1, source_target_pairs={{0,1},{1,0},{2,3},{3,2},{4,5},{5,4},{6,7},{7,6},{8,9},{9,8},{10,11... | collective-permute-start | bytes 11010056 | tf_op jit(solution)/shard_map/ppermute | solution.py:45
  0.8 16.5 %collective-permute-start.5 = (bf16[1,7168,256]{2,1,0:T(8,128)(2,1)}, bf16[1,7168,256]{2,1,0:T(8,128)(2,1)}, u32[]{:S(2)}, u32[]{:S(2)}) collective-permute-start(bf16[1,7168,256]{2,1,0:T(8,128)(2,1)} %s2_.3), channel_id=1, source_target_pairs={{0,1},{1,0},{2,3},{3,2},{4,5},{5,4},{6,7},{7,6},{8,9},{9,8},{10,11... | collective-permute-start | bytes 11010056 | tf_op jit(solution)/shard_map/ppermute | solution.py:45
  1.3 33.4 %collective-permute-start.9 = (bf16[1,256,7168]{2,1,0:T(8,128)(2,1)}, bf16[1,256,7168]{2,1,0:T(8,128)(2,1)}, u32[]{:S(2)}, u32[]{:S(2)}) collective-permute-start(bf16[1,256,7168]{2,1,0:T(8,128)(2,1)} %own_low.3), channel_id=1, source_target_pairs={{0,1},{1,0},{2,3},{3,2},{4,5},{5,4},{6,7},{7,6},{8,9},{9,8},{10,11... | collective-permute-start | bytes 11010056 | tf_op jit(solution)/shard_map/ppermute | solution.py:45
  3.9 4.4 %collective-permute-start = (bf16[1,8,4864]{2,1,0:T(8,128)(2,1)S(1)}, bf16[1,8,4864]{2,1,0:T(8,128)(2,1)S(1)}, u32[]{:S(2)}, u32[]{:S(2)}) collective-permute-start(bf16[1,8,4864]{2,1,0:T(8,128)(2,1)S(1)} %bitcast.33), channel_id=1, source_target_pairs={{0,2},{1,67},{2,0},{3,65},{4,6},{5,71},{6,4},{7,69},{8,10},{9,75},... | collective-permute-start | bytes 233480 | tf_op jit(solution)/shard_map/ppermute | solution.py:41
  5.6 5.8 %collective-permute-start.2 = (bf16[1,8,2432]{2,1,0:T(8,128)(2,1)S(1)}, bf16[1,8,2432]{2,1,0:T(8,128)(2,1)S(1)}, u32[]{:S(2)}, u32[]{:S(2)}) collective-permute-start(bf16[1,8,2432]{2,1,0:T(8,128)(2,1)S(1)} %bitcast.35), channel_id=1, source_target_pairs={{0,4},{1,17},{2,6},{3,19},{4,0},{5,21},{6,2},{7,23},{8,12},{9,25},... | collective-permute-start | bytes 116744 | tf_op jit(solution)/shard_map/ppermute | solution.py:41
  8.4 8.8 %collective-permute-start.1 = (bf16[2,8,4864]{2,1,0:T(8,128)(2,1)S(1)}, bf16[2,8,4864]{2,1,0:T(8,128)(2,1)S(1)}, u32[]{:S(2)}, u32[]{:S(2)}) collective-permute-start(bf16[2,8,4864]{2,1,0:T(8,128)(2,1)S(1)} %constant_dynamic-update-slice_fusion.4), channel_id=1, source_target_pairs={{0,66},{1,3},{2,64},{3,1},{4,70},{5,7},{6,68},{7,5},{8,74},{9,11},... | collective-permute-start | bytes 466952 | tf_op jit(solution)/shard_map/ppermute | solution.py:41
  11.5 5.7 %collective-permute-start.3 = (bf16[2,8,2432]{2,1,0:T(8,128)(2,1)S(1)}, bf16[2,8,2432]{2,1,0:T(8,128)(2,1)S(1)}, u32[]{:S(2)}, u32[]{:S(2)}) collective-permute-start(bf16[2,8,2432]{2,1,0:T(8,128)(2,1)S(1)} %constant_dynamic-update-slice_fusion.3), channel_id=1, source_target_pairs={{0,12},{1,49},{2,14},{3,51},{4,8},{5,53},{6,10},{7,55},{8,4},{9,57... | collective-permute-start | bytes 233480 | tf_op jit(solution)/shard_map/ppermute | solution.py:41
  17.2 8.6 %collective-permute-start.6 = (bf16[4,8,7296]{2,1,0:T(8,128)(2,1)S(1)}, bf16[4,8,7296]{2,1,0:T(8,128)(2,1)S(1)}, u32[]{:S(2)}, u32[]{:S(2)}) collective-permute-start(bf16[4,8,7296]{2,1,0:T(8,128)(2,1)S(1)} %maximum_maximum_fusion), channel_id=1, source_target_pairs={{0,16},{1,5},{2,18},{3,7},{4,20},{5,1},{6,22},{7,3},{8,24},{9,13},... | collective-permute-start | bytes 1400840 | tf_op jit(solution)/shard_map/ppermute | solution.py:41
  19.2 13.6 %collective-permute-start.7 = (bf16[4,8,7296]{2,1,0:T(8,128)(2,1)S(1)}, bf16[4,8,7296]{2,1,0:T(8,128)(2,1)S(1)}, u32[]{:S(2)}, u32[]{:S(2)}) collective-permute-start(bf16[4,8,7296]{2,1,0:T(8,128)(2,1)S(1)} %maximum_maximum_fusion), channel_id=1, source_target_pairs={{0,48},{1,13},{2,50},{3,15},{4,52},{5,9},{6,54},{7,11},{8,56},{9,5... | collective-permute-start | bytes 1400840 | tf_op jit(solution)/shard_map/ppermute | solution.py:41
  21.8 12.6 %collective-permute-start.8 = (bf16[4,8,7296]{2,1,0:T(8,128)(2,1)S(1)}, bf16[4,8,7296]{2,1,0:T(8,128)(2,1)S(1)}, u32[]{:S(2)}, u32[]{:S(2)}) collective-permute-start(bf16[4,8,7296]{2,1,0:T(8,128)(2,1)S(1)} %maximum_maximum_fusion), channel_id=1, source_target_pairs={{0,32},{1,9},{2,34},{3,11},{4,36},{5,13},{6,38},{7,15},{8,40},{9,1... | collective-permute-start | bytes 1400840 | tf_op jit(solution)/shard_map/ppermute | solution.py:41
  34.8 10.6 %collective-permute-start.14 = (bf16[128,2432]{1,0:T(8,128)(2,1)S(1)}, bf16[128,2432]{1,0:T(8,128)(2,1)S(1)}, u32[]{:S(2)}, u32[]{:S(2)}) collective-permute-start(bf16[128,2432]{1,0:T(8,128)(2,1)S(1)} %bitcast.43), channel_id=1, source_target_pairs={{0,2},{1,67},{2,0},{3,65},{4,6},{5,71},{6,4},{7,69},{8,10},{9,75},... | collective-permute-start | bytes 1867784 | tf_op jit(solution)/shard_map/ppermute | solution.py:41
  35.0 11.4 %collective-permute-start.12 = (bf16[128,2432]{1,0:T(8,128)(2,1)S(1)}, bf16[128,2432]{1,0:T(8,128)(2,1)S(1)}, u32[]{:S(2)}, u32[]{:S(2)}) collective-permute-start(bf16[128,2432]{1,0:T(8,128)(2,1)S(1)} %bitcast.41), channel_id=1, source_target_pairs={{0,12},{1,49},{2,14},{3,51},{4,8},{5,53},{6,10},{7,55},{8,4},{9,57... | collective-permute-start | bytes 1867784 | tf_op jit(solution)/shard_map/ppermute | solution.py:41
  40.2 10.2 %collective-permute-start.10 = (bf16[128,2432]{1,0:T(8,128)(2,1)S(1)}, bf16[128,2432]{1,0:T(8,128)(2,1)S(1)}, u32[]{:S(2)}, u32[]{:S(2)}) collective-permute-start(bf16[128,2432]{1,0:T(8,128)(2,1)S(1)} %bitcast.40), channel_id=1, source_target_pairs={{0,4},{1,17},{2,6},{3,19},{4,0},{5,21},{6,2},{7,23},{8,12},{9,25},... | collective-permute-start | bytes 1867784 | tf_op jit(solution)/shard_map/ppermute | solution.py:41
  45.5 19.4 %collective-permute-start.15 = (bf16[256,2432]{1,0:T(8,128)(2,1)S(1)}, bf16[256,2432]{1,0:T(8,128)(2,1)}, u32[]{:S(2)}, u32[]{:S(2)}) collective-permute-start(bf16[256,2432]{1,0:T(8,128)(2,1)S(1)} %constant_dynamic-update-slice_fusion.x3), channel_id=1, source_target_pairs={{0,66},{1,3},{2,64},{3,1},{4,70},{5,7},{6,68},{7,5},{8,74},{9,11},... | collective-permute-start | bytes 3735560 | tf_op jit(solution)/shard_map/ppermute | solution.py:41
  47.4 17.6 %collective-permute-start.13 = (bf16[256,2432]{1,0:T(8,128)(2,1)}, bf16[256,2432]{1,0:T(8,128)(2,1)}, u32[]{:S(2)}, u32[]{:S(2)}) collective-permute-start(bf16[256,2432]{1,0:T(8,128)(2,1)} %constant_dynamic-update-slice_fusion.1.x2), channel_id=1, source_target_pairs={{0,4},{1,17},{2,6},{3,19},{4,0},{5,21},{6,2},{7,23},{8,12},{9,25},... | collective-permute-start | bytes 3735560 | tf_op jit(solution)/shard_map/ppermute | solution.py:41
  51.3 18.4 %collective-permute-start.11 = (bf16[256,2432]{1,0:T(8,128)(2,1)}, bf16[256,2432]{1,0:T(8,128)(2,1)}, u32[]{:S(2)}, u32[]{:S(2)}) collective-permute-start(bf16[256,2432]{1,0:T(8,128)(2,1)} %constant_dynamic-update-slice_fusion.2.x1), channel_id=1, source_target_pairs={{0,12},{1,49},{2,14},{3,51},{4,8},{5,53},{6,10},{7,55},{8,4},{9,57... | collective-permute-start | bytes 3735560 | tf_op jit(solution)/shard_map/ppermute | solution.py:41
  81.9 18.7 %collective-permute-start.20 = (bf16[256,2304]{1,0:T(8,128)(2,1)S(1)}, bf16[256,2304]{1,0:T(8,128)(2,1)S(1)}, u32[]{:S(2)}, u32[]{:S(2)}) collective-permute-start(bf16[256,2304]{1,0:T(8,128)(2,1)S(1)} %get-tuple-element.40), channel_id=1, source_target_pairs={{0,66},{1,3},{2,64},{3,1},{4,70},{5,7},{6,68},{7,5},{8,74},{9,11},... | collective-permute-start | bytes 3538952 | tf_op jit(solution)/shard_map/ppermute | solution.py:41
  83.5 19.5 %collective-permute-start.16 = (bf16[256,2432]{1,0:T(8,128)(2,1)S(1)}, bf16[256,2432]{1,0:T(8,128)(2,1)S(1)}, u32[]{:S(2)}, u32[]{:S(2)}) collective-permute-start(bf16[256,2432]{1,0:T(8,128)(2,1)S(1)} %get-tuple-element.36), channel_id=1, source_target_pairs={{0,12},{1,49},{2,14},{3,51},{4,8},{5,53},{6,10},{7,55},{8,4},{9,57... | collective-permute-start | bytes 3735560 | tf_op jit(solution)/shard_map/ppermute | solution.py:41
  86.7 17.0 %collective-permute-start.18 = (bf16[256,2432]{1,0:T(8,128)(2,1)S(1)}, bf16[256,2432]{1,0:T(8,128)(2,1)S(1)}, u32[]{:S(2)}, u32[]{:S(2)}) collective-permute-start(bf16[256,2432]{1,0:T(8,128)(2,1)S(1)} %get-tuple-element.38), channel_id=1, source_target_pairs={{0,4},{1,17},{2,6},{3,19},{4,0},{5,21},{6,2},{7,23},{8,12},{9,25},... | collective-permute-start | bytes 3735560 | tf_op jit(solution)/shard_map/ppermute | solution.py:41
  100.9 10.0 %collective-permute-start.21 = (bf16[128,2304]{1,0:T(8,128)(2,1)S(1)}, bf16[128,2304]{1,0:T(8,128)(2,1)S(1)}, u32[]{:S(2)}, u32[]{:S(2)}) collective-permute-start(bf16[128,2304]{1,0:T(8,128)(2,1)S(1)} %slice.180), channel_id=1, source_target_pairs={{0,2},{1,67},{2,0},{3,65},{4,6},{5,71},{6,4},{7,69},{8,10},{9,75},... | collective-permute-start | bytes 1769480 | tf_op jit(solution)/shard_map/ppermute | solution.py:41
  103.4 10.3 %collective-permute-start.17 = (bf16[128,2432]{1,0:T(8,128)(2,1)S(1)}, bf16[128,2432]{1,0:T(8,128)(2,1)S(1)}, u32[]{:S(2)}, u32[]{:S(2)}) collective-permute-start(bf16[128,2432]{1,0:T(8,128)(2,1)S(1)} %slice.179), channel_id=1, source_target_pairs={{0,4},{1,17},{2,6},{3,19},{4,0},{5,21},{6,2},{7,23},{8,12},{9,25},... | collective-permute-start | bytes 1867784 | tf_op jit(solution)/shard_map/ppermute | solution.py:41
  104.0 11.5 %collective-permute-start.19 = (bf16[128,2432]{1,0:T(8,128)(2,1)S(1)}, bf16[128,2432]{1,0:T(8,128)(2,1)S(1)}, u32[]{:S(2)}, u32[]{:S(2)}) collective-permute-start(bf16[128,2432]{1,0:T(8,128)(2,1)S(1)} %slice.178), channel_id=1, source_target_pairs={{0,12},{1,49},{2,14},{3,51},{4,8},{5,53},{6,10},{7,55},{8,4},{9,57... | collective-permute-start | bytes 1867784 | tf_op jit(solution)/shard_map/ppermute | solution.py:41
  113.8 1.8 %collective-permute-start.22 = (bf16[8,128]{1,0:T(8,128)(2,1)S(1)}, bf16[8,128]{1,0:T(8,128)(2,1)S(1)}, u32[]{:S(2)}, u32[]{:S(2)}) collective-permute-start(bf16[8,128]{1,0:T(8,128)(2,1)S(1)} %slice.130), channel_id=1, source_target_pairs={{0,1},{1,0},{2,3},{3,2},{4,5},{5,4},{6,7},{7,6},{8,9},{9,8},{10,11... | collective-permute-start | bytes 6152 | tf_op jit(solution)/shard_map/ppermute | solution.py:45
  117.4 8.6 %collective-permute-start.23 = (bf16[4,8,7168]{2,1,0:T(8,128)(2,1)S(1)}, bf16[4,8,7168]{2,1,0:T(8,128)(2,1)S(1)}, u32[]{:S(2)}, u32[]{:S(2)}) collective-permute-start(bf16[4,8,7168]{2,1,0:T(8,128)(2,1)S(1)} %get-tuple-element.51), channel_id=1, source_target_pairs={{0,16},{1,5},{2,18},{3,7},{4,20},{5,1},{6,22},{7,3},{8,24},{9,13},... | collective-permute-start | bytes 1376264 | tf_op jit(solution)/shard_map/ppermute | solution.py:41
  118.1 14.7 %collective-permute-start.24 = (bf16[4,8,7168]{2,1,0:T(8,128)(2,1)S(1)}, bf16[4,8,7168]{2,1,0:T(8,128)(2,1)S(1)}, u32[]{:S(2)}, u32[]{:S(2)}) collective-permute-start(bf16[4,8,7168]{2,1,0:T(8,128)(2,1)S(1)} %get-tuple-element.53), channel_id=1, source_target_pairs={{0,48},{1,13},{2,50},{3,15},{4,52},{5,9},{6,54},{7,11},{8,56},{9,5... | collective-permute-start | bytes 1376264 | tf_op jit(solution)/shard_map/ppermute | solution.py:41
  121.9 12.0 %collective-permute-start.25 = (bf16[4,8,7168]{2,1,0:T(8,128)(2,1)S(1)}, bf16[4,8,7168]{2,1,0:T(8,128)(2,1)S(1)}, u32[]{:S(2)}, u32[]{:S(2)}) collective-permute-start(bf16[4,8,7168]{2,1,0:T(8,128)(2,1)S(1)} %get-tuple-element.52), channel_id=1, source_target_pairs={{0,32},{1,9},{2,34},{3,11},{4,36},{5,13},{6,38},{7,15},{8,40},{9,1... | collective-permute-start | bytes 1376264 | tf_op jit(solution)/shard_map/ppermute | solution.py:41
  134.1 5.6 %collective-permute-start.29 = (bf16[2,8,2304]{2,1,0:T(8,128)(2,1)S(1)}, bf16[2,8,2304]{2,1,0:T(8,128)(2,1)S(1)}, u32[]{:S(2)}, u32[]{:S(2)}) collective-permute-start(bf16[2,8,2304]{2,1,0:T(8,128)(2,1)S(1)} %slice.140), channel_id=1, source_target_pairs={{0,12},{1,49},{2,14},{3,51},{4,8},{5,53},{6,10},{7,55},{8,4},{9,57... | collective-permute-start | bytes 221192 | tf_op jit(solution)/shard_map/ppermute | solution.py:41
  134.7 5.2 %collective-permute-start.26 = (bf16[1,8,4864]{2,1,0:T(8,128)(2,1)S(1)}, bf16[1,8,4864]{2,1,0:T(8,128)(2,1)S(1)}, u32[]{:S(2)}, u32[]{:S(2)}) collective-permute-start(bf16[1,8,4864]{2,1,0:T(8,128)(2,1)S(1)} %get-tuple-element.54), channel_id=1, source_target_pairs={{0,2},{1,67},{2,0},{3,65},{4,6},{5,71},{6,4},{7,69},{8,10},{9,75},... | collective-permute-start | bytes 233480 | tf_op jit(solution)/shard_map/ppermute | solution.py:41
  135.4 5.8 %collective-permute-start.27 = (bf16[1,8,4864]{2,1,0:T(8,128)(2,1)S(1)}, bf16[1,8,4864]{2,1,0:T(8,128)(2,1)S(1)}, u32[]{:S(2)}, u32[]{:S(2)}) collective-permute-start(bf16[1,8,4864]{2,1,0:T(8,128)(2,1)S(1)} %get-tuple-element.56), channel_id=1, source_target_pairs={{0,66},{1,3},{2,64},{3,1},{4,70},{5,7},{6,68},{7,5},{8,74},{9,11},... | collective-permute-start | bytes 233480 | tf_op jit(solution)/shard_map/ppermute | solution.py:41
  138.4 5.9 %collective-permute-start.28 = (bf16[1,8,4864]{2,1,0:T(8,128)(2,1)S(1)}, bf16[1,8,4864]{2,1,0:T(8,128)(2,1)S(1)}, u32[]{:S(2)}, u32[]{:S(2)}) collective-permute-start(bf16[1,8,4864]{2,1,0:T(8,128)(2,1)S(1)} %get-tuple-element.55), channel_id=1, source_target_pairs={{0,64},{1,65},{2,66},{3,67},{4,68},{5,69},{6,70},{7,71},{8,72},{9,... | collective-permute-start | bytes 233480 | tf_op jit(solution)/shard_map/ppermute | solution.py:41
  139.8 4.5 %collective-permute-start.30 = (bf16[1,8,2304]{2,1,0:T(8,128)(2,1)S(1)}, bf16[1,8,2304]{2,1,0:T(8,128)(2,1)S(1)}, u32[]{:S(2)}, u32[]{:S(2)}) collective-permute-start(bf16[1,8,2304]{2,1,0:T(8,128)(2,1)S(1)} %slice.181), channel_id=1, source_target_pairs={{0,4},{1,17},{2,6},{3,19},{4,0},{5,21},{6,2},{7,23},{8,12},{9,25},... | collective-permute-start | bytes 110600 | tf_op jit(solution)/shard_map/ppermute | solution.py:41
  (12 other events, 120.4 us)
